TPU v7x, 1024 devices: a whole 8x8x8 slice. The times are simulated.
1024 devices in a mesh: dp: 64 (over z, y), fsdp: 16 (over x, core).
Axes of the slice: x: 8, y: 8, z: 8, core: 2. Of those that a mesh axis runs over, the one named last changes fastest.
Arguments:
- qkv_codes: bfloat16 [64, 16, 128, 3, 896], P('dp', 'fsdp'), may hold values from -4 to 4, as said below
- block_scales: bfloat16 [64, 16, 128, 3, 7], P('dp', 'fsdp'), may hold values from 0.25 to 2
- home_segments: int32 [64, 16, 128], P('dp', 'fsdp'), may hold values from -1 to 131, as said below
- kept_rows: int32 [64, 16], P('dp', 'fsdp'), may hold values from 32 to 64, as said below
- pack_list: int32 [64, 16, 4, 3], P(None, 'fsdp'), may hold values from 0 to 112, as said below
- w_out: bfloat16 [896, 1792], P('fsdp'), may hold values from -0.1875 to 0.1875
- cotangent: bfloat16 [64, 16, 128, 1792], P('dp', 'fsdp'), may hold values from -4 to 4
Outputs:
- output: bfloat16 [64, 16, 128, 1792], P('dp', 'fsdp')
- grad_codes: bfloat16 [64, 16, 128, 3, 896], P('dp', 'fsdp')
- grad_w_out: float32 [64, 896, 1792], P('dp', 'fsdp')
Inputs may be any that keep to these rules, and one draw needn't show every extreme that they name: Rows below kept_rows are whole images or the first part of one, and stay in place; the first image of every device has at least 3 rows. `pack_list`: one table for each fsdp index, the same on all its dp devices. Entry [s, d] describes the one whole image that dp index s sends to s + offset(d), offsets +1, -1, +2, -2, always inside the axis; length 0 means none, with the other entries 0. Lengths run from 3 to 16 and reach 16. Sent images lie at or above the source's kept_rows without intersection; placed images lie at or above the target's kept_rows without intersection, below 128. `home_segments`: kept rows carry their image number, runs of equal numbers; rows of the image sent in direction d carry 128 + d; other rows -1. `qkv_codes`: every entry is a value of the e4m3 8-bit float format.
All inputs are finite; a program needn't handle non-finite values.
Results may differ from a plain program's by a relative error of at most 0.02.
Values may be sent and summed in bfloat16 or wider, within the bound.
No kernel may reach another device: no remote copies, remote signals or barrier semaphores. Data moves between devices by JAX's collectives and lax.ppermute only.
A program may use at most 32 MiB of HBM per device.

v0:
```python
import math

import jax
import jax.numpy as jnp
from jax import lax
from jax.sharding import PartitionSpec as P

HEADS = 8


offsets = (1, -1, 2, -2)


def shifted(block, axis, distance):
    devices = range(lax.axis_size(axis))
    route = [(i - distance, i) for i in devices if i - distance in devices]
    return lax.ppermute(block, axis, route)


def dequantize(codes, scales):
    count = codes.shape[0]
    blocks = scales.shape[-1]
    scaled = (
        codes.astype(jnp.float32).reshape(count, 3, blocks, -1)
        * scales.astype(jnp.float32)[..., None]
    )
    return scaled.reshape(count, 3, -1).astype(jnp.bfloat16)


def local_layer(codes, scales, labels, w_full, grad_out):
    count = codes.shape[0]
    width = w_full.shape[0]
    head_size = width // HEADS
    factor = 1.0 / math.sqrt(head_size)
    values = dequantize(codes, scales)
    query = values[:, 0].reshape(count, HEADS, head_size)
    keys = values[:, 1].reshape(count, HEADS, head_size)
    value_rows = values[:, 2].reshape(count, HEADS, head_size)
    scores = jnp.einsum("qhd,khd->hqk", query, keys, preferred_element_type=jnp.float32) * factor
    same = labels[:, None] == labels[None, :]
    scores = jnp.where(same[None], scores, -jnp.inf)
    top = jnp.max(scores, axis=-1, keepdims=True)
    weights = jnp.exp(scores - top)
    probs = weights / jnp.sum(weights, axis=-1, keepdims=True)
    probs_b = probs.astype(jnp.bfloat16)
    context = jnp.einsum("hqk,khd->qhd", probs_b, value_rows, preferred_element_type=jnp.float32)
    context = context.reshape(count, width).astype(jnp.bfloat16)
    output = jnp.dot(context, w_full, preferred_element_type=jnp.float32).astype(jnp.bfloat16)
    grad_context = lax.dot_general(
        grad_out, w_full, (((1,), (1,)), ((), ())), preferred_element_type=jnp.float32
    )
    grad_context = grad_context.astype(jnp.bfloat16).reshape(count, HEADS, head_size)
    grad_probs = jnp.einsum(
        "qhd,khd->hqk", grad_context, value_rows, preferred_element_type=jnp.float32
    )
    total = jnp.sum(probs * grad_probs, axis=-1, keepdims=True)
    grad_scores = (probs * (grad_probs - total) * factor).astype(jnp.bfloat16)
    grad_query = jnp.einsum("hqk,khd->qhd", grad_scores, keys, preferred_element_type=jnp.float32)
    grad_keys = jnp.einsum("hqk,qhd->khd", grad_scores, query, preferred_element_type=jnp.float32)
    grad_values = jnp.einsum(
        "hqk,qhd->khd", probs_b, grad_context, preferred_element_type=jnp.float32
    )
    grads = jnp.stack([grad_query, grad_keys, grad_values], axis=1).reshape(count, 3, -1)
    blocks = scales.shape[-1]
    grads = (grads.reshape(count, 3, blocks, -1) * scales.astype(jnp.float32)[..., None]).reshape(
        count, 3, -1
    )
    return (output, grads.astype(jnp.bfloat16), context)


def pad_rows(array, extra_rows, fill):
    extra = jnp.full((extra_rows,) + array.shape[1:], fill, array.dtype)
    return jnp.concatenate([array, extra], axis=0)


def cut_rows(buffer, at_row, length, slot):
    piece = lax.dynamic_slice_in_dim(buffer, at_row, slot, 0)
    present = (jnp.arange(slot) < length).reshape((slot,) + (1,) * (buffer.ndim - 1))
    return jnp.where(present, piece, jnp.zeros_like(piece))


def put_rows(buffer, piece, at_row, length):
    slot = piece.shape[0]
    old = lax.dynamic_slice_in_dim(buffer, at_row, slot, 0)
    present = (jnp.arange(slot) < length).reshape((slot,) + (1,) * (buffer.ndim - 1))
    return lax.dynamic_update_slice_in_dim(buffer, jnp.where(present, piece, old), at_row, 0)


def local(qkv_codes, block_scales, home_segments, kept_rows, pack_list, w_out, cotangent):
    position = lax.axis_index("dp")
    group_size = lax.axis_size("dp")
    codes = qkv_codes[0, 0]
    scales = block_scales[0, 0]
    segments = home_segments[0, 0]
    kept = kept_rows[0, 0]
    table = pack_list[:, 0]
    grad_out = cotangent[0, 0]
    row_count = codes.shape[0]
    slot = row_count // 8
    w_full = lax.all_gather(w_out, "fsdp", axis=0, tiled=True)
    inside = jnp.arange(row_count) < kept
    own_entries = lax.dynamic_index_in_dim(table, position, 0, keepdims=False)
    home_codes = pad_rows(codes, slot, 0)
    home_scales = pad_rows(scales, slot, 0)
    sent_codes = [
        cut_rows(home_codes, own_entries[route, 0], own_entries[route, 1], slot)
        for route in range(4)
    ]
    sent_scales = [
        cut_rows(home_scales, own_entries[route, 0], own_entries[route, 1], slot)
        for route in range(4)
    ]
    received = [
        shifted((sent_codes[route], sent_scales[route]), "dp", offsets[route]) for route in range(4)
    ]
    landing = []
    arrived = []
    for route in range(4):
        source = position - offsets[route]
        allowed = (source >= 0) & (source < group_size)
        entries = lax.dynamic_index_in_dim(
            table, jnp.clip(source, 0, group_size - 1), 0, keepdims=False
        )
        arrived.append(jnp.where(allowed, entries[route, 1], 0))
        landing.append(entries[route, 2])
    bal_codes = pad_rows(jnp.where(inside[:, None, None], codes, jnp.zeros_like(codes)), slot, 0)
    bal_scales = pad_rows(jnp.where(inside[:, None, None], scales, jnp.zeros_like(scales)), slot, 0)
    labels = pad_rows(jnp.where(inside, segments, -1), slot, -1)
    for route in range(4):
        bal_codes = put_rows(bal_codes, received[route][0], landing[route], arrived[route])
        bal_scales = put_rows(bal_scales, received[route][1], landing[route], arrived[route])
        marks = jnp.full((slot,), 100000 + route, jnp.int32)
        labels = put_rows(labels, marks, landing[route], arrived[route])
    output, grads, context = local_layer(
        bal_codes[:row_count], bal_scales[:row_count], labels[:row_count], w_full, grad_out
    )
    grads_padded = pad_rows(grads, slot, 0)
    going_back = [
        cut_rows(grads_padded, landing[route], arrived[route], slot) for route in range(4)
    ]
    returned = [shifted(going_back[route], "dp", -offsets[route]) for route in range(4)]
    home_grads = pad_rows(jnp.where(inside[:, None, None], grads, jnp.zeros_like(grads)), slot, 0)
    for route in range(4):
        home_grads = put_rows(
            home_grads, returned[route], own_entries[route, 0], own_entries[route, 1]
        )
    grad_codes = home_grads[:row_count]
    term = lax.dot_general(
        context, grad_out, (((0,), (0,)), ((), ())), preferred_element_type=jnp.float32
    )
    grad_w = lax.psum_scatter(
        term.astype(jnp.bfloat16), "fsdp", scatter_dimension=0, tiled=True
    ).astype(jnp.float32)
    return (output[None, None], grad_codes[None, None], grad_w[None])


def solution(mesh):
    return jax.shard_map(
        local,
        mesh=mesh,
        in_specs=(
            P("dp", "fsdp", None, None, None),
            P("dp", "fsdp", None, None, None),
            P("dp", "fsdp", None),
            P("dp", "fsdp"),
            P(None, "fsdp", None, None),
            P("fsdp", None),
            P("dp", "fsdp", None, None),
        ),
        out_specs=(
            P("dp", "fsdp", None, None),
            P("dp", "fsdp", None, None, None),
            P("dp", "fsdp", None),
        ),
        check_vma=False,
    )
```

profile of v0, /device:TPU:494, one launch (start us, length us, event | category | flops | bytes accessed | tf_op | source)
XLA Modules:
  0.0 234.8 jit_solution(4343152600337548600)
XLA Ops:
  7.2 0.7 all-gather.2.cloned.1.call-update
  8.0 1.0 constant_dynamic-slice_fusion.4
  9.1 0.7 fusion.51
  14.6 1.4 copy.40
  16.7 1.3 iota_compare_fusion
  19.2 1.3 iota_compare_fusion.4
  21.1 2.0 fusion.21
  23.1 2.0 copy.43
  25.1 2.8 %collective-permute-start = (bf16[16,3,896]{2,0,1:T(8,128)(2,1)}, bf16[16,3,896]{2,0,1:T(8,128)(2,1)}, u32[]{:S(2)}, u32[]{:S(2)}) collective-permute-start(bf16[16,3,896]{2,0,1:T(8,128)(2,1)} %copy.43), channel_id=1, source_target_pairs={{0,16},{16,32},{32,48},{48,64},{64,80},{80,96},{96,112},{112,128},... | collective-permute-start | bytes 258056 | tf_op jit(solution)/shard_map/ppermute | solution.py:17
  27.9 0.9 copy.46
  28.8 3.1 %collective-permute-start.1 = (bf16[16,3,896]{2,0,1:T(8,128)(2,1)}, bf16[16,3,896]{2,0,1:T(8,128)(2,1)}, u32[]{:S(2)}, u32[]{:S(2)}) collective-permute-start(bf16[16,3,896]{2,0,1:T(8,128)(2,1)} %copy.46), channel_id=1, source_target_pairs={{16,0},{32,16},{48,32},{64,48},{80,64},{96,80},{112,96},{128,112},... | collective-permute-start | bytes 258056 | tf_op jit(solution)/shard_map/ppermute | solution.py:17
  32.2 8.4 %collective-permute-start.2 = (bf16[16,3,896]{2,0,1:T(8,128)(2,1)S(1)}, bf16[16,3,896]{2,0,1:T(8,128)(2,1)}, u32[]{:S(2)}, u32[]{:S(2)}) collective-permute-start(bf16[16,3,896]{2,0,1:T(8,128)(2,1)S(1)} %copy.49), channel_id=1, source_target_pairs={{0,32},{16,48},{32,64},{48,80},{64,96},{80,112},{96,128},{112,144}... | collective-permute-start | bytes 258056 | tf_op jit(solution)/shard_map/ppermute | solution.py:17
  40.8 1.9 collective-permute-start.3
  42.8 0.7 fusion.40
  43.5 1.9 collective-permute-start.4
  45.5 0.7 fusion.54
  47.5 0.7 fusion.53
  49.6 0.7 fusion.52
  51.6 0.6 fusion.50
  60.0 0.6 iota_compare_fusion.3
  61.4 3.9 %collective-permute-start.5 = (bf16[16,3,7]{0,2,1:T(8,128)(2,1)S(1)}, bf16[16,3,7]{0,2,1:T(8,128)(2,1)S(1)}, u32[]{:S(2)}, u32[]{:S(2)}) collective-permute-start(bf16[16,3,7]{0,2,1:T(8,128)(2,1)S(1)} %copy-done.13), channel_id=1, source_target_pairs={{16,0},{32,16},{48,32},{64,48},{80,64},{96,80},{112,96},{128,112},... | collective-permute-start | bytes 2024 | tf_op jit(solution)/shard_map/ppermute | solution.py:17
  65.6 6.1 %collective-permute-done.5 = bf16[16,3,7]{0,2,1:T(8,128)(2,1)S(1)} collective-permute-done((bf16[16,3,7]{0,2,1:T(8,128)(2,1)S(1)}, bf16[16,3,7]{0,2,1:T(8,128)(2,1)S(1)}, u32[]{:S(2)}, u32[]{:S(2)}) %collective-permute-start.5) | collective-permute-done | bytes 704 | tf_op jit(solution)/shard_map/ppermute | solution.py:17
  71.7 6.4 %collective-permute-start.6 = (bf16[16,3,7]{0,2,1:T(8,128)(2,1)S(1)}, bf16[16,3,7]{0,2,1:T(8,128)(2,1)S(1)}, u32[]{:S(2)}, u32[]{:S(2)}) collective-permute-start(bf16[16,3,7]{0,2,1:T(8,128)(2,1)S(1)} %copy-done.12), channel_id=1, source_target_pairs={{0,32},{16,48},{32,64},{48,80},{64,96},{80,112},{96,128},{112,144}... | collective-permute-start | bytes 2024 | tf_op jit(solution)/shard_map/ppermute | solution.py:17
  78.2 0.5 dynamic_update_slice.53
  78.7 0.7 collective-permute-done.6
  79.5 2.1 collective-permute-start.7
  81.6 0.5 dynamic_update_slice.54
  82.2 7.3 %collective-permute-done.7 = bf16[16,3,7]{0,2,1:T(8,128)(2,1)S(1)} collective-permute-done((bf16[16,3,7]{0,2,1:T(8,128)(2,1)S(1)}, bf16[16,3,7]{0,2,1:T(8,128)(2,1)S(1)}, u32[]{:S(2)}, u32[]{:S(2)}) %collective-permute-start.7) | collective-permute-done | bytes 704 | tf_op jit(solution)/shard_map/ppermute | solution.py:17
  89.5 0.5 dynamic_update_slice.55
  90.1 2.0 copy.44
  92.1 1.4 dynamic-slice_select_fusion.7
  93.5 7.7 %dynamic_update_slice.48 = bf16[144,3,896]{0,2,1:T(8,128)(2,1)S(1)} dynamic-update-slice(bf16[144,3,896]{0,2,1:T(8,128)(2,1)S(1)} %concatenate.23, bf16[16,3,896]{0,2,1:T(8,128)(2,1)S(1)} %dynamic-slice_select_fusion.7, s32[]{:T(128)S(6)} %select_n.192, s32[]{:T(128)} %constant.53.clone.1, s32[]{:T(128)} %constant.53.clone.1) | dynamic-update-slice | bytes 172036 | tf_op jit(solution)/shard_map/dynamic_update_slice | solution.py:86
  101.2 1.3 copy.47
  102.9 10.2 %dynamic_update_slice.49 = bf16[144,3,896]{0,2,1:T(8,128)(2,1)S(1)} dynamic-update-slice(bf16[144,3,896]{0,2,1:T(8,128)(2,1)S(1)} %dynamic_update_slice.48, bf16[16,3,896]{0,2,1:T(8,128)(2,1)S(1)} %dynamic-slice_select_fusion.6, s32[]{:T(128)S(6)} %select_n.197, s32[]{:T(128)} %constant.53.clone.1, s32[]{:T(128)} %constant.53.clone.1) | dynamic-update-slice | bytes 172036 | tf_op jit(solution)/shard_map/dynamic_update_slice | solution.py:86
  113.1 1.3 copy.50
  114.7 10.2 %dynamic_update_slice.50 = bf16[144,3,896]{0,2,1:T(8,128)(2,1)S(1)} dynamic-update-slice(bf16[144,3,896]{0,2,1:T(8,128)(2,1)S(1)} %dynamic_update_slice.49, bf16[16,3,896]{0,2,1:T(8,128)(2,1)S(1)} %dynamic-slice_select_fusion.5, s32[]{:T(128)S(6)} %select_n.202, s32[]{:T(128)} %constant.53.clone.1, s32[]{:T(128)} %constant.53.clone.1) | dynamic-update-slice | bytes 172036 | tf_op jit(solution)/shard_map/dynamic_update_slice | solution.py:86
  125.7 10.2 %dynamic_update_slice.51 = bf16[144,3,896]{0,2,1:T(8,128)(2,1)S(1)} dynamic-update-slice(bf16[144,3,896]{0,2,1:T(8,128)(2,1)S(1)} %dynamic_update_slice.50, bf16[16,3,896]{0,2,1:T(8,128)(2,1)S(1)} %dynamic-slice_select_fusion.4, s32[]{:T(128)S(6)} %select_n.207, s32[]{:T(128)} %constant.53.clone.1, s32[]{:T(128)} %constant.53.clone.1) | dynamic-update-slice | bytes 172036 | tf_op jit(solution)/shard_map/dynamic_update_slice | solution.py:86
  136.1 1.2 fusion.55
  137.2 0.5 convolution_convert_fusion.3
  137.8 2.7 %convolution_convert_fusion = bf16[896,1792]{1,0:T(8,128)(2,1)} fusion(bf16[128,896]{0,1:T(8,128)(2,1)S(1)} %bitcast.87, bf16[1,1,128,1792]{3,2,1,0:T(8,128)(2,1)S(1)} %copy-done), kind=kOutput, calls=%fused_computation.2 | convolution fusion | flops 412647424 | bytes 3899392 | tf_op jit(solution)/shard_map/dot_general | solution.py:148
  140.5 3.0 %convolution_convert_fusion.2 = bf16[128,896]{1,0:T(8,128)(2,1)S(1)} fusion(bf16[896,1792]{1,0:T(8,128)(2,1)} %all-gather.2.cloned.1.call-done, bf16[1,1,128,1792]{3,2,1,0:T(8,128)(2,1)S(1)} %copy-done), kind=kOutput, calls=%fused_computation.25 | convolution fusion | flops 411156480 | bytes 3899392 | tf_op jit(solution)/shard_map/dot_general | solution.py:49
  144.0 1.5 fusion.12
  145.6 1.6 fusion.13
  147.2 0.6 fusion.30
  148.4 2.0 fusion.25
  150.5 2.0 copy.59
  152.4 2.1 collective-permute-start.8
  154.6 0.9 copy.61
  155.5 5.6 %collective-permute-start.9 = (bf16[16,3,896]{2,0,1:T(8,128)(2,1)}, bf16[16,3,896]{2,0,1:T(8,128)(2,1)}, u32[]{:S(2)}, u32[]{:S(2)}) collective-permute-start(bf16[16,3,896]{2,0,1:T(8,128)(2,1)} %copy.61), channel_id=1, source_target_pairs={{0,16},{16,32},{32,48},{48,64},{64,80},{80,96},{96,112},{112,128},... | collective-permute-start | bytes 258056 | tf_op jit(solution)/shard_map/ppermute | solution.py:17
  161.1 0.9 copy.63
  162.0 1.9 collective-permute-start.10
  164.1 8.2 %collective-permute-start.11 = (bf16[16,3,896]{2,0,1:T(8,128)(2,1)S(1)}, bf16[16,3,896]{2,0,1:T(8,128)(2,1)}, u32[]{:S(2)}, u32[]{:S(2)}) collective-permute-start(bf16[16,3,896]{2,0,1:T(8,128)(2,1)S(1)} %copy.65), channel_id=1, source_target_pairs={{0,32},{16,48},{32,64},{48,80},{64,96},{80,112},{96,128},{112,144}... | collective-permute-start | bytes 258056 | tf_op jit(solution)/shard_map/ppermute | solution.py:17
  172.3 3.4 %fusion.2 = bf16[1,1,128,1792]{3,2,1,0:T(8,128)(2,1)} fusion(bf16[128,896]{0,1:T(8,128)(2,1)S(1)} %bitcast.88, bf16[896,1792]{1,0:T(8,128)(2,1)} %all-gather.2.cloned.1.call-done), kind=kOutput, calls=%fused_computation.4 | convolution fusion | flops 411271168 | bytes 3899392 | tf_op jit(solution)/shard_map/dot_general | solution.py:48
  175.8 2.0 copy.60
  177.9 1.5 dynamic-slice_select_fusion.3
  179.3 10.2 %dynamic_update_slice.60 = bf16[144,3,896]{0,2,1:T(8,128)(2,1)S(1)} dynamic-update-slice(bf16[144,3,896]{0,2,1:T(8,128)(2,1)S(1)} %concatenate.28, bf16[16,3,896]{0,2,1:T(8,128)(2,1)S(1)} %dynamic-slice_select_fusion.3, s32[]{:T(128)S(6)} %select_n.190, s32[]{:T(128)} %constant.53.clone.1, s32[]{:T(128)} %constant.53.clone.1) | dynamic-update-slice | bytes 172036 | tf_op jit(solution)/shard_map/dynamic_update_slice | solution.py:86
  189.5 1.3 copy.62
  191.2 10.2 %dynamic_update_slice.61 = bf16[144,3,896]{0,2,1:T(8,128)(2,1)S(1)} dynamic-update-slice(bf16[144,3,896]{0,2,1:T(8,128)(2,1)S(1)} %dynamic_update_slice.60, bf16[16,3,896]{0,2,1:T(8,128)(2,1)S(1)} %dynamic-slice_select_fusion.2, s32[]{:T(128)S(6)} %select_n.195, s32[]{:T(128)} %constant.53.clone.1, s32[]{:T(128)} %constant.53.clone.1) | dynamic-update-slice | bytes 172036 | tf_op jit(solution)/shard_map/dynamic_update_slice | solution.py:86
  201.4 1.3 copy.64
  203.0 10.2 %dynamic_update_slice.62 = bf16[144,3,896]{0,2,1:T(8,128)(2,1)S(1)} dynamic-update-slice(bf16[144,3,896]{0,2,1:T(8,128)(2,1)S(1)} %dynamic_update_slice.61, bf16[16,3,896]{0,2,1:T(8,128)(2,1)S(1)} %dynamic-slice_select_fusion.1, s32[]{:T(128)S(6)} %select_n.200, s32[]{:T(128)} %constant.53.clone.1, s32[]{:T(128)} %constant.53.clone.1) | dynamic-update-slice | bytes 172036 | tf_op jit(solution)/shard_map/dynamic_update_slice | solution.py:86
  213.2 1.3 copy.66
  214.8 10.2 %dynamic_update_slice.63 = bf16[144,3,896]{0,2,1:T(8,128)(2,1)S(1)} dynamic-update-slice(bf16[144,3,896]{0,2,1:T(8,128)(2,1)S(1)} %dynamic_update_slice.62, bf16[16,3,896]{0,2,1:T(8,128)(2,1)S(1)} %dynamic-slice_select_fusion, s32[]{:T(128)S(6)} %select_n.205, s32[]{:T(128)} %constant.53.clone.1, s32[]{:T(128)} %constant.53.clone.1) | dynamic-update-slice | bytes 172036 | tf_op jit(solution)/shard_map/dynamic_update_slice | solution.py:86
  225.1 1.1 copy.67
  226.3 1.7 bitcast_convert_fusion
  (112 shorter events, 7.5 us)
Async XLA Ops:
  7.2 130.6 %copy-start = (bf16[1,1,128,1792]{3,2,1,0:T(8,128)(2,1)S(1)}, bf16[1,1,128,1792]{3,2,1,0:T(8,128)(2,1)}, u32[]{:S(2)}) copy-start(bf16[1,1,128,1792]{3,2,1,0:T(8,128)(2,1)} %param.13) | copy-start | bytes 1376260
  7.2 133.3 %all-gather.2.cloned.1.call-start = ((), (), s32[]{:S(2)}) async-start(), calls=%async_computation.1 | async-start | bytes 3411968 | tf_op jit(solution)/shard_map/all_gather | solution.py:100
  7.9 218.3 %reduce-scatter.2.cloned.1.call-start = ((), (), s32[]{:S(2)}) async-start(), calls=%async_computation.2 | async-start | bytes 3411968 | tf_op jit(solution)/shard_map/reduce_scatter | solution.py:151
  18.0 24.8 %copy-start.4 = (pred[16]{0:T(512)(128)(4,1)}, pred[16]{0:T(512)(128)(4,1)S(1)}, u32[]{:S(2)}) copy-start(pred[16]{0:T(512)(128)(4,1)S(1)} %get-tuple-element.49) | copy-start | bytes 52
  18.0 24.8 %copy-start.6 = (pred[16]{0:T(512)(128)(4,1)}, pred[16]{0:T(512)(128)(4,1)S(1)}, u32[]{:S(2)}) copy-start(pred[16]{0:T(512)(128)(4,1)S(1)} %get-tuple-element.50) | copy-start | bytes 52
  20.5 22.3 %copy-start.8 = (pred[16]{0:T(512)(128)(4,1)}, pred[16]{0:T(512)(128)(4,1)S(1)}, u32[]{:S(2)}) copy-start(pred[16]{0:T(512)(128)(4,1)S(1)} %get-tuple-element.51) | copy-start | bytes 52
  20.5 22.3 %copy-start.10 = (pred[16]{0:T(512)(128)(4,1)}, pred[16]{0:T(512)(128)(4,1)S(1)}, u32[]{:S(2)}) copy-start(pred[16]{0:T(512)(128)(4,1)S(1)} %get-tuple-element.52) | copy-start | bytes 52
  23.1 19.7 %copy-start.3 = (bf16[1,1,128,3,7]{2,4,3,1,0:T(8,128)(2,1)S(1)}, bf16[1,1,128,3,7]{2,4,3,1,0:T(8,128)(2,1)}, u32[]{:S(2)}) copy-start(bf16[1,1,128,3,7]{2,4,3,1,0:T(8,128)(2,1)} %param.8) | copy-start | bytes 16132
  25.1 29.1 %copy-start.26 = (s32[1,1,128]{2,1,0:T(1,128)S(1)}, s32[1,1,128]{2,1,0:T(1,128)}, u32[]{:S(2)}) copy-start(s32[1,1,128]{2,1,0:T(1,128)} %param.9) | copy-start | bytes 1540
  25.1 64.9 %collective-permute-start = (bf16[16,3,896]{2,0,1:T(8,128)(2,1)}, bf16[16,3,896]{2,0,1:T(8,128)(2,1)}, u32[]{:S(2)}, u32[]{:S(2)}) collective-permute-start(bf16[16,3,896]{2,0,1:T(8,128)(2,1)} %copy.43), channel_id=1, source_target_pairs={{0,16},{16,32},{32,48},{48,64},{64,80},{80,96},{96,112},{112,128},... | collective-permute-start | bytes 258056 | tf_op jit(solution)/shard_map/ppermute | solution.py:17
  28.8 72.4 %collective-permute-start.1 = (bf16[16,3,896]{2,0,1:T(8,128)(2,1)}, bf16[16,3,896]{2,0,1:T(8,128)(2,1)}, u32[]{:S(2)}, u32[]{:S(2)}) collective-permute-start(bf16[16,3,896]{2,0,1:T(8,128)(2,1)} %copy.46), channel_id=1, source_target_pairs={{16,0},{32,16},{48,32},{64,48},{80,64},{96,80},{112,96},{128,112},... | collective-permute-start | bytes 258056 | tf_op jit(solution)/shard_map/ppermute | solution.py:17
  32.2 80.9 %collective-permute-start.2 = (bf16[16,3,896]{2,0,1:T(8,128)(2,1)S(1)}, bf16[16,3,896]{2,0,1:T(8,128)(2,1)}, u32[]{:S(2)}, u32[]{:S(2)}) collective-permute-start(bf16[16,3,896]{2,0,1:T(8,128)(2,1)S(1)} %copy.49), channel_id=1, source_target_pairs={{0,32},{16,48},{32,64},{48,80},{64,96},{80,112},{96,128},{112,144}... | collective-permute-start | bytes 258056 | tf_op jit(solution)/shard_map/ppermute | solution.py:17
  40.8 84.1 %collective-permute-start.3 = (bf16[16,3,896]{2,0,1:T(8,128)(2,1)S(1)}, bf16[16,3,896]{2,0,1:T(8,128)(2,1)S(1)}, u32[]{:S(2)}, u32[]{:S(2)}) collective-permute-start(bf16[16,3,896]{2,0,1:T(8,128)(2,1)S(1)} %copy.52), channel_id=1, source_target_pairs={{32,0},{48,16},{64,32},{80,48},{96,64},{112,80},{128,96},{144,112}... | collective-permute-start | bytes 258056 | tf_op jit(solution)/shard_map/ppermute | solution.py:17
  43.5 17.7 %collective-permute-start.4 = (bf16[16,3,7]{0,2,1:T(8,128)(2,1)}, bf16[16,3,7]{0,2,1:T(8,128)(2,1)S(1)}, u32[]{:S(2)}, u32[]{:S(2)}) collective-permute-start(bf16[16,3,7]{0,2,1:T(8,128)(2,1)} %get-tuple-element.24), channel_id=1, source_target_pairs={{0,16},{16,32},{32,48},{48,64},{64,80},{80,96},{96,112},{112,128},... | collective-permute-start | bytes 2024 | tf_op jit(solution)/shard_map/ppermute | solution.py:17
  59.9 32.1 %copy-start.16 = (pred[16]{0:T(512)(128)(4,1)}, pred[16]{0:T(512)(128)(4,1)S(1)}, u32[]{:S(2)}) copy-start(pred[16]{0:T(512)(128)(4,1)S(1)} %iota_compare_fusion.7) | copy-start | bytes 52
  60.0 18.2 %copy-start.18 = (pred[16]{0:T(512)(128)(4,1)}, pred[16]{0:T(512)(128)(4,1)S(1)}, u32[]{:S(2)}) copy-start(pred[16]{0:T(512)(128)(4,1)S(1)} %iota_compare_fusion.5) | copy-start | bytes 52
  60.6 0.5 copy-start.14
  60.7 0.7 copy-start.13
  60.7 11.0 %copy-start.12 = (bf16[16,3,7]{0,2,1:T(8,128)(2,1)S(1)}, bf16[16,3,7]{0,2,1:T(8,128)(2,1)}, u32[]{:S(2)}) copy-start(bf16[16,3,7]{0,2,1:T(8,128)(2,1)} %get-tuple-element.23) | copy-start | bytes 2020
  60.8 20.8 %copy-start.21 = (pred[16]{0:T(512)(128)(4,1)S(1)}, pred[16]{0:T(512)(128)(4,1)}, u32[]{:S(2)}) copy-start(pred[16]{0:T(512)(128)(4,1)} %iota_compare_fusion.3) | copy-start | bytes 52
  61.1 29.0 %copy-start.24 = (pred[16]{0:T(512)(128)(4,1)}, pred[16]{0:T(512)(128)(4,1)S(1)}, u32[]{:S(2)}) copy-start(pred[16]{0:T(512)(128)(4,1)S(1)} %iota_compare_fusion.1) | copy-start | bytes 52
  61.4 10.3 %collective-permute-start.5 = (bf16[16,3,7]{0,2,1:T(8,128)(2,1)S(1)}, bf16[16,3,7]{0,2,1:T(8,128)(2,1)S(1)}, u32[]{:S(2)}, u32[]{:S(2)}) collective-permute-start(bf16[16,3,7]{0,2,1:T(8,128)(2,1)S(1)} %copy-done.13), channel_id=1, source_target_pairs={{16,0},{32,16},{48,32},{64,48},{80,64},{96,80},{112,96},{128,112},... | collective-permute-start | bytes 2024 | tf_op jit(solution)/shard_map/ppermute | solution.py:17
  71.7 7.7 %collective-permute-start.6 = (bf16[16,3,7]{0,2,1:T(8,128)(2,1)S(1)}, bf16[16,3,7]{0,2,1:T(8,128)(2,1)S(1)}, u32[]{:S(2)}, u32[]{:S(2)}) collective-permute-start(bf16[16,3,7]{0,2,1:T(8,128)(2,1)S(1)} %copy-done.12), channel_id=1, source_target_pairs={{0,32},{16,48},{32,64},{48,80},{64,96},{80,112},{96,128},{112,144}... | collective-permute-start | bytes 2024 | tf_op jit(solution)/shard_map/ppermute | solution.py:17
  79.5 10.0 %collective-permute-start.7 = (bf16[16,3,7]{0,2,1:T(8,128)(2,1)S(1)}, bf16[16,3,7]{0,2,1:T(8,128)(2,1)S(1)}, u32[]{:S(2)}, u32[]{:S(2)}) collective-permute-start(bf16[16,3,7]{0,2,1:T(8,128)(2,1)S(1)} %get-tuple-element.22), channel_id=1, source_target_pairs={{32,0},{48,16},{64,32},{80,48},{96,64},{112,80},{128,96},{144,112}... | collective-permute-start | bytes 2024 | tf_op jit(solution)/shard_map/ppermute | solution.py:17
  93.5 9.0 %copy-start.19 = (pred[16]{0:T(512)(128)(4,1)S(1)}, pred[16]{0:T(512)(128)(4,1)}, u32[]{:S(2)}) copy-start(pred[16]{0:T(512)(128)(4,1)} %copy-done.18) | copy-start | bytes 52
  102.9 11.5 %copy-start.22 = (pred[16]{0:T(512)(128)(4,1)S(1)}, pred[16]{0:T(512)(128)(4,1)}, u32[]{:S(2)}) copy-start(pred[16]{0:T(512)(128)(4,1)} %iota_compare_fusion.3) | copy-start | bytes 52
  114.7 10.6 %copy-start.25 = (pred[16]{0:T(512)(128)(4,1)S(1)}, pred[16]{0:T(512)(128)(4,1)}, u32[]{:S(2)}) copy-start(pred[16]{0:T(512)(128)(4,1)} %copy-done.24) | copy-start | bytes 52
  136.0 8.0 %copy-start.1 = (bf16[128,1,896]{0,2,1:T(8,128)(2,1)}, bf16[128,1,896]{0,2,1:T(8,128)(2,1)S(1)}, u32[]{:S(2)}) copy-start(bf16[128,1,896]{0,2,1:T(8,128)(2,1)S(1)} %get-tuple-element.16) | copy-start | bytes 688132
  145.6 1.6 copy-start.2
  147.2 0.6 copy-start.15
  147.7 0.6 copy-start.17
  147.8 0.7 copy-start.20
  147.8 0.7 copy-start.23
  152.4 23.4 %collective-permute-start.8 = (bf16[16,3,896]{2,0,1:T(8,128)(2,1)}, bf16[16,3,896]{2,0,1:T(8,128)(2,1)}, u32[]{:S(2)}, u32[]{:S(2)}) collective-permute-start(bf16[16,3,896]{2,0,1:T(8,128)(2,1)} %copy.59), channel_id=1, source_target_pairs={{16,0},{32,16},{48,32},{64,48},{80,64},{96,80},{112,96},{128,112},... | collective-permute-start | bytes 258056 | tf_op jit(solution)/shard_map/ppermute | solution.py:17
  155.5 34.1 %collective-permute-start.9 = (bf16[16,3,896]{2,0,1:T(8,128)(2,1)}, bf16[16,3,896]{2,0,1:T(8,128)(2,1)}, u32[]{:S(2)}, u32[]{:S(2)}) collective-permute-start(bf16[16,3,896]{2,0,1:T(8,128)(2,1)} %copy.61), channel_id=1, source_target_pairs={{0,16},{16,32},{32,48},{48,64},{64,80},{80,96},{96,112},{112,128},... | collective-permute-start | bytes 258056 | tf_op jit(solution)/shard_map/ppermute | solution.py:17
  162.0 39.4 %collective-permute-start.10 = (bf16[16,3,896]{2,0,1:T(8,128)(2,1)}, bf16[16,3,896]{2,0,1:T(8,128)(2,1)}, u32[]{:S(2)}, u32[]{:S(2)}) collective-permute-start(bf16[16,3,896]{2,0,1:T(8,128)(2,1)} %copy.63), channel_id=1, source_target_pairs={{32,0},{48,16},{64,32},{80,48},{96,64},{112,80},{128,96},{144,112}... | collective-permute-start | bytes 258056 | tf_op jit(solution)/shard_map/ppermute | solution.py:17
  164.1 49.0 %collective-permute-start.11 = (bf16[16,3,896]{2,0,1:T(8,128)(2,1)S(1)}, bf16[16,3,896]{2,0,1:T(8,128)(2,1)}, u32[]{:S(2)}, u32[]{:S(2)}) collective-permute-start(bf16[16,3,896]{2,0,1:T(8,128)(2,1)S(1)} %copy.65), channel_id=1, source_target_pairs={{0,32},{16,48},{32,64},{48,80},{64,96},{80,112},{96,128},{112,144}... | collective-permute-start | bytes 258056 | tf_op jit(solution)/shard_map/ppermute | solution.py:17
  175.7 2.2 copy-start.11
  179.3 11.5 %copy-start.9 = (pred[16]{0:T(512)(128)(4,1)S(1)}, pred[16]{0:T(512)(128)(4,1)}, u32[]{:S(2)}) copy-start(pred[16]{0:T(512)(128)(4,1)} %copy-done.8) | copy-start | bytes 52
  191.1 11.5 %copy-start.7 = (pred[16]{0:T(512)(128)(4,1)S(1)}, pred[16]{0:T(512)(128)(4,1)}, u32[]{:S(2)}) copy-start(pred[16]{0:T(512)(128)(4,1)} %copy-done.6) | copy-start | bytes 52
  203.0 11.5 %copy-start.5 = (pred[16]{0:T(512)(128)(4,1)S(1)}, pred[16]{0:T(512)(128)(4,1)}, u32[]{:S(2)}) copy-start(pred[16]{0:T(512)(128)(4,1)} %copy-done.4) | copy-start | bytes 52
Sparse Core Ops, SparseCore 0:
  10.7 51.0 all-gather.1
  140.6 61.5 reduce-scatter.1
where the time goes:
time: 236 us; the launch traced here: 235 us
  local copies, waits for them, and re-layouts  108 us (46%)
  starting transfers between devices  48.5 us (21%)
  between operations  32.9 us (14%)
  other arithmetic  16.1 us (7%)
  waiting for transfers between devices  14.9 us (6%)
  matrix products  14.8 us (6%)
    dynamic_update_slice x12, local copies, waits for them, and re-layouts, put_rows(): lax.dynamic_update_slice_in_dim(buffer, jnp.where(present, piece, old), a...  80.6 us
    ppermute x12, starting transfers between devices, shifted(): return lax.ppermute(block, axis, route)  48.4 us
    ppermute x12, waiting for transfers between devices, shifted(): return lax.ppermute(block, axis, route)  14.2 us
    ppermute x8, local copies, waits for them, and re-layouts, shifted(): return lax.ppermute(block, axis, route)  10.7 us
    select_n x8, local copies, waits for them, and re-layouts, cut_rows(): return jnp.where(present, piece, jnp.zeros_like(piece))  7.35 us
    select_n x12, other arithmetic, put_rows(): jnp.where(present, piece, old)  5.35 us
    select_n x3, other arithmetic, cut_rows(): return jnp.where(present, piece, jnp.zeros_like(piece))  4.74 us
  transfers between devices with their start and end apart: 14, of which 3 were waited for; matrix products, arithmetic and copies ran while one was open for 58% of the time, Pallas kernels for 0%

commit v1 on v0

v1 whole, which is shorter than its diff:
```python
import functools
import math

import jax
import jax.numpy as jnp
from jax import lax
from jax.experimental import pallas as pl
from jax.experimental.pallas import tpu as pltpu
from jax.sharding import PartitionSpec as P

HEADS = 8
OFFSETS = (1, -1, 2, -2)
SLOT = 16
LANES = 128
F32 = jnp.float32
BF16 = jnp.bfloat16
NT = (((1,), (1,)), ((), ()))
TN = (((0,), (0,)), ((), ()))


def shifted(block, axis, distance):
    devices = range(lax.axis_size(axis))
    route = [(i - distance, i) for i in devices if i - distance in devices]
    return lax.ppermute(block, axis, route)


def dot(a, b, dims=(((1,), (0,)), ((), ()))):
    return lax.dot_general(a, b, dims, preferred_element_type=F32)


def sent_spans(table, at):
    return [(table[0, d, at], table[1, d, at]) for d in range(4)]


def placed_spans(table, at, group):
    spans = []
    for d in range(4):
        source = at - OFFSETS[d]
        allowed = (source >= 0) & (source < group)
        source = jnp.clip(source, 0, group - 1)
        spans.append((table[2, d, source], jnp.where(allowed, table[1, d, source], 0)))
    return spans


def one_hot(spans, rows, slots_first):
    shape = (4 * SLOT, rows) if slots_first else (rows, 4 * SLOT)
    slot = lax.broadcasted_iota(jnp.int32, shape, 0 if slots_first else 1)
    row = lax.broadcasted_iota(jnp.int32, shape, 1 if slots_first else 0)
    hot = None
    for d, (first, length) in enumerate(spans):
        i = slot - SLOT * d
        here = (i >= 0) & (i < length) & (row == first + i)
        hot = here if hot is None else hot | here
    return jnp.where(hot, 1.0, 0.0).astype(BF16)


def expanded(select, scales):
    columns = dot(select, scales, NT)
    return jnp.concatenate(
        [
            jnp.broadcast_to(columns[:, b : b + 1], (select.shape[0], LANES))
            for b in range(scales.shape[0])
        ],
        axis=1,
    )


def window(head, size):
    low = head * size // LANES
    high = ((head + 1) * size - 1) // LANES + 1
    return low, high


def head_mask(head, size, rows):
    low, high = window(head, size)
    column = lax.broadcasted_iota(jnp.int32, (rows, (high - low) * LANES), 1) + low * LANES
    return (column >= head * size) & (column < (head + 1) * size)


def add_tiles(tiles, part, low):
    for i in range(part.shape[1] // LANES):
        piece = part[:, i * LANES : (i + 1) * LANES]
        tiles[low + i] = piece if tiles[low + i] is None else tiles[low + i] + piece


def pack_kernel(table, codes, scales, *sent):
    at = lax.axis_index("dp")
    rows = codes.shape[1]
    select = one_hot(sent_spans(table, at), rows, True)
    for c in range(3):
        values = dot(select, codes[c]) * expanded(select, scales[c])
        values = values.astype(BF16)
        for d in range(4):
            sent[d][c] = values[d * SLOT : (d + 1) * SLOT]


def forward_kernel(
    group, table, kept, segments, codes, scales, r0, r1, r2, r3, grad_out,
    term, context_out, balanced, probs_out, turned
):
    rows, width = codes.shape[1:]
    size = width // HEADS
    factor = 1.0 / math.sqrt(size)

    @pl.when(pl.program_id(0) == 0)
    def _():
        at = lax.axis_index("dp")
        keep = kept[0, 0]
        spans = placed_spans(table, at, group)
        place = one_hot(spans, rows, False)
        row = lax.broadcasted_iota(jnp.int32, (rows, rows), 0)
        lane = lax.broadcasted_iota(jnp.int32, (rows, rows), 1)
        eye = row == lane
        identity = jnp.where(eye, 1.0, 0.0).astype(BF16)
        along = jnp.broadcast_to(segments[...], (rows, rows))
        labels = jnp.where(lane < keep, along, -1)
        for d, (first, length) in enumerate(spans):
            labels = jnp.where((lane >= first) & (lane < first + length), 100000 + d, labels)
        labels = labels.astype(F32)
        down = jnp.sum(jnp.where(eye, labels, 0.0), axis=1, keepdims=True)
        same = labels == down
        column_row = lax.broadcasted_iota(jnp.int32, (rows, width), 0)
        for c in range(3):
            own = (codes[c].astype(F32) * expanded(identity, scales[c])).astype(BF16)
            own = jnp.where(column_row < keep, own.astype(F32), 0.0)
            arrived = jnp.concatenate([r0[c], r1[c], r2[c], r3[c]], axis=0)
            balanced[c] = (own + dot(place, arrived)).astype(BF16)
        tiles = [None] * (width // LANES)
        for head in range(HEADS):
            low, high = window(head, size)
            cut = slice(low * LANES, high * LANES)
            mask = head_mask(head, size, rows)
            query = balanced[0, :, cut]
            keys = jnp.where(mask, balanced[1, :, cut].astype(F32), 0.0).astype(BF16)
            values = jnp.where(mask, balanced[2, :, cut].astype(F32), 0.0).astype(BF16)
            scores = jnp.where(same, dot(query, keys, NT) * factor, -jnp.inf)
            weights = jnp.exp(scores - jnp.max(scores, axis=1, keepdims=True))
            probs = weights / jnp.sum(weights, axis=1, keepdims=True)
            probs_out[head] = probs
            add_tiles(tiles, dot(probs.astype(BF16), values), low)
        context = jnp.concatenate(tiles, axis=1)
        context_out[...] = context.astype(BF16)
        turned[...] = context.T.astype(BF16)

    term[...] = dot(turned[...], grad_out[...]).astype(BF16)


def backward_kernel(
    group, table, kept, w, grad_out, context, balanced, probs_in, scales,
    output, home, b0, b1, b2, b3, total_out, grad_context
):
    step = pl.program_id(0)
    rows, width = balanced.shape[1:]
    size = width // HEADS
    factor = 1.0 / math.sqrt(size)
    part = dot(context[...], w[...])

    @pl.when(step == 0)
    def _():
        total_out[...] = part

    @pl.when(step > 0)
    def _():
        total_out[...] += part

    grad_context[step] = dot(grad_out[...], w[...], NT).astype(BF16)

    @pl.when(step == pl.num_programs(0) - 1)
    def _():
        output[...] = total_out[...].astype(BF16)
        at = lax.axis_index("dp")
        keep = kept[0, 0]
        count = width // LANES
        grads = [[None] * count for _ in range(3)]
        for head in range(HEADS):
            low, high = window(head, size)
            cut = slice(low * LANES, high * LANES)
            mask = head_mask(head, size, rows)

            def masked(values):
                return jnp.where(mask, values.astype(F32), 0.0).astype(BF16)

            query = masked(balanced[0, :, cut])
            keys = masked(balanced[1, :, cut])
            values = balanced[2, :, cut]
            upstream = masked(jnp.concatenate([grad_context[i] for i in range(low, high)], axis=1))
            probs = probs_in[head]
            grad_probs = dot(upstream, values, NT)
            total = jnp.sum(probs * grad_probs, axis=1, keepdims=True)
            grad_scores = probs * (grad_probs - total) * factor
            add_tiles(grads[0], dot(grad_scores.astype(BF16), keys), low)
            add_tiles(grads[1], dot(grad_scores.T.astype(BF16), query), low)
            add_tiles(grads[2], dot(probs.T.astype(BF16), upstream), low)
        select = one_hot(placed_spans(table, at, group), rows, True)
        row = lax.broadcasted_iota(jnp.int32, (rows, rows), 0)
        lane = lax.broadcasted_iota(jnp.int32, (rows, rows), 1)
        identity = jnp.where((row == lane) & (row < keep), 1.0, 0.0).astype(BF16)
        for c in range(3):
            grad = jnp.concatenate(grads[c], axis=1)
            home[c] = (grad * expanded(identity, scales[c])).astype(BF16)
            back = dot(select, grad.astype(BF16)).astype(BF16)
            for d, ref in enumerate((b0, b1, b2, b3)):
                ref[c] = back[d * SLOT : (d + 1) * SLOT]


def return_kernel(table, home, scales, r0, r1, r2, r3, grad_codes):
    at = lax.axis_index("dp")
    rows = home.shape[1]
    place = one_hot(sent_spans(table, at), rows, False)
    row = lax.broadcasted_iota(jnp.int32, (rows, rows), 0)
    lane = lax.broadcasted_iota(jnp.int32, (rows, rows), 1)
    identity = jnp.where(row == lane, 1.0, 0.0).astype(BF16)
    for c in range(3):
        arrived = jnp.concatenate([r0[c], r1[c], r2[c], r3[c]], axis=0)
        moved = dot(place, arrived) * expanded(identity, scales[c])
        grad_codes[c] = (home[c].astype(F32) + moved).astype(BF16)


def whole(shape):
    return pl.BlockSpec(shape, lambda *_: (0,) * len(shape))


def local(qkv_codes, block_scales, home_segments, kept_rows, pack_list, w_out, cotangent):
    group = lax.axis_size("dp")
    codes = jnp.transpose(qkv_codes[0, 0], (1, 0, 2))
    scales = jnp.transpose(block_scales[0, 0], (1, 2, 0))
    segments = home_segments[0]
    table = jnp.transpose(pack_list[:, 0], (2, 1, 0))
    grad_out = cotangent[0, 0]
    _, rows, width = codes.shape
    depth = w_out.shape[1]
    blocks = scales.shape[1]
    smem = pl.BlockSpec(memory_space=pltpu.SMEM)
    params = pltpu.CompilerParams(vmem_limit_bytes=24 * 1024 * 1024)
    piece = jax.ShapeDtypeStruct((3, SLOT, width), BF16)
    piece_spec = whole((3, SLOT, width))
    codes_spec = whole((3, rows, width))
    scales_spec = whole((3, blocks, rows))

    w_full = lax.all_gather(w_out, "fsdp", axis=0, tiled=True)

    sent = pl.pallas_call(
        pack_kernel,
        out_shape=[piece] * 4,
        in_specs=[smem, codes_spec, scales_spec],
        out_specs=[piece_spec] * 4,
        compiler_params=params,
        name="pack",
    )(table, codes, scales)
    received = [shifted(sent[d], "dp", OFFSETS[d]) for d in range(4)]

    chunk = 256
    term, context, balanced, probs = pl.pallas_call(
        functools.partial(forward_kernel, group),
        grid=(depth // chunk,),
        out_shape=[
            jax.ShapeDtypeStruct((width, depth), BF16),
            jax.ShapeDtypeStruct((rows, width), BF16),
            jax.ShapeDtypeStruct((3, rows, width), BF16),
            jax.ShapeDtypeStruct((HEADS, rows, rows), F32),
        ],
        in_specs=[smem, smem, whole((1, rows)), codes_spec, scales_spec]
        + [piece_spec] * 4
        + [pl.BlockSpec((rows, chunk), lambda n: (0, n))],
        out_specs=[
            pl.BlockSpec((width, chunk), lambda n: (0, n)),
            whole((rows, width)),
            codes_spec,
            whole((HEADS, rows, rows)),
        ],
        scratch_shapes=[pltpu.VMEM((width, rows), BF16)],
        compiler_params=params,
        name="forward",
    )(table, kept_rows, segments, codes, scales, *received, grad_out)

    grad_w = lax.psum_scatter(term, "fsdp", scatter_dimension=0, tiled=True).astype(F32)

    output, home, *back = pl.pallas_call(
        functools.partial(backward_kernel, group),
        grid=(width // LANES,),
        out_shape=[
            jax.ShapeDtypeStruct((rows, depth), BF16),
            jax.ShapeDtypeStruct((3, rows, width), BF16),
        ]
        + [piece] * 4,
        in_specs=[
            smem,
            smem,
            pl.BlockSpec((LANES, depth), lambda n: (n, 0)),
            whole((rows, depth)),
            pl.BlockSpec((rows, LANES), lambda n: (0, n)),
            codes_spec,
            whole((HEADS, rows, rows)),
            scales_spec,
        ],
        out_specs=[whole((rows, depth)), codes_spec] + [piece_spec] * 4,
        scratch_shapes=[
            pltpu.VMEM((rows, depth), F32),
            pltpu.VMEM((width // LANES, rows, LANES), BF16),
        ],
        compiler_params=params,
        name="backward",
    )(table, kept_rows, w_full, grad_out, context, balanced, probs, scales)
    returned = [shifted(back[d], "dp", -OFFSETS[d]) for d in range(4)]

    grad_codes = pl.pallas_call(
        return_kernel,
        out_shape=jax.ShapeDtypeStruct((3, rows, width), BF16),
        in_specs=[smem, codes_spec, scales_spec] + [piece_spec] * 4,
        out_specs=codes_spec,
        compiler_params=params,
        name="restore",
    )(table, home, scales, *returned)
    grad_codes = jnp.transpose(grad_codes, (1, 0, 2))
    return (output[None, None], grad_codes[None, None], grad_w[None])


def solution(mesh):
    return jax.shard_map(
        local,
        mesh=mesh,
        in_specs=(
            P("dp", "fsdp", None, None, None),
            P("dp", "fsdp", None, None, None),
            P("dp", "fsdp", None),
            P("dp", "fsdp"),
            P(None, "fsdp", None, None),
            P("fsdp", None),
            P("dp", "fsdp", None, None),
        ),
        out_specs=(
            P("dp", "fsdp", None, None),
            P("dp", "fsdp", None, None, None),
            P("dp", "fsdp", None),
        ),
        check_vma=False,
    )
```

time: 236 us -> 147 us (0.62)
  the two profiles are of different devices: /device:TPU:494 before, /device:TPU:112 now
where the time goes in v1:
time: 147 us; the launch traced here: 145 us
  waiting for transfers between devices  72.3 us (49%)
  starting transfers between devices  29.5 us (20%)
  Pallas kernels  20.3 us (14%)
  between operations  14.8 us (10%)
  local copies, waits for them, and re-layouts  6.07 us (4%)
  other arithmetic  1.7 us (1%)
    reduce_scatter x1, waiting for transfers between devices, local(): lax.psum_scatter(term, 'fsdp', scatter_dimension=0, tiled=True).astype(F32)  35.7 us
    ppermute x8, starting transfers between devices, shifted(): return lax.ppermute(block, axis, route)  29.4 us
    all_gather x1, waiting for transfers between devices, local(): w_full = lax.all_gather(w_out, 'fsdp', axis=0, tiled=True)  25.8 us
    ppermute x8, waiting for transfers between devices, shifted(): return lax.ppermute(block, axis, route)  10.1 us
    pallas_call x1, Pallas kernels, local(): pl.pallas_call(functools.partial(backward_kernel, group), grid=(width //...  9.99 us
    pallas_call x1, Pallas kernels, local(): pl.pallas_call(functools.partial(forward_kernel, group), grid=(depth // c...  6.9 us
    unnamed x18, local copies, waits for them, and re-layouts  6.07 us
  transfers between devices with their start and end apart: 10, of which 6 were waited for; matrix products, arithmetic and copies ran while one was open for 0% of the time, Pallas kernels for 14%

profile of v1, /device:TPU:112, one launch (start us, length us, event | category | flops | bytes accessed | tf_op | source)
XLA Modules:
  0.0 144.6 jit_solution(7915001713948891198)
XLA Ops:
  7.2 0.0 copy-start.5
  7.2 0.0 copy-start.7
  7.2 0.0 all-gather.2.cloned.1.call-start
  7.2 0.7 all-gather.2.cloned.1.call-update
  7.9 0.0 reduce-scatter.2.cloned.1.call-start
  8.0 0.0 copy-start.1
  8.0 1.1 copy-done.1
  9.1 0.0 copy-start.4
  9.1 0.7 copy-done.4
  9.8 0.0 copy-start.6
  9.8 0.7 copy-done.6
  10.4 0.0 copy-start.3
  10.5 1.1 pack.1
  11.6 3.6 %collective-permute-start = (bf16[3,16,896]{2,1,0:T(8,128)(2,1)S(1)}, bf16[3,16,896]{2,1,0:T(8,128)(2,1)S(1)}, u32[]{:S(2)}, u32[]{:S(2)}) collective-permute-start(bf16[3,16,896]{2,1,0:T(8,128)(2,1)S(1)} %get-tuple-element.17), channel_id=1, source_target_pairs={{0,16},{16,32},{32,48},{48,64},{64,80},{80,96},{96,112},{112,128},... | collective-permute-start | bytes 258056 | tf_op jit(solution)/shard_map/ppermute | solution.py:24
  15.2 2.2 %collective-permute-start.1 = (bf16[3,16,896]{2,1,0:T(8,128)(2,1)S(1)}, bf16[3,16,896]{2,1,0:T(8,128)(2,1)S(1)}, u32[]{:S(2)}, u32[]{:S(2)}) collective-permute-start(bf16[3,16,896]{2,1,0:T(8,128)(2,1)S(1)} %get-tuple-element.18), channel_id=1, source_target_pairs={{16,0},{32,16},{48,32},{64,48},{80,64},{96,80},{112,96},{128,112},... | collective-permute-start | bytes 258056 | tf_op jit(solution)/shard_map/ppermute | solution.py:24
  17.4 4.7 %collective-permute-start.2 = (bf16[3,16,896]{2,1,0:T(8,128)(2,1)S(1)}, bf16[3,16,896]{2,1,0:T(8,128)(2,1)S(1)}, u32[]{:S(2)}, u32[]{:S(2)}) collective-permute-start(bf16[3,16,896]{2,1,0:T(8,128)(2,1)S(1)} %get-tuple-element.19), channel_id=1, source_target_pairs={{0,32},{16,48},{32,64},{48,80},{64,96},{80,112},{96,128},{112,144}... | collective-permute-start | bytes 258056 | tf_op jit(solution)/shard_map/ppermute | solution.py:24
  22.2 2.0 %collective-permute-start.3 = (bf16[3,16,896]{2,1,0:T(8,128)(2,1)S(1)}, bf16[3,16,896]{2,1,0:T(8,128)(2,1)S(1)}, u32[]{:S(2)}, u32[]{:S(2)}) collective-permute-start(bf16[3,16,896]{2,1,0:T(8,128)(2,1)S(1)} %get-tuple-element.20), channel_id=1, source_target_pairs={{32,0},{48,16},{64,32},{80,48},{96,64},{112,80},{128,96},{144,112}... | collective-permute-start | bytes 258056 | tf_op jit(solution)/shard_map/ppermute | solution.py:24
  24.8 0.0 collective-permute-done.r0
  24.9 0.0 collective-permute-done.1.r1
  24.9 0.3 collective-permute-done.2.r2
  25.2 7.3 %collective-permute-done.3.r3 = bf16[3,16,896]{2,1,0:T(8,128)(2,1)S(1)} collective-permute-done((bf16[3,16,896]{2,1,0:T(8,128)(2,1)S(1)}, bf16[3,16,896]{2,1,0:T(8,128)(2,1)S(1)}, u32[]{:S(2)}, u32[]{:S(2)}) %collective-permute-start.3) | collective-permute-done | bytes 86048 | tf_op jit(solution)/shard_map/ppermute | solution.py:24
  32.5 0.0 copy-start.2
  32.5 1.0 copy-done.2
  33.5 0.0 copy-start.8
  33.5 0.7 copy-done.8
  34.2 6.9 %forward.1 = (bf16[896,1792]{1,0:T(8,128)(2,1)}, bf16[128,896]{1,0:T(8,128)(2,1)S(1)}, bf16[3,128,896]{2,1,0:T(8,128)(2,1)S(1)}, f32[8,128,128]{2,1,0:T(8,128)S(1)}) custom-call(s32[3,4,64]{2,1,0:T(4,128)S(1)} %bitcast.23, s32[1,1]{1,0:T(1,128)S(6)} %copy.10.kept, s32[1,128]{1,0:T(1,128)S(1)} %bitcast.30, bf16[3,128,896]{2,1,0:T(8,128)(2,1)S(1)} %bitcast.19, ...), custom_call_target="tpu_custom_call" | custom-call | tf_op jit(solution)/shard_map/forward/pallas_call | solution.py:253
  41.1 0.0 reduce-scatter.2.cloned.1.call-update
  41.1 25.8 %all-gather.2.cloned.1.call-done.w = bf16[896,1792]{1,0:T(8,128)(2,1)} async-done(((bf16[56,1792]{1,0:T(8,128)(2,1)}), bf16[896,1792]{1,0:T(8,128)(2,1)}) %all-gather.2.cloned.1.call-update) | async-done | bytes 3211280 | tf_op jit(solution)/shard_map/all_gather | solution.py:240
  66.9 0.0 copy-done.5
  66.9 0.0 copy-done.7
  66.9 0.0 copy-done.3
  66.9 0.0 copy-start
  66.9 1.9 %copy-done = bf16[896,1792]{1,0:T(8,128)(2,1)S(1)} copy-done((bf16[896,1792]{1,0:T(8,128)(2,1)S(1)}, bf16[896,1792]{1,0:T(8,128)(2,1)}, u32[]{:S(2)}) %copy-start) | copy-done | bytes 3211288
  68.8 10.0 %backward.1 = (bf16[128,1792]{1,0:T(8,128)(2,1)}, bf16[3,128,896]{2,1,0:T(8,128)(2,1)S(1)}, bf16[3,16,896]{2,1,0:T(8,128)(2,1)S(1)}, bf16[3,16,896]{2,1,0:T(8,12...) custom-call(s32[3,4,64]{2,1,0:T(4,128)S(1)} %bitcast.24, s32[1,1]{1,0:T(1,128)S(6)} %copy.10.kept, ...), custom_call_target="tpu_custom_call" | custom-call | tf_op jit(solution)/shard_map/backward/pallas_call | solution.py:278
  78.8 3.3 %collective-permute-start.4 = (bf16[3,16,896]{2,1,0:T(8,128)(2,1)S(1)}, bf16[3,16,896]{2,1,0:T(8,128)(2,1)S(1)}, u32[]{:S(2)}, u32[]{:S(2)}) collective-permute-start(bf16[3,16,896]{2,1,0:T(8,128)(2,1)S(1)} %get-tuple-element.26), channel_id=1, source_target_pairs={{16,0},{32,16},{48,32},{64,48},{80,64},{96,80},{112,96},{128,112},... | collective-permute-start | bytes 258056 | tf_op jit(solution)/shard_map/ppermute | solution.py:24
  82.1 4.6 %collective-permute-start.5 = (bf16[3,16,896]{2,1,0:T(8,128)(2,1)S(1)}, bf16[3,16,896]{2,1,0:T(8,128)(2,1)S(1)}, u32[]{:S(2)}, u32[]{:S(2)}) collective-permute-start(bf16[3,16,896]{2,1,0:T(8,128)(2,1)S(1)} %get-tuple-element.27), channel_id=1, source_target_pairs={{0,16},{16,32},{32,48},{48,64},{64,80},{80,96},{96,112},{112,128},... | collective-permute-start | bytes 258056 | tf_op jit(solution)/shard_map/ppermute | solution.py:24
  86.8 2.1 %collective-permute-start.6 = (bf16[3,16,896]{2,1,0:T(8,128)(2,1)S(1)}, bf16[3,16,896]{2,1,0:T(8,128)(2,1)S(1)}, u32[]{:S(2)}, u32[]{:S(2)}) collective-permute-start(bf16[3,16,896]{2,1,0:T(8,128)(2,1)S(1)} %get-tuple-element.28), channel_id=1, source_target_pairs={{32,0},{48,16},{64,32},{80,48},{96,64},{112,80},{128,96},{144,112}... | collective-permute-start | bytes 258056 | tf_op jit(solution)/shard_map/ppermute | solution.py:24
  88.9 6.8 %collective-permute-start.7 = (bf16[3,16,896]{2,1,0:T(8,128)(2,1)S(1)}, bf16[3,16,896]{2,1,0:T(8,128)(2,1)S(1)}, u32[]{:S(2)}, u32[]{:S(2)}) collective-permute-start(bf16[3,16,896]{2,1,0:T(8,128)(2,1)S(1)} %get-tuple-element.29), channel_id=1, source_target_pairs={{0,32},{16,48},{32,64},{48,80},{64,96},{80,112},{96,128},{112,144}... | collective-permute-start | bytes 258056 | tf_op jit(solution)/shard_map/ppermute | solution.py:24
  95.7 0.0 collective-permute-done.4.r0
  95.7 0.0 collective-permute-done.5.r1
  95.7 0.9 collective-permute-done.6.r2
  96.5 1.6 %collective-permute-done.7.r3 = bf16[3,16,896]{2,1,0:T(8,128)(2,1)S(1)} collective-permute-done((bf16[3,16,896]{2,1,0:T(8,128)(2,1)S(1)}, bf16[3,16,896]{2,1,0:T(8,128)(2,1)S(1)}, u32[]{:S(2)}, u32[]{:S(2)}) %collective-permute-start.7) | collective-permute-done | bytes 86048 | tf_op jit(solution)/shard_map/ppermute | solution.py:24
  98.1 2.2 %restore.1 = bf16[3,128,896]{2,1,0:T(8,128)(2,1)} custom-call(s32[3,4,64]{2,1,0:T(4,128)S(1)} %bitcast.25, bf16[3,128,896]{2,1,0:T(8,128)(2,1)S(1)} %get-tuple-element.25.home, bf16[3,7,128]{2,1,0:T(8,128)(2,1)S(1)} %bitcast.29, bf16[3,16,896]{2,1,0:T(8,128)(2,1)S(1)} %collective-permute-done.4.r0, bf16[3,16,896]{2,1,0:T(8,128)(2,1)S(1)} %collective-permute-done.5.r1, ...), custom_call_target="tpu_custom_call" | custom-call | tf_op jit(solution)/shard_map/restore/pallas_call | solution.py:306
  100.4 35.7 %reduce-scatter.2.cloned.1.call-done = bf16[56,1792]{1,0:T(8,128)(2,1)} async-done(((bf16[896,1792]{1,0:T(8,128)(2,1)}), bf16[56,1792]{1,0:T(8,128)(2,1)}) %reduce-scatter.2.cloned.1.call-update) | async-done | bytes 200720 | tf_op jit(solution)/shard_map/reduce_scatter | solution.py:276
  136.0 1.7 %bitcast_convert_fusion = f32[1,56,1792]{2,1,0:T(8,128)} fusion(bf16[56,1792]{1,0:T(8,128)(2,1)} %reduce-scatter.2.cloned.1.call-done), kind=kLoop, calls=%fused_computation | loop fusion | flops 100352 | bytes 602112 | tf_op jit(solution)/shard_map/broadcast_in_dim | solution.py:315
Async XLA Ops:
  7.2 59.8 %copy-start.5 = (s32[64,1,4,3]{0,2,3,1:T(4,128)S(1)}, s32[64,1,4,3]{0,2,3,1:T(4,128)}, u32[]{:S(2)}) copy-start(s32[64,1,4,3]{0,2,3,1:T(4,128)} %param.11) | copy-start | bytes 9220
  7.2 59.8 %copy-start.7 = (bf16[1,1,128,3,7]{2,4,3,1,0:T(8,128)(2,1)S(1)}, bf16[1,1,128,3,7]{2,4,3,1,0:T(8,128)(2,1)}, u32[]{:S(2)}) copy-start(bf16[1,1,128,3,7]{2,4,3,1,0:T(8,128)(2,1)} %param.8) | copy-start | bytes 16132
  7.2 59.7 %all-gather.2.cloned.1.call-start = ((), (), s32[]{:S(2)}) async-start(), calls=%async_computation.1 | async-start | bytes 3411968 | tf_op jit(solution)/shard_map/all_gather | solution.py:240
  7.9 128.1 %reduce-scatter.2.cloned.1.call-start = ((), (), s32[]{:S(2)}) async-start(), calls=%async_computation.2 | async-start | bytes 3411968 | tf_op jit(solution)/shard_map/reduce_scatter | solution.py:276
  8.0 1.1 copy-start.1
  9.1 0.7 copy-start.4
  9.8 0.7 copy-start.6
  10.4 56.5 %copy-start.3 = (bf16[1,1,128,1792]{3,2,1,0:T(8,128)(2,1)S(1)}, bf16[1,1,128,1792]{3,2,1,0:T(8,128)(2,1)}, u32[]{:S(2)}) copy-start(bf16[1,1,128,1792]{3,2,1,0:T(8,128)(2,1)} %param.13) | copy-start | bytes 1376260
  11.6 13.3 %collective-permute-start = (bf16[3,16,896]{2,1,0:T(8,128)(2,1)S(1)}, bf16[3,16,896]{2,1,0:T(8,128)(2,1)S(1)}, u32[]{:S(2)}, u32[]{:S(2)}) collective-permute-start(bf16[3,16,896]{2,1,0:T(8,128)(2,1)S(1)} %get-tuple-element.17), channel_id=1, source_target_pairs={{0,16},{16,32},{32,48},{48,64},{64,80},{80,96},{96,112},{112,128},... | collective-permute-start | bytes 258056 | tf_op jit(solution)/shard_map/ppermute | solution.py:24
  15.2 9.7 %collective-permute-start.1 = (bf16[3,16,896]{2,1,0:T(8,128)(2,1)S(1)}, bf16[3,16,896]{2,1,0:T(8,128)(2,1)S(1)}, u32[]{:S(2)}, u32[]{:S(2)}) collective-permute-start(bf16[3,16,896]{2,1,0:T(8,128)(2,1)S(1)} %get-tuple-element.18), channel_id=1, source_target_pairs={{16,0},{32,16},{48,32},{64,48},{80,64},{96,80},{112,96},{128,112},... | collective-permute-start | bytes 258056 | tf_op jit(solution)/shard_map/ppermute | solution.py:24
  17.4 7.7 %collective-permute-start.2 = (bf16[3,16,896]{2,1,0:T(8,128)(2,1)S(1)}, bf16[3,16,896]{2,1,0:T(8,128)(2,1)S(1)}, u32[]{:S(2)}, u32[]{:S(2)}) collective-permute-start(bf16[3,16,896]{2,1,0:T(8,128)(2,1)S(1)} %get-tuple-element.19), channel_id=1, source_target_pairs={{0,32},{16,48},{32,64},{48,80},{64,96},{80,112},{96,128},{112,144}... | collective-permute-start | bytes 258056 | tf_op jit(solution)/shard_map/ppermute | solution.py:24
  22.2 10.3 %collective-permute-start.3 = (bf16[3,16,896]{2,1,0:T(8,128)(2,1)S(1)}, bf16[3,16,896]{2,1,0:T(8,128)(2,1)S(1)}, u32[]{:S(2)}, u32[]{:S(2)}) collective-permute-start(bf16[3,16,896]{2,1,0:T(8,128)(2,1)S(1)} %get-tuple-element.20), channel_id=1, source_target_pairs={{32,0},{48,16},{64,32},{80,48},{96,64},{112,80},{128,96},{144,112}... | collective-permute-start | bytes 258056 | tf_op jit(solution)/shard_map/ppermute | solution.py:24
  32.5 1.0 copy-start.2
  33.5 0.7 copy-start.8
  66.9 1.9 %copy-start = (bf16[896,1792]{1,0:T(8,128)(2,1)S(1)}, bf16[896,1792]{1,0:T(8,128)(2,1)}, u32[]{:S(2)}) copy-start(bf16[896,1792]{1,0:T(8,128)(2,1)} %all-gather.2.cloned.1.call-done.w) | copy-start | bytes 9633796
  78.8 16.8 %collective-permute-start.4 = (bf16[3,16,896]{2,1,0:T(8,128)(2,1)S(1)}, bf16[3,16,896]{2,1,0:T(8,128)(2,1)S(1)}, u32[]{:S(2)}, u32[]{:S(2)}) collective-permute-start(bf16[3,16,896]{2,1,0:T(8,128)(2,1)S(1)} %get-tuple-element.26), channel_id=1, source_target_pairs={{16,0},{32,16},{48,32},{64,48},{80,64},{96,80},{112,96},{128,112},... | collective-permute-start | bytes 258056 | tf_op jit(solution)/shard_map/ppermute | solution.py:24
  82.1 13.5 %collective-permute-start.5 = (bf16[3,16,896]{2,1,0:T(8,128)(2,1)S(1)}, bf16[3,16,896]{2,1,0:T(8,128)(2,1)S(1)}, u32[]{:S(2)}, u32[]{:S(2)}) collective-permute-start(bf16[3,16,896]{2,1,0:T(8,128)(2,1)S(1)} %get-tuple-element.27), channel_id=1, source_target_pairs={{0,16},{16,32},{32,48},{48,64},{64,80},{80,96},{96,112},{112,128},... | collective-permute-start | bytes 258056 | tf_op jit(solution)/shard_map/ppermute | solution.py:24
  86.8 9.7 %collective-permute-start.6 = (bf16[3,16,896]{2,1,0:T(8,128)(2,1)S(1)}, bf16[3,16,896]{2,1,0:T(8,128)(2,1)S(1)}, u32[]{:S(2)}, u32[]{:S(2)}) collective-permute-start(bf16[3,16,896]{2,1,0:T(8,128)(2,1)S(1)} %get-tuple-element.28), channel_id=1, source_target_pairs={{32,0},{48,16},{64,32},{80,48},{96,64},{112,80},{128,96},{144,112}... | collective-permute-start | bytes 258056 | tf_op jit(solution)/shard_map/ppermute | solution.py:24
  88.9 9.3 %collective-permute-start.7 = (bf16[3,16,896]{2,1,0:T(8,128)(2,1)S(1)}, bf16[3,16,896]{2,1,0:T(8,128)(2,1)S(1)}, u32[]{:S(2)}, u32[]{:S(2)}) collective-permute-start(bf16[3,16,896]{2,1,0:T(8,128)(2,1)S(1)} %get-tuple-element.29), channel_id=1, source_target_pairs={{0,32},{16,48},{32,64},{48,80},{64,96},{80,112},{96,128},{112,144}... | collective-permute-start | bytes 258056 | tf_op jit(solution)/shard_map/ppermute | solution.py:24
Sparse Core Ops, SparseCore 0:
  10.7 56.1 all-gather.1
  70.4 65.6 reduce-scatter.1

commit v2 on v1

--- a/solution.py
+++ b/solution.py
@@ -94,9 +94,22 @@
             sent[d][c] = values[d * SLOT : (d + 1) * SLOT]
 
 
+def split_order(width, half, core):
+    count = width // 2
+    part = width // HEADS // 2
+    slot = lax.broadcasted_iota(jnp.int32, (1, count), 1)
+    chip = jnp.zeros((1, count), jnp.int32)
+    for x in range(1, HEADS):
+        chip += jnp.where(slot >= x * part, 1, 0)
+    side = core if half == 0 else 1 - core
+    source = slot + part * chip + part * side
+    row = lax.broadcasted_iota(jnp.int32, (width, count), 0)
+    return jnp.where(row == source, 1.0, 0.0).astype(BF16)
+
+
 def forward_kernel(
     group, table, kept, segments, codes, scales, r0, r1, r2, r3, grad_out,
-    term, context_out, balanced, probs_out, turned
+    term_other, context_own, context_other, turned_own, orders, balanced, probs_out, turned
 ):
     rows, width = codes.shape[1:]
     size = width // HEADS
@@ -105,6 +118,7 @@
     @pl.when(pl.program_id(0) == 0)
     def _():
         at = lax.axis_index("dp")
+        core = lax.rem(lax.axis_index("fsdp"), 2)
         keep = kept[0, 0]
         spans = placed_spans(table, at, group)
         place = one_hot(spans, rows, False)
@@ -138,69 +152,73 @@
             probs = weights / jnp.sum(weights, axis=1, keepdims=True)
             probs_out[head] = probs
             add_tiles(tiles, dot(probs.astype(BF16), values), low)
-        context = jnp.concatenate(tiles, axis=1)
-        context_out[...] = context.astype(BF16)
-        turned[...] = context.T.astype(BF16)
-
-    term[...] = dot(turned[...], grad_out[...]).astype(BF16)
+        context = jnp.concatenate(tiles, axis=1).astype(BF16)
+        for half, (side, flipped) in enumerate(((context_own, turned_own), (context_other, turned))):
+            orders[half] = split_order(width, half, core)
+            picked = dot(context, orders[half])
+            side[...] = picked.astype(BF16)
+            flipped[...] = picked.T.astype(BF16)
+
+    term_other[...] = dot(turned[...], grad_out[...]).astype(BF16)
+
+
+def fold_kernel(turned_own, grad_out, arrived, folded):
+    own = dot(turned_own[...], grad_out[...]).astype(BF16)
+    folded[...] = (own.astype(F32) + arrived[...].astype(F32)).astype(BF16)
+
+
+def upstream_kernel(grad_out, w, grad_context):
+    grad_context[...] = dot(grad_out[...], w[...], NT).astype(BF16)
+
+
+def output_kernel(context_own, context_other, w_own, w_other, output):
+    total = dot(context_own[...], w_own[...]) + dot(context_other[...], w_other[...])
+    output[...] = total.astype(BF16)
 
 
 def backward_kernel(
-    group, table, kept, w, grad_out, context, balanced, probs_in, scales,
-    output, home, b0, b1, b2, b3, total_out, grad_context
+    group, table, kept, w_other, grad_out, upstream_own, orders, balanced, probs_in, scales,
+    home, b0, b1, b2, b3, upstream_all
 ):
-    step = pl.program_id(0)
     rows, width = balanced.shape[1:]
     size = width // HEADS
     factor = 1.0 / math.sqrt(size)
-    part = dot(context[...], w[...])
-
-    @pl.when(step == 0)
-    def _():
-        total_out[...] = part
-
-    @pl.when(step > 0)
-    def _():
-        total_out[...] += part
-
-    grad_context[step] = dot(grad_out[...], w[...], NT).astype(BF16)
-
-    @pl.when(step == pl.num_programs(0) - 1)
-    def _():
-        output[...] = total_out[...].astype(BF16)
-        at = lax.axis_index("dp")
-        keep = kept[0, 0]
-        count = width // LANES
-        grads = [[None] * count for _ in range(3)]
-        for head in range(HEADS):
-            low, high = window(head, size)
-            cut = slice(low * LANES, high * LANES)
-            mask = head_mask(head, size, rows)
-
-            def masked(values):
-                return jnp.where(mask, values.astype(F32), 0.0).astype(BF16)
-
-            query = masked(balanced[0, :, cut])
-            keys = masked(balanced[1, :, cut])
-            values = balanced[2, :, cut]
-            upstream = masked(jnp.concatenate([grad_context[i] for i in range(low, high)], axis=1))
-            probs = probs_in[head]
-            grad_probs = dot(upstream, values, NT)
-            total = jnp.sum(probs * grad_probs, axis=1, keepdims=True)
-            grad_scores = probs * (grad_probs - total) * factor
-            add_tiles(grads[0], dot(grad_scores.astype(BF16), keys), low)
-            add_tiles(grads[1], dot(grad_scores.T.astype(BF16), query), low)
-            add_tiles(grads[2], dot(probs.T.astype(BF16), upstream), low)
-        select = one_hot(placed_spans(table, at, group), rows, True)
-        row = lax.broadcasted_iota(jnp.int32, (rows, rows), 0)
-        lane = lax.broadcasted_iota(jnp.int32, (rows, rows), 1)
-        identity = jnp.where((row == lane) & (row < keep), 1.0, 0.0).astype(BF16)
-        for c in range(3):
-            grad = jnp.concatenate(grads[c], axis=1)
-            home[c] = (grad * expanded(identity, scales[c])).astype(BF16)
-            back = dot(select, grad.astype(BF16)).astype(BF16)
-            for d, ref in enumerate((b0, b1, b2, b3)):
-                ref[c] = back[d * SLOT : (d + 1) * SLOT]
+    upstream_other = dot(grad_out[...], w_other[...], NT).astype(BF16)
+    upstream_all[...] = (
+        dot(upstream_own[...], orders[0], NT) + dot(upstream_other, orders[1], NT)
+    ).astype(BF16)
+    at = lax.axis_index("dp")
+    keep = kept[0, 0]
+    grads = [[None] * (width // LANES) for _ in range(3)]
+    for head in range(HEADS):
+        low, high = window(head, size)
+        cut = slice(low * LANES, high * LANES)
+        mask = head_mask(head, size, rows)
+
+        def masked(values):
+            return jnp.where(mask, values.astype(F32), 0.0).astype(BF16)
+
+        query = masked(balanced[0, :, cut])
+        keys = masked(balanced[1, :, cut])
+        values = balanced[2, :, cut]
+        upstream = masked(upstream_all[:, cut])
+        probs = probs_in[head]
+        grad_probs = dot(upstream, values, NT)
+        total = jnp.sum(probs * grad_probs, axis=1, keepdims=True)
+        grad_scores = probs * (grad_probs - total) * factor
+        add_tiles(grads[0], dot(grad_scores.astype(BF16), keys), low)
+        add_tiles(grads[1], dot(grad_scores.T.astype(BF16), query), low)
+        add_tiles(grads[2], dot(probs.T.astype(BF16), upstream), low)
+    select = one_hot(placed_spans(table, at, group), rows, True)
+    row = lax.broadcasted_iota(jnp.int32, (rows, rows), 0)
+    lane = lax.broadcasted_iota(jnp.int32, (rows, rows), 1)
+    identity = jnp.where((row == lane) & (row < keep), 1.0, 0.0).astype(BF16)
+    for c in range(3):
+        grad = jnp.concatenate(grads[c], axis=1)
+        home[c] = (grad * expanded(identity, scales[c])).astype(BF16)
+        back = dot(select, grad.astype(BF16)).astype(BF16)
+        for d, ref in enumerate((b0, b1, b2, b3)):
+            ref[c] = back[d * SLOT : (d + 1) * SLOT]
 
 
 def return_kernel(table, home, scales, r0, r1, r2, r3, grad_codes):
@@ -230,14 +248,19 @@
     _, rows, width = codes.shape
     depth = w_out.shape[1]
     blocks = scales.shape[1]
+    devices = lax.axis_size("fsdp")
+    half = width // 2
+    cores = [list(range(core, devices, 2)) for core in range(2)]
+    swap = [(i, i + 1 - 2 * (i % 2)) for i in range(devices)]
     smem = pl.BlockSpec(memory_space=pltpu.SMEM)
-    params = pltpu.CompilerParams(vmem_limit_bytes=24 * 1024 * 1024)
+    params = pltpu.CompilerParams(vmem_limit_bytes=48 * 1024 * 1024)
+    small = pl.CostEstimate(flops=1, bytes_accessed=1, transcendentals=0)
     piece = jax.ShapeDtypeStruct((3, SLOT, width), BF16)
     piece_spec = whole((3, SLOT, width))
     codes_spec = whole((3, rows, width))
     scales_spec = whole((3, blocks, rows))
 
-    w_full = lax.all_gather(w_out, "fsdp", axis=0, tiled=True)
+    w_own = lax.all_gather(w_out, "fsdp", axis=0, tiled=True, axis_index_groups=cores)
 
     sent = pl.pallas_call(
         pack_kernel,
@@ -245,62 +268,96 @@
         in_specs=[smem, codes_spec, scales_spec],
         out_specs=[piece_spec] * 4,
         compiler_params=params,
+        cost_estimate=small,
         name="pack",
     )(table, codes, scales)
     received = [shifted(sent[d], "dp", OFFSETS[d]) for d in range(4)]
 
     chunk = 256
-    term, context, balanced, probs = pl.pallas_call(
+    half_context = jax.ShapeDtypeStruct((rows, half), BF16)
+    half_term = jax.ShapeDtypeStruct((half, depth), BF16)
+    term_spec = pl.BlockSpec((half, chunk), lambda n: (0, n))
+    grad_spec = pl.BlockSpec((rows, chunk), lambda n: (0, n))
+    term_other, context_own, context_other, turned_own, orders, balanced, probs = pl.pallas_call(
         functools.partial(forward_kernel, group),
         grid=(depth // chunk,),
         out_shape=[
-            jax.ShapeDtypeStruct((width, depth), BF16),
-            jax.ShapeDtypeStruct((rows, width), BF16),
+            half_term,
+            half_context,
+            half_context,
+            jax.ShapeDtypeStruct((half, rows), BF16),
+            jax.ShapeDtypeStruct((2, width, half), BF16),
             jax.ShapeDtypeStruct((3, rows, width), BF16),
             jax.ShapeDtypeStruct((HEADS, rows, rows), F32),
         ],
         in_specs=[smem, smem, whole((1, rows)), codes_spec, scales_spec]
         + [piece_spec] * 4
-        + [pl.BlockSpec((rows, chunk), lambda n: (0, n))],
+        + [grad_spec],
         out_specs=[
-            pl.BlockSpec((width, chunk), lambda n: (0, n)),
-            whole((rows, width)),
+            term_spec,
+            whole((rows, half)),
+            whole((rows, half)),
+            whole((half, rows)),
+            whole((2, width, half)),
             codes_spec,
             whole((HEADS, rows, rows)),
         ],
-        scratch_shapes=[pltpu.VMEM((width, rows), BF16)],
-        compiler_params=params,
+        scratch_shapes=[pltpu.VMEM((half, rows), BF16)],
+        compiler_params=params,
+        cost_estimate=small,
         name="forward",
     )(table, kept_rows, segments, codes, scales, *received, grad_out)
-
-    grad_w = lax.psum_scatter(term, "fsdp", scatter_dimension=0, tiled=True).astype(F32)
-
-    output, home, *back = pl.pallas_call(
+    w_own, term_other = lax.optimization_barrier((w_own, term_other))
+    arrived = lax.ppermute(term_other, "fsdp", swap)
+    w_other = lax.ppermute(w_own, "fsdp", swap)
+    folded = pl.pallas_call(
+        fold_kernel,
+        grid=(depth // chunk,),
+        out_shape=half_term,
+        in_specs=[whole((half, rows)), grad_spec, term_spec],
+        out_specs=term_spec,
+        compiler_params=params,
+        name="fold",
+    )(turned_own, grad_out, arrived)
+    grad_w = lax.psum_scatter(
+        folded, "fsdp", scatter_dimension=0, tiled=True, axis_index_groups=cores
+    ).astype(F32)
+
+    upstream_own = pl.pallas_call(
+        upstream_kernel,
+        out_shape=half_context,
+        compiler_params=params,
+        name="upstream",
+    )(grad_out, w_own)
+    home, *back = pl.pallas_call(
         functools.partial(backward_kernel, group),
-        grid=(width // LANES,),
-        out_shape=[
-            jax.ShapeDtypeStruct((rows, depth), BF16),
-            jax.ShapeDtypeStruct((3, rows, width), BF16),
-        ]
-        + [piece] * 4,
+        out_shape=[jax.ShapeDtypeStruct((3, rows, width), BF16)] + [piece] * 4,
         in_specs=[
             smem,
             smem,
-            pl.BlockSpec((LANES, depth), lambda n: (n, 0)),
+            whole((half, depth)),
             whole((rows, depth)),
-            pl.BlockSpec((rows, LANES), lambda n: (0, n)),
+            whole((rows, half)),
+            whole((2, width, half)),
             codes_spec,
             whole((HEADS, rows, rows)),
             scales_spec,
         ],
-        out_specs=[whole((rows, depth)), codes_spec] + [piece_spec] * 4,
-        scratch_shapes=[
-            pltpu.VMEM((rows, depth), F32),
-            pltpu.VMEM((width // LANES, rows, LANES), BF16),
-        ],
+        out_specs=[codes_spec] + [piece_spec] * 4,
+        scratch_shapes=[pltpu.VMEM((rows, width), BF16)],
         compiler_params=params,
         name="backward",
-    )(table, kept_rows, w_full, grad_out, context, balanced, probs, scales)
+    )(table, kept_rows, w_other, grad_out, upstream_own, orders, balanced, probs, scales)
+    weight_spec = pl.BlockSpec((half, chunk), lambda n: (0, n))
+    output = pl.pallas_call(
+        output_kernel,
+        grid=(depth // chunk,),
+        out_shape=jax.ShapeDtypeStruct((rows, depth), BF16),
+        in_specs=[whole((rows, half))] * 2 + [weight_spec] * 2,
+        out_specs=grad_spec,
+        compiler_params=params,
+        name="project",
+    )(context_own, context_other, w_own, w_other)
     returned = [shifted(back[d], "dp", -OFFSETS[d]) for d in range(4)]
 
     grad_codes = pl.pallas_call(

time: 147 us -> 130 us (0.88)
  waiting for transfers between devices: 72.3 us -> 46.6 us
  local copies, waits for them, and re-layouts: 6.07 us -> 10.4 us
  starting transfers between devices: 29.5 us -> 33.4 us
    reduce_scatter x1, waiting for transfers between devices: 35.7 us -> 9.93 us  [local(): lax.psum_scatter(folded, 'fsdp', scatter_dimension=0, tiled=True, axis_in...]
    ppermute x0 -> x2, waiting for transfers between devices: none -> 6.34 us  [the longest x1 3.63 us: local(): arrived = lax.ppermute(term_other, 'fsdp', swap)]
    unnamed x18 -> x28, local copies, waits for them, and re-layouts: 6.07 us -> 10.4 us
    ppermute x0 -> x2, starting transfers between devices: none -> 3.93 us  [the longest x1 2.02 us: local(): w_other = lax.ppermute(w_own, 'fsdp', swap)]
    all_gather x1, waiting for transfers between devices: 25.8 us -> 21.9 us  [local(): lax.all_gather(w_out, 'fsdp', axis=0, tiled=True, axis_index_groups=cores)]
    ppermute x8, waiting for transfers between devices: 10.1 us -> 7.65 us  [shifted(): return lax.ppermute(block, axis, route)]
    pallas_call x1 -> x4, Pallas kernels: 9.99 us -> 11.7 us  [the longest x1 5.67 us: local(): pl.pallas_call(functools.partial(backward_kernel, group), out_shape=[jax....]
  transfers between devices with their start and end apart: 10 -> 12, of which waited for: 6 -> 6; matrix products, arithmetic and copies ran while one was open for 0% -> 0% of each run, Pallas kernels for 14% -> 15%
where the time goes in v2:
time: 130 us; the launch traced here: 128 us
  waiting for transfers between devices  46.6 us (36%)
  starting transfers between devices  33.4 us (26%)
  Pallas kernels  21.1 us (16%)
  between operations  14.8 us (11%)
  local copies, waits for them, and re-layouts  10.4 us (8%)
  other arithmetic  1.7 us (1%)
    ppermute x8, starting transfers between devices, shifted(): return lax.ppermute(block, axis, route)  29.4 us
    all_gather x1, waiting for transfers between devices, local(): lax.all_gather(w_out, 'fsdp', axis=0, tiled=True, axis_index_groups=cores)  21.9 us
    unnamed x28, local copies, waits for them, and re-layouts  10.4 us
    reduce_scatter x1, waiting for transfers between devices, local(): lax.psum_scatter(folded, 'fsdp', scatter_dimension=0, tiled=True, axis_in...  9.93 us
    ppermute x8, waiting for transfers between devices, shifted(): return lax.ppermute(block, axis, route)  7.65 us
    pallas_call x1, Pallas kernels, local(): pl.pallas_call(functools.partial(forward_kernel, group), grid=(depth // c...  6.1 us
    pallas_call x1, Pallas kernels, local(): pl.pallas_call(functools.partial(backward_kernel, group), out_shape=[jax....  5.67 us
    ppermute x1, waiting for transfers between devices, local(): arrived = lax.ppermute(term_other, 'fsdp', swap)  3.63 us
  transfers between devices with their start and end apart: 12, of which 6 were waited for; matrix products, arithmetic and copies ran while one was open for 0% of the time, Pallas kernels for 15%

profile of v2, /device:TPU:112, one launch (start us, length us, event | category | flops | bytes accessed | tf_op | source)
XLA Modules:
  0.0 128.0 jit_solution(10383237536698495593)
XLA Ops:
  7.2 0.0 copy-start.1
  7.2 0.0 all-gather.2.cloned.1.call-start
  7.2 0.7 all-gather.2.cloned.1.call-update
  7.9 0.0 reduce-scatter.2.cloned.1.call-start
  8.0 0.0 copy-start.4
  8.0 1.1 copy-done.4
  9.1 0.0 copy-start.6
  9.1 0.7 copy-done.6
  9.8 0.0 copy-start.9
  9.8 0.7 copy-done.9
  10.4 1.1 pack.1
  11.6 3.6 %collective-permute-start = (bf16[3,16,896]{2,1,0:T(8,128)(2,1)S(1)}, bf16[3,16,896]{2,1,0:T(8,128)(2,1)S(1)}, u32[]{:S(2)}, u32[]{:S(2)}) collective-permute-start(bf16[3,16,896]{2,1,0:T(8,128)(2,1)S(1)} %get-tuple-element.21), channel_id=1, source_target_pairs={{0,16},{16,32},{32,48},{48,64},{64,80},{80,96},{96,112},{112,128},... | collective-permute-start | bytes 258056 | tf_op jit(solution)/shard_map/ppermute | solution.py:24
  15.2 2.2 %collective-permute-start.1 = (bf16[3,16,896]{2,1,0:T(8,128)(2,1)S(1)}, bf16[3,16,896]{2,1,0:T(8,128)(2,1)S(1)}, u32[]{:S(2)}, u32[]{:S(2)}) collective-permute-start(bf16[3,16,896]{2,1,0:T(8,128)(2,1)S(1)} %get-tuple-element.22), channel_id=1, source_target_pairs={{16,0},{32,16},{48,32},{64,48},{80,64},{96,80},{112,96},{128,112},... | collective-permute-start | bytes 258056 | tf_op jit(solution)/shard_map/ppermute | solution.py:24
  17.4 4.7 %collective-permute-start.2 = (bf16[3,16,896]{2,1,0:T(8,128)(2,1)S(1)}, bf16[3,16,896]{2,1,0:T(8,128)(2,1)S(1)}, u32[]{:S(2)}, u32[]{:S(2)}) collective-permute-start(bf16[3,16,896]{2,1,0:T(8,128)(2,1)S(1)} %get-tuple-element.23), channel_id=1, source_target_pairs={{0,32},{16,48},{32,64},{48,80},{64,96},{80,112},{96,128},{112,144}... | collective-permute-start | bytes 258056 | tf_op jit(solution)/shard_map/ppermute | solution.py:24
  22.2 2.0 %collective-permute-start.3 = (bf16[3,16,896]{2,1,0:T(8,128)(2,1)S(1)}, bf16[3,16,896]{2,1,0:T(8,128)(2,1)S(1)}, u32[]{:S(2)}, u32[]{:S(2)}) collective-permute-start(bf16[3,16,896]{2,1,0:T(8,128)(2,1)S(1)} %get-tuple-element.24), channel_id=1, source_target_pairs={{32,0},{48,16},{64,32},{80,48},{96,64},{112,80},{128,96},{144,112}... | collective-permute-start | bytes 258056 | tf_op jit(solution)/shard_map/ppermute | solution.py:24
  24.8 0.0 collective-permute-done.r0
  24.8 0.0 collective-permute-done.1.r1
  24.9 0.3 collective-permute-done.2.r2
  25.2 7.3 %collective-permute-done.3.r3 = bf16[3,16,896]{2,1,0:T(8,128)(2,1)S(1)} collective-permute-done((bf16[3,16,896]{2,1,0:T(8,128)(2,1)S(1)}, bf16[3,16,896]{2,1,0:T(8,128)(2,1)S(1)}, u32[]{:S(2)}, u32[]{:S(2)}) %collective-permute-start.3) | collective-permute-done | bytes 86048 | tf_op jit(solution)/shard_map/ppermute | solution.py:24
  32.5 0.0 copy-start
  32.5 1.0 copy-done
  33.5 0.0 copy-start.5
  33.5 1.1 copy-done.5
  34.6 0.0 copy-start.7
  34.6 0.7 copy-done.7
  35.3 0.0 copy-start.10
  35.3 0.7 copy-done.10
  36.0 0.0 copy-start.12
  36.0 0.7 copy-done.12
  36.7 6.1 %forward.1 = (bf16[448,1792]{1,0:T(8,128)(2,1)S(1)}, bf16[128,448]{1,0:T(8,128)(2,1)S(1)}, bf16[128,448]{1,0:T(8,128)(2,1)S(1)}, bf16[448,128]{1,0:T(8,128)(2,1)...) custom-call(s32[3,4,64]{2,1,0:T(4,128)S(1)} %bitcast.25, ...), custom_call_target="tpu_custom_call" | custom-call | flops 1 | bytes 1 | tf_op jit(solution)/shard_map/forward/pallas_call | solution.py:281
  42.8 0.0 copy-start.13
  42.8 1.2 copy-done.13
  43.9 21.9 %all-gather.2.cloned.1.call-done.w_own.w = bf16[448,1792]{1,0:T(8,128)(2,1)} async-done(((bf16[56,1792]{1,0:T(8,128)(2,1)}), bf16[448,1792]{1,0:T(8,128)(2,1)}) %all-gather.2.cloned.1.call-update) | async-done | bytes 1605648 | tf_op jit(solution)/shard_map/all_gather | solution.py:263
  65.9 1.9 %collective-permute-start.9 = (bf16[448,1792]{1,0:T(8,128)(2,1)}, bf16[448,1792]{1,0:T(8,128)(2,1)S(1)}, u32[]{:S(2)}, u32[]{:S(2)}) collective-permute-start(bf16[448,1792]{1,0:T(8,128)(2,1)} %copy-done.13), channel_id=1, source_target_pairs={{0,1},{1,0},{2,3},{3,2},{4,5},{5,4},{6,7},{7,6},{8,9},{9,8},{10,11... | collective-permute-start | bytes 4816904 | tf_op jit(solution)/shard_map/ppermute | solution.py:311
  67.8 3.6 %collective-permute-done.9.arrived = bf16[448,1792]{1,0:T(8,128)(2,1)S(1)} collective-permute-done((bf16[448,1792]{1,0:T(8,128)(2,1)}, bf16[448,1792]{1,0:T(8,128)(2,1)S(1)}, u32[]{:S(2)}, u32[]{:S(2)}) %collective-permute-start.9) | collective-permute-done | bytes 1605664 | tf_op jit(solution)/shard_map/ppermute | solution.py:311
  71.4 0.0 copy-done.1
  71.4 1.8 %fold.1 = bf16[448,1792]{1,0:T(8,128)(2,1)S(1)} custom-call(bf16[448,128]{1,0:T(8,128)(2,1)S(1)} %get-tuple-element.37.turned_own, bf16[128,1792]{1,0:T(8,128)(2,1)S(1)} %bitcast.19, bf16[448,1792]{1,0:T(8,128)(2,1)S(1)} %collective-permute-done.9.arrived), custom_call_target="tpu_custom_call" | custom-call | tf_op jit(solution)/shard_map/fold/pallas_call | solution.py:313
  73.2 0.0 copy-start.3
  73.2 1.2 copy-done.3
  74.4 0.0 copy-start.2
  74.4 0.0 copy-start.8
  74.4 0.0 copy-start.11
  74.4 0.0 reduce-scatter.2.cloned.1.call-update
  74.4 1.4 %copy-done.2 = bf16[448,1792]{1,0:T(8,128)(2,1)S(1)} copy-done((bf16[448,1792]{1,0:T(8,128)(2,1)S(1)}, bf16[448,1792]{1,0:T(8,128)(2,1)}, u32[]{:S(2)}) %copy-start.2) | copy-done | bytes 1605656
  75.8 2.0 %collective-permute-start.4 = (bf16[448,1792]{1,0:T(8,128)(2,1)S(1)}, bf16[448,1792]{1,0:T(8,128)(2,1)S(1)}, u32[]{:S(2)}, u32[]{:S(2)}) collective-permute-start(bf16[448,1792]{1,0:T(8,128)(2,1)S(1)} %copy-done.2), channel_id=1, source_target_pairs={{0,1},{1,0},{2,3},{3,2},{4,5},{5,4},{6,7},{7,6},{8,9},{9,8},{10,11... | collective-permute-start | bytes 4816904 | tf_op jit(solution)/shard_map/ppermute | solution.py:312
  77.8 0.6 upstream.1.upstream_own
  78.4 2.7 %collective-permute-done.4.w_other = bf16[448,1792]{1,0:T(8,128)(2,1)S(1)} collective-permute-done((bf16[448,1792]{1,0:T(8,128)(2,1)S(1)}, bf16[448,1792]{1,0:T(8,128)(2,1)S(1)}, u32[]{:S(2)}, u32[]{:S(2)}) %collective-permute-start.4) | collective-permute-done | bytes 1605664 | tf_op jit(solution)/shard_map/ppermute | solution.py:312
  81.1 0.0 copy-done.8
  81.1 0.0 copy-done.11
  81.1 5.7 %backward.1 = (bf16[3,128,896]{2,1,0:T(8,128)(2,1)S(1)}, bf16[3,16,896]{2,1,0:T(8,128)(2,1)S(1)}, bf16[3,16,896]{2,1,0:T(8,128)(2,1)S(1)}, bf16[3,16,896]{2,1,0:T(8,128)(2,1)S(1)}, bf16[3,16,896]{2,1,0:T(8,128)(2,1)S(1)}) custom-call(s32[3,4,64]{2,1,0:T(4,128)S(1)} %bitcast.26, s32[1,1]{1,0:T(1,128)S(6)} %copy.10.kept, ...), custom_call_target="tpu_custom_call" | custom-call | tf_op jit(solution)/shard_map/backward/pallas_call | solution.py:332
  86.8 3.3 %collective-permute-start.5 = (bf16[3,16,896]{2,1,0:T(8,128)(2,1)S(1)}, bf16[3,16,896]{2,1,0:T(8,128)(2,1)S(1)}, u32[]{:S(2)}, u32[]{:S(2)}) collective-permute-start(bf16[3,16,896]{2,1,0:T(8,128)(2,1)S(1)} %get-tuple-element.33), channel_id=1, source_target_pairs={{16,0},{32,16},{48,32},{64,48},{80,64},{96,80},{112,96},{128,112},... | collective-permute-start | bytes 258056 | tf_op jit(solution)/shard_map/ppermute | solution.py:24
  90.1 4.6 %collective-permute-start.6 = (bf16[3,16,896]{2,1,0:T(8,128)(2,1)S(1)}, bf16[3,16,896]{2,1,0:T(8,128)(2,1)S(1)}, u32[]{:S(2)}, u32[]{:S(2)}) collective-permute-start(bf16[3,16,896]{2,1,0:T(8,128)(2,1)S(1)} %get-tuple-element.34), channel_id=1, source_target_pairs={{0,16},{16,32},{32,48},{48,64},{64,80},{80,96},{96,112},{112,128},... | collective-permute-start | bytes 258056 | tf_op jit(solution)/shard_map/ppermute | solution.py:24
  94.8 2.0 %collective-permute-start.7 = (bf16[3,16,896]{2,1,0:T(8,128)(2,1)S(1)}, bf16[3,16,896]{2,1,0:T(8,128)(2,1)S(1)}, u32[]{:S(2)}, u32[]{:S(2)}) collective-permute-start(bf16[3,16,896]{2,1,0:T(8,128)(2,1)S(1)} %get-tuple-element.35), channel_id=1, source_target_pairs={{32,0},{48,16},{64,32},{80,48},{96,64},{112,80},{128,96},{144,112}... | collective-permute-start | bytes 258056 | tf_op jit(solution)/shard_map/ppermute | solution.py:24
  96.8 6.8 %collective-permute-start.8 = (bf16[3,16,896]{2,1,0:T(8,128)(2,1)S(1)}, bf16[3,16,896]{2,1,0:T(8,128)(2,1)S(1)}, u32[]{:S(2)}, u32[]{:S(2)}) collective-permute-start(bf16[3,16,896]{2,1,0:T(8,128)(2,1)S(1)} %get-tuple-element.36), channel_id=1, source_target_pairs={{0,32},{16,48},{32,64},{48,80},{64,96},{80,112},{96,128},{112,144}... | collective-permute-start | bytes 258056 | tf_op jit(solution)/shard_map/ppermute | solution.py:24
  103.7 3.6 %project.1 = bf16[128,1792]{1,0:T(8,128)(2,1)} custom-call(bf16[128,448]{1,0:T(8,128)(2,1)S(1)} %get-tuple-element.25.context_own, bf16[128,448]{1,0:T(8,128)(2,1)S(1)} %get-tuple-element.26.context_other, bf16[448,1792]{1,0:T(8,128)(2,1)S(1)} %copy-done.2, bf16[448,1792]{1,0:T(8,128)(2,1)S(1)} %collective-permute-done.4.w_other), custom_call_target="tpu_custom_call" | custom-call | tf_op jit(solution)/shard_map/project/pallas_call | solution.py:352
  107.3 0.0 collective-permute-done.5.r0
  107.3 0.0 collective-permute-done.6.r1
  107.3 0.0 collective-permute-done.7.r2
  107.3 0.0 collective-permute-done.8.r3
  107.3 2.2 %restore.1 = bf16[3,128,896]{2,1,0:T(8,128)(2,1)} custom-call(s32[3,4,64]{2,1,0:T(4,128)S(1)} %bitcast.27, bf16[3,128,896]{2,1,0:T(8,128)(2,1)S(1)} %get-tuple-element.32.home, bf16[3,7,128]{2,1,0:T(8,128)(2,1)S(1)} %bitcast.31, bf16[3,16,896]{2,1,0:T(8,128)(2,1)S(1)} %collective-permute-done.5.r0, bf16[3,16,896]{2,1,0:T(8,128)(2,1)S(1)} %collective-permute-done.6.r1, ...), custom_call_target="tpu_custom_call" | custom-call | tf_op jit(solution)/shard_map/restore/pallas_call | solution.py:363
  109.5 9.9 %reduce-scatter.2.cloned.1.call-done = bf16[56,1792]{1,0:T(8,128)(2,1)} async-done(((bf16[448,1792]{1,0:T(8,128)(2,1)}), bf16[56,1792]{1,0:T(8,128)(2,1)}) %reduce-scatter.2.cloned.1.call-update) | async-done | bytes 200720 | tf_op jit(solution)/shard_map/reduce_scatter | solution.py:322
  119.5 1.7 %bitcast_convert_fusion = f32[1,56,1792]{2,1,0:T(8,128)} fusion(bf16[56,1792]{1,0:T(8,128)(2,1)} %reduce-scatter.2.cloned.1.call-done), kind=kLoop, calls=%fused_computation | loop fusion | flops 100352 | bytes 602112 | tf_op jit(solution)/shard_map/broadcast_in_dim | solution.py:372
Async XLA Ops:
  7.2 64.3 %copy-start.1 = (bf16[1,1,128,1792]{3,2,1,0:T(8,128)(2,1)S(1)}, bf16[1,1,128,1792]{3,2,1,0:T(8,128)(2,1)}, u32[]{:S(2)}) copy-start(bf16[1,1,128,1792]{3,2,1,0:T(8,128)(2,1)} %param.13) | copy-start | bytes 1376260
  7.2 58.7 %all-gather.2.cloned.1.call-start = ((), (), s32[]{:S(2)}) async-start(), calls=%async_computation.1 | async-start | bytes 1806336 | tf_op jit(solution)/shard_map/all_gather | solution.py:263
  7.9 111.6 %reduce-scatter.2.cloned.1.call-start = ((), (), s32[]{:S(2)}) async-start(), calls=%async_computation.2 | async-start | bytes 1806336 | tf_op jit(solution)/shard_map/reduce_scatter | solution.py:322
  8.0 1.1 copy-start.4
  9.1 0.7 copy-start.6
  9.8 0.7 copy-start.9
  11.6 13.3 %collective-permute-start = (bf16[3,16,896]{2,1,0:T(8,128)(2,1)S(1)}, bf16[3,16,896]{2,1,0:T(8,128)(2,1)S(1)}, u32[]{:S(2)}, u32[]{:S(2)}) collective-permute-start(bf16[3,16,896]{2,1,0:T(8,128)(2,1)S(1)} %get-tuple-element.21), channel_id=1, source_target_pairs={{0,16},{16,32},{32,48},{48,64},{64,80},{80,96},{96,112},{112,128},... | collective-permute-start | bytes 258056 | tf_op jit(solution)/shard_map/ppermute | solution.py:24
  15.2 9.7 %collective-permute-start.1 = (bf16[3,16,896]{2,1,0:T(8,128)(2,1)S(1)}, bf16[3,16,896]{2,1,0:T(8,128)(2,1)S(1)}, u32[]{:S(2)}, u32[]{:S(2)}) collective-permute-start(bf16[3,16,896]{2,1,0:T(8,128)(2,1)S(1)} %get-tuple-element.22), channel_id=1, source_target_pairs={{16,0},{32,16},{48,32},{64,48},{80,64},{96,80},{112,96},{128,112},... | collective-permute-start | bytes 258056 | tf_op jit(solution)/shard_map/ppermute | solution.py:24
  17.4 7.7 %collective-permute-start.2 = (bf16[3,16,896]{2,1,0:T(8,128)(2,1)S(1)}, bf16[3,16,896]{2,1,0:T(8,128)(2,1)S(1)}, u32[]{:S(2)}, u32[]{:S(2)}) collective-permute-start(bf16[3,16,896]{2,1,0:T(8,128)(2,1)S(1)} %get-tuple-element.23), channel_id=1, source_target_pairs={{0,32},{16,48},{32,64},{48,80},{64,96},{80,112},{96,128},{112,144}... | collective-permute-start | bytes 258056 | tf_op jit(solution)/shard_map/ppermute | solution.py:24
  22.2 10.3 %collective-permute-start.3 = (bf16[3,16,896]{2,1,0:T(8,128)(2,1)S(1)}, bf16[3,16,896]{2,1,0:T(8,128)(2,1)S(1)}, u32[]{:S(2)}, u32[]{:S(2)}) collective-permute-start(bf16[3,16,896]{2,1,0:T(8,128)(2,1)S(1)} %get-tuple-element.24), channel_id=1, source_target_pairs={{32,0},{48,16},{64,32},{80,48},{96,64},{112,80},{128,96},{144,112}... | collective-permute-start | bytes 258056 | tf_op jit(solution)/shard_map/ppermute | solution.py:24
  32.5 1.0 copy-start
  33.5 1.1 copy-start.5
  34.6 0.7 copy-start.7
  35.3 0.7 copy-start.10
  36.0 0.7 copy-start.12
  42.8 1.2 copy-start.13
  65.9 5.5 %collective-permute-start.9 = (bf16[448,1792]{1,0:T(8,128)(2,1)}, bf16[448,1792]{1,0:T(8,128)(2,1)S(1)}, u32[]{:S(2)}, u32[]{:S(2)}) collective-permute-start(bf16[448,1792]{1,0:T(8,128)(2,1)} %copy-done.13), channel_id=1, source_target_pairs={{0,1},{1,0},{2,3},{3,2},{4,5},{5,4},{6,7},{7,6},{8,9},{9,8},{10,11... | collective-permute-start | bytes 4816904 | tf_op jit(solution)/shard_map/ppermute | solution.py:311
  73.2 1.2 copy-start.3
  74.4 1.4 %copy-start.2 = (bf16[448,1792]{1,0:T(8,128)(2,1)S(1)}, bf16[448,1792]{1,0:T(8,128)(2,1)}, u32[]{:S(2)}) copy-start(bf16[448,1792]{1,0:T(8,128)(2,1)} %all-gather.2.cloned.1.call-done.w_own.w) | copy-start | bytes 4816900
  74.4 6.8 %copy-start.8 = (s32[64,1,4,3]{0,2,3,1:T(4,128)S(1)}, s32[64,1,4,3]{0,2,3,1:T(4,128)}, u32[]{:S(2)}) copy-start(s32[64,1,4,3]{0,2,3,1:T(4,128)} %param.11) | copy-start | bytes 9220
  74.4 6.8 %copy-start.11 = (bf16[1,1,128,3,7]{2,4,3,1,0:T(8,128)(2,1)S(1)}, bf16[1,1,128,3,7]{2,4,3,1,0:T(8,128)(2,1)}, u32[]{:S(2)}) copy-start(bf16[1,1,128,3,7]{2,4,3,1,0:T(8,128)(2,1)} %param.8) | copy-start | bytes 16132
  75.8 5.3 %collective-permute-start.4 = (bf16[448,1792]{1,0:T(8,128)(2,1)S(1)}, bf16[448,1792]{1,0:T(8,128)(2,1)S(1)}, u32[]{:S(2)}, u32[]{:S(2)}) collective-permute-start(bf16[448,1792]{1,0:T(8,128)(2,1)S(1)} %copy-done.2), channel_id=1, source_target_pairs={{0,1},{1,0},{2,3},{3,2},{4,5},{5,4},{6,7},{7,6},{8,9},{9,8},{10,11... | collective-permute-start | bytes 4816904 | tf_op jit(solution)/shard_map/ppermute | solution.py:312
  86.8 20.5 %collective-permute-start.5 = (bf16[3,16,896]{2,1,0:T(8,128)(2,1)S(1)}, bf16[3,16,896]{2,1,0:T(8,128)(2,1)S(1)}, u32[]{:S(2)}, u32[]{:S(2)}) collective-permute-start(bf16[3,16,896]{2,1,0:T(8,128)(2,1)S(1)} %get-tuple-element.33), channel_id=1, source_target_pairs={{16,0},{32,16},{48,32},{64,48},{80,64},{96,80},{112,96},{128,112},... | collective-permute-start | bytes 258056 | tf_op jit(solution)/shard_map/ppermute | solution.py:24
  90.1 17.1 %collective-permute-start.6 = (bf16[3,16,896]{2,1,0:T(8,128)(2,1)S(1)}, bf16[3,16,896]{2,1,0:T(8,128)(2,1)S(1)}, u32[]{:S(2)}, u32[]{:S(2)}) collective-permute-start(bf16[3,16,896]{2,1,0:T(8,128)(2,1)S(1)} %get-tuple-element.34), channel_id=1, source_target_pairs={{0,16},{16,32},{32,48},{48,64},{64,80},{80,96},{96,112},{112,128},... | collective-permute-start | bytes 258056 | tf_op jit(solution)/shard_map/ppermute | solution.py:24
  94.8 12.5 %collective-permute-start.7 = (bf16[3,16,896]{2,1,0:T(8,128)(2,1)S(1)}, bf16[3,16,896]{2,1,0:T(8,128)(2,1)S(1)}, u32[]{:S(2)}, u32[]{:S(2)}) collective-permute-start(bf16[3,16,896]{2,1,0:T(8,128)(2,1)S(1)} %get-tuple-element.35), channel_id=1, source_target_pairs={{32,0},{48,16},{64,32},{80,48},{96,64},{112,80},{128,96},{144,112}... | collective-permute-start | bytes 258056 | tf_op jit(solution)/shard_map/ppermute | solution.py:24
  96.8 10.4 %collective-permute-start.8 = (bf16[3,16,896]{2,1,0:T(8,128)(2,1)S(1)}, bf16[3,16,896]{2,1,0:T(8,128)(2,1)S(1)}, u32[]{:S(2)}, u32[]{:S(2)}) collective-permute-start(bf16[3,16,896]{2,1,0:T(8,128)(2,1)S(1)} %get-tuple-element.36), channel_id=1, source_target_pairs={{0,32},{16,48},{32,64},{48,80},{64,96},{80,112},{96,128},{112,144}... | collective-permute-start | bytes 258056 | tf_op jit(solution)/shard_map/ppermute | solution.py:24
Sparse Core Ops, SparseCore 0:
  10.7 55.1 all-gather.1
  74.5 44.8 reduce-scatter.1

commit v3 on v1

--- a/solution.py
+++ b/solution.py
@@ -94,9 +94,22 @@
             sent[d][c] = values[d * SLOT : (d + 1) * SLOT]
 
 
+def split_order(width, half, core):
+    count = width // 2
+    part = width // HEADS // 2
+    slot = lax.broadcasted_iota(jnp.int32, (1, count), 1)
+    chip = jnp.zeros((1, count), jnp.int32)
+    for x in range(1, HEADS):
+        chip += jnp.where(slot >= x * part, 1, 0)
+    side = core if half == 0 else 1 - core
+    source = slot + part * chip + part * side
+    row = lax.broadcasted_iota(jnp.int32, (width, count), 0)
+    return jnp.where(row == source, 1.0, 0.0).astype(BF16)
+
+
 def forward_kernel(
     group, table, kept, segments, codes, scales, r0, r1, r2, r3, grad_out,
-    term, context_out, balanced, probs_out, turned
+    term_other, context_out, turned_own, balanced, probs_out, turned
 ):
     rows, width = codes.shape[1:]
     size = width // HEADS
@@ -105,6 +118,7 @@
     @pl.when(pl.program_id(0) == 0)
     def _():
         at = lax.axis_index("dp")
+        core = lax.rem(lax.axis_index("fsdp"), 2)
         keep = kept[0, 0]
         spans = placed_spans(table, at, group)
         place = one_hot(spans, rows, False)
@@ -138,40 +152,61 @@
             probs = weights / jnp.sum(weights, axis=1, keepdims=True)
             probs_out[head] = probs
             add_tiles(tiles, dot(probs.astype(BF16), values), low)
-        context = jnp.concatenate(tiles, axis=1)
-        context_out[...] = context.astype(BF16)
-        turned[...] = context.T.astype(BF16)
-
-    term[...] = dot(turned[...], grad_out[...]).astype(BF16)
+        context = jnp.concatenate(tiles, axis=1).astype(BF16)
+        context_out[...] = context
+        part = width // HEADS // 2
+        for half, flipped in enumerate((turned_own, turned)):
+            across = dot(context, split_order(width, half, core)).T
+            upper, lower = [
+                [across[x * part + low : x * part + low + part // 2] for x in range(HEADS)]
+                for low in (0, part // 2)
+            ]
+            flipped[0] = jnp.concatenate(upper + lower, axis=0).astype(BF16)
+            flipped[1] = across.astype(BF16)
+
+    term_other[...] = dot(turned[pl.program_id(0)], grad_out[...]).astype(BF16)
+
+
+def fold_kernel(turned_own, grad_out, arrived, paired, plain):
+    own = dot(turned_own[0], grad_out[...]).astype(BF16)
+    folded = (own.astype(F32) + arrived[...].astype(F32)).astype(BF16)
+
+    @pl.when(pl.program_id(0) == 0)
+    def _():
+        count = folded.shape[0] // 2
+        paired[...] = jnp.concatenate([folded[:count], folded[count:]], axis=1)
+
+    @pl.when(pl.program_id(0) == 1)
+    def _():
+        plain[...] = folded
+
+
+def join_kernel(paired, plain, grad_w):
+    columns = plain.shape[1]
+    left = paired[...].astype(F32)
+    left = jnp.concatenate([left[:, :columns], left[:, columns:]], axis=0)
+    grad_w[...] = jnp.concatenate([left, plain[...].astype(F32)], axis=1)
+
+
+def output_kernel(context, w, output):
+    output[...] = dot(context[...], w[...]).astype(BF16)
 
 
 def backward_kernel(
-    group, table, kept, w, grad_out, context, balanced, probs_in, scales,
-    output, home, b0, b1, b2, b3, total_out, grad_context
+    group, table, kept, w, grad_out, balanced, probs_in, scales,
+    home, b0, b1, b2, b3, upstream_all
 ):
     step = pl.program_id(0)
     rows, width = balanced.shape[1:]
     size = width // HEADS
     factor = 1.0 / math.sqrt(size)
-    part = dot(context[...], w[...])
-
-    @pl.when(step == 0)
-    def _():
-        total_out[...] = part
-
-    @pl.when(step > 0)
-    def _():
-        total_out[...] += part
-
-    grad_context[step] = dot(grad_out[...], w[...], NT).astype(BF16)
+    upstream_all[step] = dot(grad_out[...], w[...], NT).astype(BF16)
 
     @pl.when(step == pl.num_programs(0) - 1)
     def _():
-        output[...] = total_out[...].astype(BF16)
         at = lax.axis_index("dp")
         keep = kept[0, 0]
-        count = width // LANES
-        grads = [[None] * count for _ in range(3)]
+        grads = [[None] * (width // LANES) for _ in range(3)]
         for head in range(HEADS):
             low, high = window(head, size)
             cut = slice(low * LANES, high * LANES)
@@ -183,7 +218,7 @@
             query = masked(balanced[0, :, cut])
             keys = masked(balanced[1, :, cut])
             values = balanced[2, :, cut]
-            upstream = masked(jnp.concatenate([grad_context[i] for i in range(low, high)], axis=1))
+            upstream = masked(jnp.concatenate([upstream_all[i] for i in range(low, high)], axis=1))
             probs = probs_in[head]
             grad_probs = dot(upstream, values, NT)
             total = jnp.sum(probs * grad_probs, axis=1, keepdims=True)
@@ -230,8 +265,14 @@
     _, rows, width = codes.shape
     depth = w_out.shape[1]
     blocks = scales.shape[1]
+    devices = lax.axis_size("fsdp")
+    half = width // 2
+    cores = [list(range(core, devices, 2)) for core in range(2)]
+    swap = [(i, i + 1 - 2 * (i % 2)) for i in range(devices)]
     smem = pl.BlockSpec(memory_space=pltpu.SMEM)
-    params = pltpu.CompilerParams(vmem_limit_bytes=24 * 1024 * 1024)
+    params = pltpu.CompilerParams(vmem_limit_bytes=56 * 1024 * 1024)
+    light = pltpu.CompilerParams(vmem_limit_bytes=24 * 1024 * 1024)
+    small = pl.CostEstimate(flops=1, bytes_accessed=1, transcendentals=0)
     piece = jax.ShapeDtypeStruct((3, SLOT, width), BF16)
     piece_spec = whole((3, SLOT, width))
     codes_spec = whole((3, rows, width))
@@ -245,62 +286,92 @@
         in_specs=[smem, codes_spec, scales_spec],
         out_specs=[piece_spec] * 4,
         compiler_params=params,
+        cost_estimate=small,
         name="pack",
     )(table, codes, scales)
     received = [shifted(sent[d], "dp", OFFSETS[d]) for d in range(4)]
 
-    chunk = 256
-    term, context, balanced, probs = pl.pallas_call(
+    span = depth // 2
+    term_spec = pl.BlockSpec((half, span), lambda n: (0, n))
+    grad_spec = pl.BlockSpec((rows, span), lambda n: (0, n))
+    term_other, context, turned_own, balanced, probs = pl.pallas_call(
         functools.partial(forward_kernel, group),
-        grid=(depth // chunk,),
+        grid=(2,),
         out_shape=[
-            jax.ShapeDtypeStruct((width, depth), BF16),
+            jax.ShapeDtypeStruct((half, depth), BF16),
             jax.ShapeDtypeStruct((rows, width), BF16),
+            jax.ShapeDtypeStruct((2, half, rows), BF16),
             jax.ShapeDtypeStruct((3, rows, width), BF16),
             jax.ShapeDtypeStruct((HEADS, rows, rows), F32),
         ],
         in_specs=[smem, smem, whole((1, rows)), codes_spec, scales_spec]
         + [piece_spec] * 4
-        + [pl.BlockSpec((rows, chunk), lambda n: (0, n))],
+        + [grad_spec],
         out_specs=[
-            pl.BlockSpec((width, chunk), lambda n: (0, n)),
+            term_spec,
             whole((rows, width)),
+            whole((2, half, rows)),
             codes_spec,
             whole((HEADS, rows, rows)),
         ],
-        scratch_shapes=[pltpu.VMEM((width, rows), BF16)],
+        scratch_shapes=[pltpu.VMEM((2, half, rows), BF16)],
         compiler_params=params,
+        cost_estimate=small,
         name="forward",
     )(table, kept_rows, segments, codes, scales, *received, grad_out)
-
-    grad_w = lax.psum_scatter(term, "fsdp", scatter_dimension=0, tiled=True).astype(F32)
-
-    output, home, *back = pl.pallas_call(
+    arrived = lax.ppermute(term_other, "fsdp", swap)
+    paired, plain = pl.pallas_call(
+        fold_kernel,
+        grid=(2,),
+        out_shape=[
+            jax.ShapeDtypeStruct((half // 2, depth), BF16),
+            jax.ShapeDtypeStruct((half, span), BF16),
+        ],
+        in_specs=[
+            pl.BlockSpec((1, half, rows), lambda n: (n, 0, 0)),
+            grad_spec,
+            term_spec,
+        ],
+        out_specs=[whole((half // 2, depth)), whole((half, span))],
+        compiler_params=light,
+        name="fold",
+    )(turned_own, grad_out, arrived)
+    plain = lax.psum_scatter(
+        plain, "fsdp", scatter_dimension=0, tiled=True, axis_index_groups=cores
+    )
+    paired = lax.psum_scatter(
+        paired, "fsdp", scatter_dimension=0, tiled=True, axis_index_groups=cores
+    )
+    balanced, paired = lax.optimization_barrier((balanced, paired))
+
+    home, *back = pl.pallas_call(
         functools.partial(backward_kernel, group),
         grid=(width // LANES,),
-        out_shape=[
-            jax.ShapeDtypeStruct((rows, depth), BF16),
-            jax.ShapeDtypeStruct((3, rows, width), BF16),
-        ]
-        + [piece] * 4,
+        out_shape=[jax.ShapeDtypeStruct((3, rows, width), BF16)] + [piece] * 4,
         in_specs=[
             smem,
             smem,
             pl.BlockSpec((LANES, depth), lambda n: (n, 0)),
             whole((rows, depth)),
-            pl.BlockSpec((rows, LANES), lambda n: (0, n)),
             codes_spec,
             whole((HEADS, rows, rows)),
             scales_spec,
         ],
-        out_specs=[whole((rows, depth)), codes_spec] + [piece_spec] * 4,
-        scratch_shapes=[
-            pltpu.VMEM((rows, depth), F32),
-            pltpu.VMEM((width // LANES, rows, LANES), BF16),
-        ],
+        out_specs=[codes_spec] + [piece_spec] * 4,
+        scratch_shapes=[pltpu.VMEM((width // LANES, rows, LANES), BF16)],
         compiler_params=params,
         name="backward",
-    )(table, kept_rows, w_full, grad_out, context, balanced, probs, scales)
+    )(table, kept_rows, w_full, grad_out, balanced, probs, scales)
+    chunk = 256
+    output = pl.pallas_call(
+        output_kernel,
+        grid=(depth // chunk,),
+        out_shape=jax.ShapeDtypeStruct((rows, depth), BF16),
+        in_specs=[whole((rows, width)), pl.BlockSpec((width, chunk), lambda n: (0, n))],
+        out_specs=pl.BlockSpec((rows, chunk), lambda n: (0, n)),
+        compiler_params=params,
+        name="project",
+    )(context, w_full)
     returned = [shifted(back[d], "dp", -OFFSETS[d]) for d in range(4)]
 
     grad_codes = pl.pallas_call(
@@ -308,9 +379,16 @@
         out_shape=jax.ShapeDtypeStruct((3, rows, width), BF16),
         in_specs=[smem, codes_spec, scales_spec] + [piece_spec] * 4,
         out_specs=codes_spec,
-        compiler_params=params,
+        compiler_params=light,
         name="restore",
     )(table, home, scales, *returned)
+    paired, grad_codes = lax.optimization_barrier((paired, grad_codes))
+    grad_w = pl.pallas_call(
+        join_kernel,
+        out_shape=jax.ShapeDtypeStruct(w_out.shape, F32),
+        compiler_params=light,
+        name="join",
+    )(paired, plain)
     grad_codes = jnp.transpose(grad_codes, (1, 0, 2))
     return (output[None, None], grad_codes[None, None], grad_w[None])
 

time: 147 us -> 127 us (0.86)
  the two profiles are of different devices: /device:TPU:112 before, /device:TPU:498 now
where the time goes in v3:
time: 127 us; the launch traced here: 126 us
  starting transfers between devices  37.5 us (30%)
  Pallas kernels  29 us (23%)
  blocking collectives  22.9 us (18%)
  between operations  17 us (13%)
  waiting for transfers between devices  15.6 us (12%)
  local copies, waits for them, and re-layouts  4.11 us (3%)
    ppermute x8, starting transfers between devices, shifted(): return lax.ppermute(block, axis, route)  32.9 us
    unnamed x1, blocking collectives  22.9 us
    pallas_call x1, Pallas kernels, local(): pl.pallas_call(functools.partial(backward_kernel, group), grid=(width //...  9.81 us
    ppermute x8, waiting for transfers between devices, shifted(): return lax.ppermute(block, axis, route)  8.3 us
    pallas_call x1, Pallas kernels, local(): pl.pallas_call(output_kernel, grid=(depth // chunk,), out_shape=jax.Shape...  5.96 us
    pallas_call x1, Pallas kernels, local(): pl.pallas_call(functools.partial(forward_kernel, group), grid=(2,), out_s...  5.95 us
    unnamed x23, local copies, waits for them, and re-layouts  4.07 us
    unnamed x4, waiting for transfers between devices  3.63 us
  transfers between devices with their start and end apart: 12, of which 5 were waited for; matrix products, arithmetic and copies ran while one was open for 19% of the time, Pallas kernels for 22%

profile of v3, /device:TPU:498, one launch (start us, length us, event | category | flops | bytes accessed | tf_op | source)
XLA Modules:
  0.0 126.1 jit_solution(4573035350554600489)
XLA Ops:
  8.0 0.0 copy-start
  8.0 0.0 all-gather.2.cloned.1.call-start
  8.1 0.7 all-gather.2.cloned.1.call-update
  8.7 0.0 reduce-scatter.6.cloned.1.call-start
  8.8 2.3 %pack.1 = (bf16[3,16,896]{2,1,0:T(8,128)(2,1)}, bf16[3,16,896]{2,1,0:T(8,128)(2,1)}, bf16[3,16,896]{2,1,0:T(8,128)(2,1)}, bf16[3,16,896]{2,1,0:T(8,128)(2,1)}) custom-call(s32[3,4,64]{2,1,0:T(4,128)} %bitcast.22, bf16[3,128,896]{2,1,0:T(8,128)(2,1)} %bitcast.30, bf16[3,7,128]{2,1,0:T(8,128)(2,1)} %bitcast.26), custom_call_target="tpu_custom_call" | custom-call | flops 1 | bytes 1 | tf_op jit(solution)/shard_map/pack/pallas_call | solution.py:283
  11.1 4.8 %collective-permute-start = (bf16[3,16,896]{2,1,0:T(8,128)(2,1)}, bf16[3,16,896]{2,1,0:T(8,128)(2,1)S(1)}, u32[]{:S(2)}, u32[]{:S(2)}) collective-permute-start(bf16[3,16,896]{2,1,0:T(8,128)(2,1)} %get-tuple-element.23), channel_id=1, source_target_pairs={{0,16},{16,32},{32,48},{48,64},{64,80},{80,96},{96,112},{112,128},... | collective-permute-start | bytes 258056 | tf_op jit(solution)/shard_map/ppermute | solution.py:24
  15.9 1.9 %collective-permute-start.1 = (bf16[3,16,896]{2,1,0:T(8,128)(2,1)}, bf16[3,16,896]{2,1,0:T(8,128)(2,1)S(1)}, u32[]{:S(2)}, u32[]{:S(2)}) collective-permute-start(bf16[3,16,896]{2,1,0:T(8,128)(2,1)} %get-tuple-element.24), channel_id=1, source_target_pairs={{16,0},{32,16},{48,32},{64,48},{80,64},{96,80},{112,96},{128,112},... | collective-permute-start | bytes 258056 | tf_op jit(solution)/shard_map/ppermute | solution.py:24
  17.8 5.0 %collective-permute-start.2 = (bf16[3,16,896]{2,1,0:T(8,128)(2,1)}, bf16[3,16,896]{2,1,0:T(8,128)(2,1)S(1)}, u32[]{:S(2)}, u32[]{:S(2)}) collective-permute-start(bf16[3,16,896]{2,1,0:T(8,128)(2,1)} %get-tuple-element.25), channel_id=1, source_target_pairs={{0,32},{16,48},{32,64},{48,80},{64,96},{80,112},{96,128},{112,144}... | collective-permute-start | bytes 258056 | tf_op jit(solution)/shard_map/ppermute | solution.py:24
  22.9 1.9 %collective-permute-start.3 = (bf16[3,16,896]{2,1,0:T(8,128)(2,1)}, bf16[3,16,896]{2,1,0:T(8,128)(2,1)S(1)}, u32[]{:S(2)}, u32[]{:S(2)}) collective-permute-start(bf16[3,16,896]{2,1,0:T(8,128)(2,1)} %get-tuple-element.26), channel_id=1, source_target_pairs={{32,0},{48,16},{64,32},{80,48},{96,64},{112,80},{128,96},{144,112}... | collective-permute-start | bytes 258056 | tf_op jit(solution)/shard_map/ppermute | solution.py:24
  25.4 0.0 collective-permute-done.r0
  25.5 0.0 copy-start.6
  25.5 0.3 collective-permute-done.1.r1
  25.8 0.0 copy-start.7
  25.8 0.8 collective-permute-done.2.r2
  26.6 0.0 copy-start.8
  26.6 7.2 %collective-permute-done.3.r3 = bf16[3,16,896]{2,1,0:T(8,128)(2,1)S(1)} collective-permute-done((bf16[3,16,896]{2,1,0:T(8,128)(2,1)}, bf16[3,16,896]{2,1,0:T(8,128)(2,1)S(1)}, u32[]{:S(2)}, u32[]{:S(2)}) %collective-permute-start.3) | collective-permute-done | bytes 86048 | tf_op jit(solution)/shard_map/ppermute | solution.py:24
  33.8 0.0 copy-start.9
  33.8 0.0 copy-done.6
  33.8 0.0 copy-done.7
  33.8 0.0 copy-done.8
  33.8 0.6 copy-done.9
  34.4 6.0 %forward.1 = (bf16[448,1792]{1,0:T(8,128)(2,1)}, bf16[128,896]{1,0:T(8,128)(2,1)}, bf16[2,448,128]{2,1,0:T(8,128)(2,1)}, bf16[3,128,896]{2,1,0:T(8,128)(2,1)}, f32[8,128,128]{2,1,0:T(8,128)}) custom-call(s32[3,4,64]{2,1,0:T(4,128)} %bitcast.23, s32[1,1]{1,0:T(1,128)S(6)} %copy.10.kept, s32[1,128]{1,0:T(1,128)} %bitcast.35, bf16[3,128,896]{2,1,0:T(8,128)(2,1)} %bitcast.31, ...), custom_call_target="tpu_custom_call" | custom-call | flops 1 | bytes 1 | tf_op jit(solution)/shard_map/forward/pallas_call | solution.py:297
  40.4 1.9 %collective-permute-start.4 = (bf16[448,1792]{1,0:T(8,128)(2,1)}, bf16[448,1792]{1,0:T(8,128)(2,1)S(1)}, u32[]{:S(2)}, u32[]{:S(2)}) collective-permute-start(bf16[448,1792]{1,0:T(8,128)(2,1)} %get-tuple-element.30), channel_id=1, source_target_pairs={{0,1},{1,0},{2,3},{3,2},{4,5},{5,4},{6,7},{7,6},{8,9},{9,8},{10,11... | collective-permute-start | bytes 4816904 | tf_op jit(solution)/shard_map/ppermute | solution.py:322
  42.3 3.6 %collective-permute-done.4.arrived = bf16[448,1792]{1,0:T(8,128)(2,1)S(1)} collective-permute-done((bf16[448,1792]{1,0:T(8,128)(2,1)}, bf16[448,1792]{1,0:T(8,128)(2,1)S(1)}, u32[]{:S(2)}, u32[]{:S(2)}) %collective-permute-start.4) | collective-permute-done | bytes 1605664 | tf_op jit(solution)/shard_map/ppermute | solution.py:322
  45.9 0.0 copy-done
  45.9 0.0 copy-start.2
  45.9 0.9 copy-done.2
  46.9 2.0 %fold.1 = (bf16[224,1792]{1,0:T(8,128)(2,1)S(1)}, bf16[448,896]{1,0:T(8,128)(2,1)}) custom-call(bf16[2,448,128]{2,1,0:T(8,128)(2,1)S(1)} %copy-done.2, bf16[128,1792]{1,0:T(8,128)(2,1)S(1)} %bitcast.21, bf16[448,1792]{1,0:T(8,128)(2,1)S(1)} %collective-permute-done.4.arrived), custom_call_target="tpu_custom_call" | custom-call | tf_op jit(solution)/shard_map/fold/pallas_call | solution.py:323
  48.8 0.0 reduce-scatter.6.cloned.1.call-update
  48.9 22.9 %fusion = bf16[32,1792]{1,0:T(8,128)(2,1)S(1)} fusion(bf16[224,1792]{1,0:T(8,128)(2,1)S(1)} %get-tuple-element.31), kind=kCustom, calls=%all-reduce-scatter | all-reduce-scatter fusion | flops 458753 | bytes 921600
  71.8 2.6 %collective-permute-start.9 = (bf16[28,1792]{1,0:T(8,128)(2,1)S(1)}, bf16[28,1792]{1,0:T(8,128)(2,1)S(1)}, u32[]{:S(2)}, u32[]{:S(2)}) collective-permute-start(bf16[28,1792]{1,0:T(8,128)(2,1)S(1)} %slice), channel_id=1, source_target_pairs={{0,2},{2,4},{4,6},{6,8},{8,10},{10,12},{12,14},{1,3},{3,5},{5,7},{... | collective-permute-start | bytes 301064
  74.5 1.3 %dynamic-slice.6 = u32[1]{0:T(128)} dynamic-slice(u32[1024]{0:T(1024)} %constant.9, u32[]{:S(6)} %partition-id.5), dynamic_slice_sizes={1} | dynamic-slice | bytes 12
  76.4 2.9 %collective-permute-done.9 = bf16[28,1792]{1,0:T(8,128)(2,1)S(1)} collective-permute-done((bf16[28,1792]{1,0:T(8,128)(2,1)S(1)}, bf16[28,1792]{1,0:T(8,128)(2,1)S(1)}, u32[]{:S(2)}, u32[]{:S(2)}) %collective-permute-start.9) | collective-permute-done | bytes 100384
  79.3 0.3 concatenate
  79.6 0.0 all-gather.2.cloned.1.call-done.w
  79.7 9.8 %backward.1 = (bf16[3,128,896]{2,1,0:T(8,128)(2,1)}, bf16[3,16,896]{2,1,0:T(8,128)(2,1)}, bf16[3,16,896]{2,1,0:T(8,128)(2,1)}, bf16[3,16,896]{2,1,0:T(8,128)(2,1)}, bf16[3,16,896]{2,1,0:T(8,128)(2,1)}) custom-call(s32[3,4,64]{2,1,0:T(4,128)} %bitcast.24, s32[1,1]{1,0:T(1,128)S(6)} %copy.10.kept, bf16[896,1792]{1,0:T(8,128)(2,1)} %all-gather.2.cloned.1.call-done.w, ...), custom_call_target="tpu_custom_call" | custom-call | tf_op jit(solution)/shard_map/backward/pallas_call | solution.py:347
  89.5 5.9 %collective-permute-start.5 = (bf16[3,16,896]{2,1,0:T(8,128)(2,1)}, bf16[3,16,896]{2,1,0:T(8,128)(2,1)S(1)}, u32[]{:S(2)}, u32[]{:S(2)}) collective-permute-start(bf16[3,16,896]{2,1,0:T(8,128)(2,1)} %get-tuple-element.36), channel_id=1, source_target_pairs={{16,0},{32,16},{48,32},{64,48},{80,64},{96,80},{112,96},{128,112},... | collective-permute-start | bytes 258056 | tf_op jit(solution)/shard_map/ppermute | solution.py:24
  95.4 3.2 %collective-permute-start.6 = (bf16[3,16,896]{2,1,0:T(8,128)(2,1)}, bf16[3,16,896]{2,1,0:T(8,128)(2,1)S(1)}, u32[]{:S(2)}, u32[]{:S(2)}) collective-permute-start(bf16[3,16,896]{2,1,0:T(8,128)(2,1)} %get-tuple-element.37), channel_id=1, source_target_pairs={{0,16},{16,32},{32,48},{48,64},{64,80},{80,96},{96,112},{112,128},... | collective-permute-start | bytes 258056 | tf_op jit(solution)/shard_map/ppermute | solution.py:24
  98.6 2.1 %collective-permute-start.7 = (bf16[3,16,896]{2,1,0:T(8,128)(2,1)}, bf16[3,16,896]{2,1,0:T(8,128)(2,1)S(1)}, u32[]{:S(2)}, u32[]{:S(2)}) collective-permute-start(bf16[3,16,896]{2,1,0:T(8,128)(2,1)} %get-tuple-element.38), channel_id=1, source_target_pairs={{32,0},{48,16},{64,32},{80,48},{96,64},{112,80},{128,96},{144,112}... | collective-permute-start | bytes 258056 | tf_op jit(solution)/shard_map/ppermute | solution.py:24
  100.7 8.0 %collective-permute-start.8 = (bf16[3,16,896]{2,1,0:T(8,128)(2,1)}, bf16[3,16,896]{2,1,0:T(8,128)(2,1)S(1)}, u32[]{:S(2)}, u32[]{:S(2)}) collective-permute-start(bf16[3,16,896]{2,1,0:T(8,128)(2,1)} %get-tuple-element.39), channel_id=1, source_target_pairs={{0,32},{16,48},{32,64},{48,80},{64,96},{80,112},{96,128},{112,144}... | collective-permute-start | bytes 258056 | tf_op jit(solution)/shard_map/ppermute | solution.py:24
  108.7 0.0 copy-start.1
  108.7 0.0 copy-start.4
  108.7 0.0 copy-start.5
  108.7 6.0 %project.1 = bf16[128,1792]{1,0:T(8,128)(2,1)} custom-call(bf16[128,896]{1,0:T(8,128)(2,1)} %get-tuple-element.27.context, bf16[896,1792]{1,0:T(8,128)(2,1)} %all-gather.2.cloned.1.call-done.w), custom_call_target="tpu_custom_call" | custom-call | tf_op jit(solution)/shard_map/project/pallas_call | solution.py:366
  114.7 0.0 collective-permute-done.5.r0
  114.7 0.0 collective-permute-done.6.r1
  114.7 0.0 collective-permute-done.7.r2
  114.7 0.0 collective-permute-done.8.r3
  114.7 0.0 copy-done.1
  114.7 0.0 copy-done.4
  114.7 0.0 copy-done.5
  114.8 2.2 %restore.1 = bf16[3,128,896]{2,1,0:T(8,128)(2,1)} custom-call(s32[3,4,64]{2,1,0:T(4,128)S(1)} %bitcast.25, bf16[3,128,896]{2,1,0:T(8,128)(2,1)S(1)} %copy-done.1, bf16[3,7,128]{2,1,0:T(8,128)(2,1)S(1)} %bitcast.29, bf16[3,16,896]{2,1,0:T(8,128)(2,1)S(1)} %collective-permute-done.5.r0, bf16[3,16,896]{2,1,0:T(8,128)(2,1)S(1)} %collective-permute-done.6.r1, ...), custom_call_target="tpu_custom_call" | custom-call | tf_op jit(solution)/shard_map/restore/pallas_call | solution.py:377
  117.0 0.0 reduce-scatter.6.cloned.1.call-done.plain
  117.0 0.0 copy-start.3
  117.0 0.9 copy-done.3
  117.9 0.8 join.1
  (2 shorter events, 0.1 us)
Async XLA Ops:
  8.0 37.9 %copy-start = (bf16[1,1,128,1792]{3,2,1,0:T(8,128)(2,1)S(1)}, bf16[1,1,128,1792]{3,2,1,0:T(8,128)(2,1)}, u32[]{:S(2)}) copy-start(bf16[1,1,128,1792]{3,2,1,0:T(8,128)(2,1)} %param.13) | copy-start | bytes 1376260
  8.0 71.6 %all-gather.2.cloned.1.call-start = ((), (), s32[]{:S(2)}) async-start(), calls=%async_computation.1 | async-start | bytes 3411968 | tf_op jit(solution)/shard_map/all_gather | solution.py:281
  8.7 108.3 %reduce-scatter.6.cloned.1.call-start = ((), (), s32[]{:S(2)}) async-start(), calls=%async_computation.2 | async-start | bytes 903168
  11.1 14.4 %collective-permute-start = (bf16[3,16,896]{2,1,0:T(8,128)(2,1)}, bf16[3,16,896]{2,1,0:T(8,128)(2,1)S(1)}, u32[]{:S(2)}, u32[]{:S(2)}) collective-permute-start(bf16[3,16,896]{2,1,0:T(8,128)(2,1)} %get-tuple-element.23), channel_id=1, source_target_pairs={{0,16},{16,32},{32,48},{48,64},{64,80},{80,96},{96,112},{112,128},... | collective-permute-start | bytes 258056 | tf_op jit(solution)/shard_map/ppermute | solution.py:24
  15.9 9.9 %collective-permute-start.1 = (bf16[3,16,896]{2,1,0:T(8,128)(2,1)}, bf16[3,16,896]{2,1,0:T(8,128)(2,1)S(1)}, u32[]{:S(2)}, u32[]{:S(2)}) collective-permute-start(bf16[3,16,896]{2,1,0:T(8,128)(2,1)} %get-tuple-element.24), channel_id=1, source_target_pairs={{16,0},{32,16},{48,32},{64,48},{80,64},{96,80},{112,96},{128,112},... | collective-permute-start | bytes 258056 | tf_op jit(solution)/shard_map/ppermute | solution.py:24
  17.8 8.8 %collective-permute-start.2 = (bf16[3,16,896]{2,1,0:T(8,128)(2,1)}, bf16[3,16,896]{2,1,0:T(8,128)(2,1)S(1)}, u32[]{:S(2)}, u32[]{:S(2)}) collective-permute-start(bf16[3,16,896]{2,1,0:T(8,128)(2,1)} %get-tuple-element.25), channel_id=1, source_target_pairs={{0,32},{16,48},{32,64},{48,80},{64,96},{80,112},{96,128},{112,144}... | collective-permute-start | bytes 258056 | tf_op jit(solution)/shard_map/ppermute | solution.py:24
  22.9 10.9 %collective-permute-start.3 = (bf16[3,16,896]{2,1,0:T(8,128)(2,1)}, bf16[3,16,896]{2,1,0:T(8,128)(2,1)S(1)}, u32[]{:S(2)}, u32[]{:S(2)}) collective-permute-start(bf16[3,16,896]{2,1,0:T(8,128)(2,1)} %get-tuple-element.26), channel_id=1, source_target_pairs={{32,0},{48,16},{64,32},{80,48},{96,64},{112,80},{128,96},{144,112}... | collective-permute-start | bytes 258056 | tf_op jit(solution)/shard_map/ppermute | solution.py:24
  25.5 8.3 %copy-start.6 = (bf16[3,16,896]{2,1,0:T(8,128)(2,1)}, bf16[3,16,896]{2,1,0:T(8,128)(2,1)S(1)}, u32[]{:S(2)}) copy-start(bf16[3,16,896]{2,1,0:T(8,128)(2,1)S(1)} %collective-permute-done.r0) | copy-start | bytes 258052
  25.8 8.0 %copy-start.7 = (bf16[3,16,896]{2,1,0:T(8,128)(2,1)}, bf16[3,16,896]{2,1,0:T(8,128)(2,1)S(1)}, u32[]{:S(2)}) copy-start(bf16[3,16,896]{2,1,0:T(8,128)(2,1)S(1)} %collective-permute-done.1.r1) | copy-start | bytes 258052
  26.6 7.2 %copy-start.8 = (bf16[3,16,896]{2,1,0:T(8,128)(2,1)}, bf16[3,16,896]{2,1,0:T(8,128)(2,1)S(1)}, u32[]{:S(2)}) copy-start(bf16[3,16,896]{2,1,0:T(8,128)(2,1)S(1)} %collective-permute-done.2.r2) | copy-start | bytes 258052
  33.8 0.7 copy-start.9
  40.4 5.5 %collective-permute-start.4 = (bf16[448,1792]{1,0:T(8,128)(2,1)}, bf16[448,1792]{1,0:T(8,128)(2,1)S(1)}, u32[]{:S(2)}, u32[]{:S(2)}) collective-permute-start(bf16[448,1792]{1,0:T(8,128)(2,1)} %get-tuple-element.30), channel_id=1, source_target_pairs={{0,1},{1,0},{2,3},{3,2},{4,5},{5,4},{6,7},{7,6},{8,9},{9,8},{10,11... | collective-permute-start | bytes 4816904 | tf_op jit(solution)/shard_map/ppermute | solution.py:322
  45.9 0.9 copy-start.2
  71.8 7.5 %collective-permute-start.9 = (bf16[28,1792]{1,0:T(8,128)(2,1)S(1)}, bf16[28,1792]{1,0:T(8,128)(2,1)S(1)}, u32[]{:S(2)}, u32[]{:S(2)}) collective-permute-start(bf16[28,1792]{1,0:T(8,128)(2,1)S(1)} %slice), channel_id=1, source_target_pairs={{0,2},{2,4},{4,6},{6,8},{8,10},{10,12},{12,14},{1,3},{3,5},{5,7},{... | collective-permute-start | bytes 301064
  89.5 25.2 %collective-permute-start.5 = (bf16[3,16,896]{2,1,0:T(8,128)(2,1)}, bf16[3,16,896]{2,1,0:T(8,128)(2,1)S(1)}, u32[]{:S(2)}, u32[]{:S(2)}) collective-permute-start(bf16[3,16,896]{2,1,0:T(8,128)(2,1)} %get-tuple-element.36), channel_id=1, source_target_pairs={{16,0},{32,16},{48,32},{64,48},{80,64},{96,80},{112,96},{128,112},... | collective-permute-start | bytes 258056 | tf_op jit(solution)/shard_map/ppermute | solution.py:24
  95.4 19.3 %collective-permute-start.6 = (bf16[3,16,896]{2,1,0:T(8,128)(2,1)}, bf16[3,16,896]{2,1,0:T(8,128)(2,1)S(1)}, u32[]{:S(2)}, u32[]{:S(2)}) collective-permute-start(bf16[3,16,896]{2,1,0:T(8,128)(2,1)} %get-tuple-element.37), channel_id=1, source_target_pairs={{0,16},{16,32},{32,48},{48,64},{64,80},{80,96},{96,112},{112,128},... | collective-permute-start | bytes 258056 | tf_op jit(solution)/shard_map/ppermute | solution.py:24
  98.6 16.1 %collective-permute-start.7 = (bf16[3,16,896]{2,1,0:T(8,128)(2,1)}, bf16[3,16,896]{2,1,0:T(8,128)(2,1)S(1)}, u32[]{:S(2)}, u32[]{:S(2)}) collective-permute-start(bf16[3,16,896]{2,1,0:T(8,128)(2,1)} %get-tuple-element.38), channel_id=1, source_target_pairs={{32,0},{48,16},{64,32},{80,48},{96,64},{112,80},{128,96},{144,112}... | collective-permute-start | bytes 258056 | tf_op jit(solution)/shard_map/ppermute | solution.py:24
  100.7 14.0 %collective-permute-start.8 = (bf16[3,16,896]{2,1,0:T(8,128)(2,1)}, bf16[3,16,896]{2,1,0:T(8,128)(2,1)S(1)}, u32[]{:S(2)}, u32[]{:S(2)}) collective-permute-start(bf16[3,16,896]{2,1,0:T(8,128)(2,1)} %get-tuple-element.39), channel_id=1, source_target_pairs={{0,32},{16,48},{32,64},{48,80},{64,96},{80,112},{96,128},{112,144}... | collective-permute-start | bytes 258056 | tf_op jit(solution)/shard_map/ppermute | solution.py:24
  108.7 6.0 %copy-start.1 = (bf16[3,128,896]{2,1,0:T(8,128)(2,1)S(1)}, bf16[3,128,896]{2,1,0:T(8,128)(2,1)}, u32[]{:S(2)}) copy-start(bf16[3,128,896]{2,1,0:T(8,128)(2,1)} %get-tuple-element.35.home) | copy-start | bytes 2064388
  108.7 6.0 %copy-start.4 = (s32[64,1,4,3]{0,2,3,1:T(4,128)S(1)}, s32[64,1,4,3]{0,2,3,1:T(4,128)}, u32[]{:S(2)}) copy-start(s32[64,1,4,3]{0,2,3,1:T(4,128)} %param.11) | copy-start | bytes 9220
  108.7 6.0 %copy-start.5 = (bf16[1,1,128,3,7]{2,4,3,1,0:T(8,128)(2,1)S(1)}, bf16[1,1,128,3,7]{2,4,3,1,0:T(8,128)(2,1)}, u32[]{:S(2)}) copy-start(bf16[1,1,128,3,7]{2,4,3,1,0:T(8,128)(2,1)} %param.8) | copy-start | bytes 16132
  117.0 0.9 copy-start.3
Sparse Core Ops, SparseCore 0:
  11.5 52.6 all-gather.1
Sparse Core Ops, SparseCore 1:
  48.9 45.6 reduce-scatter.5

commit v4 on v2

--- a/solution.py
+++ b/solution.py
@@ -109,7 +109,7 @@
 
 def forward_kernel(
     group, table, kept, segments, codes, scales, r0, r1, r2, r3, grad_out,
-    term_other, context_own, context_other, turned_own, orders, balanced, probs_out, turned
+    term_other, context_out, turned_own, balanced, probs_out, turned
 ):
     rows, width = codes.shape[1:]
     size = width // HEADS
@@ -153,11 +153,9 @@
             probs_out[head] = probs
             add_tiles(tiles, dot(probs.astype(BF16), values), low)
         context = jnp.concatenate(tiles, axis=1).astype(BF16)
-        for half, (side, flipped) in enumerate(((context_own, turned_own), (context_other, turned))):
-            orders[half] = split_order(width, half, core)
-            picked = dot(context, orders[half])
-            side[...] = picked.astype(BF16)
-            flipped[...] = picked.T.astype(BF16)
+        context_out[...] = context
+        for half, flipped in enumerate((turned_own, turned)):
+            flipped[...] = dot(context, split_order(width, half, core)).T.astype(BF16)
 
     term_other[...] = dot(turned[...], grad_out[...]).astype(BF16)
 
@@ -167,26 +165,22 @@
     folded[...] = (own.astype(F32) + arrived[...].astype(F32)).astype(BF16)
 
 
-def upstream_kernel(grad_out, w, grad_context):
-    grad_context[...] = dot(grad_out[...], w[...], NT).astype(BF16)
-
-
-def output_kernel(context_own, context_other, w_own, w_other, output):
-    total = dot(context_own[...], w_own[...]) + dot(context_other[...], w_other[...])
-    output[...] = total.astype(BF16)
+def widen_kernel(narrow, wide):
+    wide[...] = narrow[...].astype(F32)
+
+
+def output_kernel(context, w, output):
+    output[...] = dot(context[...], w[...]).astype(BF16)
 
 
 def backward_kernel(
-    group, table, kept, w_other, grad_out, upstream_own, orders, balanced, probs_in, scales,
+    group, table, kept, w, grad_out, balanced, probs_in, scales,
     home, b0, b1, b2, b3, upstream_all
 ):
     rows, width = balanced.shape[1:]
     size = width // HEADS
     factor = 1.0 / math.sqrt(size)
-    upstream_other = dot(grad_out[...], w_other[...], NT).astype(BF16)
-    upstream_all[...] = (
-        dot(upstream_own[...], orders[0], NT) + dot(upstream_other, orders[1], NT)
-    ).astype(BF16)
+    upstream_all[...] = dot(grad_out[...], w[...], NT).astype(BF16)
     at = lax.axis_index("dp")
     keep = kept[0, 0]
     grads = [[None] * (width // LANES) for _ in range(3)]
@@ -253,14 +247,15 @@
     cores = [list(range(core, devices, 2)) for core in range(2)]
     swap = [(i, i + 1 - 2 * (i % 2)) for i in range(devices)]
     smem = pl.BlockSpec(memory_space=pltpu.SMEM)
-    params = pltpu.CompilerParams(vmem_limit_bytes=48 * 1024 * 1024)
+    params = pltpu.CompilerParams(vmem_limit_bytes=56 * 1024 * 1024)
+    light = pltpu.CompilerParams(vmem_limit_bytes=24 * 1024 * 1024)
     small = pl.CostEstimate(flops=1, bytes_accessed=1, transcendentals=0)
     piece = jax.ShapeDtypeStruct((3, SLOT, width), BF16)
     piece_spec = whole((3, SLOT, width))
     codes_spec = whole((3, rows, width))
     scales_spec = whole((3, blocks, rows))
 
-    w_own = lax.all_gather(w_out, "fsdp", axis=0, tiled=True, axis_index_groups=cores)
+    w_full = lax.all_gather(w_out, "fsdp", axis=0, tiled=True)
 
     sent = pl.pallas_call(
         pack_kernel,
@@ -273,20 +268,16 @@
     )(table, codes, scales)
     received = [shifted(sent[d], "dp", OFFSETS[d]) for d in range(4)]
 
-    chunk = 256
-    half_context = jax.ShapeDtypeStruct((rows, half), BF16)
-    half_term = jax.ShapeDtypeStruct((half, depth), BF16)
-    term_spec = pl.BlockSpec((half, chunk), lambda n: (0, n))
-    grad_spec = pl.BlockSpec((rows, chunk), lambda n: (0, n))
-    term_other, context_own, context_other, turned_own, orders, balanced, probs = pl.pallas_call(
+    span = depth // 2
+    term_spec = pl.BlockSpec((half, span), lambda n: (0, n))
+    grad_spec = pl.BlockSpec((rows, span), lambda n: (0, n))
+    term_other, context, turned_own, balanced, probs = pl.pallas_call(
         functools.partial(forward_kernel, group),
-        grid=(depth // chunk,),
+        grid=(2,),
         out_shape=[
-            half_term,
-            half_context,
-            half_context,
+            jax.ShapeDtypeStruct((half, depth), BF16),
+            jax.ShapeDtypeStruct((rows, width), BF16),
             jax.ShapeDtypeStruct((half, rows), BF16),
-            jax.ShapeDtypeStruct((2, width, half), BF16),
             jax.ShapeDtypeStruct((3, rows, width), BF16),
             jax.ShapeDtypeStruct((HEADS, rows, rows), F32),
         ],
@@ -295,10 +286,8 @@
         + [grad_spec],
         out_specs=[
             term_spec,
-            whole((rows, half)),
-            whole((rows, half)),
+            whole((rows, width)),
             whole((half, rows)),
-            whole((2, width, half)),
             codes_spec,
             whole((HEADS, rows, rows)),
         ],
@@ -307,57 +296,48 @@
         cost_estimate=small,
         name="forward",
     )(table, kept_rows, segments, codes, scales, *received, grad_out)
-    w_own, term_other = lax.optimization_barrier((w_own, term_other))
     arrived = lax.ppermute(term_other, "fsdp", swap)
-    w_other = lax.ppermute(w_own, "fsdp", swap)
     folded = pl.pallas_call(
         fold_kernel,
-        grid=(depth // chunk,),
-        out_shape=half_term,
+        grid=(2,),
+        out_shape=jax.ShapeDtypeStruct((half, depth), BF16),
         in_specs=[whole((half, rows)), grad_spec, term_spec],
         out_specs=term_spec,
-        compiler_params=params,
+        compiler_params=light,
         name="fold",
     )(turned_own, grad_out, arrived)
-    grad_w = lax.psum_scatter(
+    balanced, folded = lax.optimization_barrier((balanced, folded))
+    scattered = lax.psum_scatter(
         folded, "fsdp", scatter_dimension=0, tiled=True, axis_index_groups=cores
-    ).astype(F32)
-
-    upstream_own = pl.pallas_call(
-        upstream_kernel,
-        out_shape=half_context,
-        compiler_params=params,
-        name="upstream",
-    )(grad_out, w_own)
+    )
+
     home, *back = pl.pallas_call(
         functools.partial(backward_kernel, group),
         out_shape=[jax.ShapeDtypeStruct((3, rows, width), BF16)] + [piece] * 4,
         in_specs=[
             smem,
             smem,
-            whole((half, depth)),
+            whole((width, depth)),
             whole((rows, depth)),
-            whole((rows, half)),
-            whole((2, width, half)),
             codes_spec,
             whole((HEADS, rows, rows)),
             scales_spec,
         ],
         out_specs=[codes_spec] + [piece_spec] * 4,
         scratch_shapes=[pltpu.VMEM((rows, width), BF16)],
-        compiler_params=params,
+        compiler_params=light,
         name="backward",
-    )(table, kept_rows, w_other, grad_out, upstream_own, orders, balanced, probs, scales)
-    weight_spec = pl.BlockSpec((half, chunk), lambda n: (0, n))
+    )(table, kept_rows, w_full, grad_out, balanced, probs, scales)
+    chunk = 256
     output = pl.pallas_call(
         output_kernel,
         grid=(depth // chunk,),
         out_shape=jax.ShapeDtypeStruct((rows, depth), BF16),
-        in_specs=[whole((rows, half))] * 2 + [weight_spec] * 2,
-        out_specs=grad_spec,
-        compiler_params=params,
+        in_specs=[whole((rows, width)), pl.BlockSpec((width, chunk), lambda n: (0, n))],
+        out_specs=pl.BlockSpec((rows, chunk), lambda n: (0, n)),
+        compiler_params=light,
         name="project",
-    )(context_own, context_other, w_own, w_other)
+    )(context, w_full)
     returned = [shifted(back[d], "dp", -OFFSETS[d]) for d in range(4)]
 
     grad_codes = pl.pallas_call(
@@ -365,9 +345,15 @@
         out_shape=jax.ShapeDtypeStruct((3, rows, width), BF16),
         in_specs=[smem, codes_spec, scales_spec] + [piece_spec] * 4,
         out_specs=codes_spec,
-        compiler_params=params,
+        compiler_params=light,
         name="restore",
     )(table, home, scales, *returned)
+    grad_w = pl.pallas_call(
+        widen_kernel,
+        out_shape=jax.ShapeDtypeStruct(w_out.shape, F32),
+        compiler_params=params,
+        name="widen",
+    )(scattered)
     grad_codes = jnp.transpose(grad_codes, (1, 0, 2))
     return (output[None, None], grad_codes[None, None], grad_w[None])
 

time: 130 us -> 118 us (0.908)
  waiting for transfers between devices: 46.6 us -> 37.6 us
  local copies, waits for them, and re-layouts: 10.4 us -> 7.49 us
  starting transfers between devices: 33.4 us -> 31.4 us
  other arithmetic: 1.7 us -> 0 us
  Pallas kernels: 21.1 us -> 22.8 us
  between operations: 14.8 us -> 16.3 us
    reduce_scatter x1, waiting for transfers between devices: 9.93 us -> 4.48 us  [local(): lax.psum_scatter(folded, 'fsdp', scatter_dimension=0, tiled=True, axis_in...]
    unnamed x28 -> x32, local copies, waits for them, and re-layouts: 10.4 us -> 7.49 us
    ppermute x1 -> x0, waiting for transfers between devices: 2.7 us -> none  [local(): w_other = lax.ppermute(w_own, 'fsdp', swap)]
    ppermute x1 -> x0, starting transfers between devices: 2.02 us -> none  [local(): w_other = lax.ppermute(w_own, 'fsdp', swap)]
    broadcast_in_dim x1 -> x0, other arithmetic: 1.7 us -> none  [local(): return (output[None, None], grad_codes[None, None], grad_w[None])]
  transfers between devices with their start and end apart: 12 -> 11, of which waited for: 6 -> 5; matrix products, arithmetic and copies ran while one was open for 0% -> 0% of each run, Pallas kernels for 15% -> 17%
where the time goes in v4:
time: 118 us; the launch traced here: 115 us
  waiting for transfers between devices  37.6 us (32%)
  starting transfers between devices  31.4 us (27%)
  Pallas kernels  22.8 us (19%)
  between operations  16.3 us (14%)
  local copies, waits for them, and re-layouts  7.49 us (6%)
    ppermute x8, starting transfers between devices, shifted(): return lax.ppermute(block, axis, route)  29.4 us
    all_gather x1, waiting for transfers between devices, local(): w_full = lax.all_gather(w_out, 'fsdp', axis=0, tiled=True)  20.9 us
    ppermute x8, waiting for transfers between devices, shifted(): return lax.ppermute(block, axis, route)  7.84 us
    unnamed x32, local copies, waits for them, and re-layouts  7.49 us
    pallas_call x1, Pallas kernels, local(): pl.pallas_call(functools.partial(forward_kernel, group), grid=(2,), out_s...  5.65 us
    pallas_call x1, Pallas kernels, local(): pl.pallas_call(functools.partial(backward_kernel, group), out_shape=[jax....  5.07 us
    reduce_scatter x1, waiting for transfers between devices, local(): lax.psum_scatter(folded, 'fsdp', scatter_dimension=0, tiled=True, axis_in...  4.48 us
    ppermute x1, waiting for transfers between devices, local(): arrived = lax.ppermute(term_other, 'fsdp', swap)  3.63 us
  transfers between devices with their start and end apart: 11, of which 5 were waited for; matrix products, arithmetic and copies ran while one was open for 0% of the time, Pallas kernels for 17%

profile of v4, /device:TPU:112, one launch (start us, length us, event | category | flops | bytes accessed | tf_op | source)
XLA Modules:
  0.0 115.5 jit_solution(14451856328795103852)
XLA Ops:
  8.0 0.0 copy-start.2
  8.0 0.0 all-gather.2.cloned.1.call-start
  8.1 0.7 all-gather.2.cloned.1.call-update
  8.7 0.0 reduce-scatter.2.cloned.1.call-start
  8.8 2.3 %pack.1 = (bf16[3,16,896]{2,1,0:T(8,128)(2,1)}, bf16[3,16,896]{2,1,0:T(8,128)(2,1)}, bf16[3,16,896]{2,1,0:T(8,128)(2,1)}, bf16[3,16,896]{2,1,0:T(8,128)(2,1)}) custom-call(s32[3,4,64]{2,1,0:T(4,128)} %bitcast.19, bf16[3,128,896]{2,1,0:T(8,128)(2,1)} %bitcast.27, bf16[3,7,128]{2,1,0:T(8,128)(2,1)} %bitcast.23), custom_call_target="tpu_custom_call" | custom-call | flops 1 | bytes 1 | tf_op jit(solution)/shard_map/pack/pallas_call | solution.py:260
  11.1 3.6 %collective-permute-start = (bf16[3,16,896]{2,1,0:T(8,128)(2,1)}, bf16[3,16,896]{2,1,0:T(8,128)(2,1)S(1)}, u32[]{:S(2)}, u32[]{:S(2)}) collective-permute-start(bf16[3,16,896]{2,1,0:T(8,128)(2,1)} %get-tuple-element.19), channel_id=1, source_target_pairs={{0,16},{16,32},{32,48},{48,64},{64,80},{80,96},{96,112},{112,128},... | collective-permute-start | bytes 258056 | tf_op jit(solution)/shard_map/ppermute | solution.py:24
  14.7 2.2 %collective-permute-start.1 = (bf16[3,16,896]{2,1,0:T(8,128)(2,1)}, bf16[3,16,896]{2,1,0:T(8,128)(2,1)S(1)}, u32[]{:S(2)}, u32[]{:S(2)}) collective-permute-start(bf16[3,16,896]{2,1,0:T(8,128)(2,1)} %get-tuple-element.20), channel_id=1, source_target_pairs={{16,0},{32,16},{48,32},{64,48},{80,64},{96,80},{112,96},{128,112},... | collective-permute-start | bytes 258056 | tf_op jit(solution)/shard_map/ppermute | solution.py:24
  16.9 4.7 %collective-permute-start.2 = (bf16[3,16,896]{2,1,0:T(8,128)(2,1)}, bf16[3,16,896]{2,1,0:T(8,128)(2,1)S(1)}, u32[]{:S(2)}, u32[]{:S(2)}) collective-permute-start(bf16[3,16,896]{2,1,0:T(8,128)(2,1)} %get-tuple-element.21), channel_id=1, source_target_pairs={{0,32},{16,48},{32,64},{48,80},{64,96},{80,112},{96,128},{112,144}... | collective-permute-start | bytes 258056 | tf_op jit(solution)/shard_map/ppermute | solution.py:24
  21.7 2.0 %collective-permute-start.3 = (bf16[3,16,896]{2,1,0:T(8,128)(2,1)}, bf16[3,16,896]{2,1,0:T(8,128)(2,1)S(1)}, u32[]{:S(2)}, u32[]{:S(2)}) collective-permute-start(bf16[3,16,896]{2,1,0:T(8,128)(2,1)} %get-tuple-element.22), channel_id=1, source_target_pairs={{32,0},{48,16},{64,32},{80,48},{96,64},{112,80},{128,96},{144,112}... | collective-permute-start | bytes 258056 | tf_op jit(solution)/shard_map/ppermute | solution.py:24
  24.3 0.0 collective-permute-done.r0
  24.3 0.0 copy-start.12
  24.3 0.0 collective-permute-done.1.r1
  24.4 0.0 copy-start.13
  24.4 0.5 collective-permute-done.2.r2
  24.9 0.0 copy-start.14
  24.9 7.3 %collective-permute-done.3.r3 = bf16[3,16,896]{2,1,0:T(8,128)(2,1)S(1)} collective-permute-done((bf16[3,16,896]{2,1,0:T(8,128)(2,1)}, bf16[3,16,896]{2,1,0:T(8,128)(2,1)S(1)}, u32[]{:S(2)}, u32[]{:S(2)}) %collective-permute-start.3) | collective-permute-done | bytes 86048 | tf_op jit(solution)/shard_map/ppermute | solution.py:24
  32.2 0.0 copy-start.15
  32.2 0.0 copy-done.12
  32.2 0.0 copy-done.13
  32.2 0.0 copy-done.14
  32.2 0.6 copy-done.15
  32.8 5.6 %forward.1 = (bf16[448,1792]{1,0:T(8,128)(2,1)}, bf16[128,896]{1,0:T(8,128)(2,1)}, bf16[448,128]{1,0:T(8,128)(2,1)}, bf16[3,128,896]{2,1,0:T(8,128)(2,1)}, f32[8,128,128]{2,1,0:T(8,128)}) custom-call(s32[3,4,64]{2,1,0:T(4,128)} %bitcast.20, s32[1,1]{1,0:T(1,128)S(6)} %copy.10.kept, s32[1,128]{1,0:T(1,128)} %bitcast.32, bf16[3,128,896]{2,1,0:T(8,128)(2,1)} %bitcast.28, ...), custom_call_target="tpu_custom_call" | custom-call | flops 1 | bytes 1 | tf_op jit(solution)/shard_map/forward/pallas_call | solution.py:274
  38.5 1.9 %collective-permute-start.4 = (bf16[448,1792]{1,0:T(8,128)(2,1)}, bf16[448,1792]{1,0:T(8,128)(2,1)S(1)}, u32[]{:S(2)}, u32[]{:S(2)}) collective-permute-start(bf16[448,1792]{1,0:T(8,128)(2,1)} %get-tuple-element.26), channel_id=1, source_target_pairs={{0,1},{1,0},{2,3},{3,2},{4,5},{5,4},{6,7},{7,6},{8,9},{9,8},{10,11... | collective-permute-start | bytes 4816904 | tf_op jit(solution)/shard_map/ppermute | solution.py:299
  40.4 3.6 %collective-permute-done.4.arrived = bf16[448,1792]{1,0:T(8,128)(2,1)S(1)} collective-permute-done((bf16[448,1792]{1,0:T(8,128)(2,1)}, bf16[448,1792]{1,0:T(8,128)(2,1)S(1)}, u32[]{:S(2)}, u32[]{:S(2)}) %collective-permute-start.4) | collective-permute-done | bytes 1605664 | tf_op jit(solution)/shard_map/ppermute | solution.py:299
  44.0 0.0 copy-done.2
  44.0 0.0 copy-start.9
  44.0 0.9 copy-done.9
  44.9 1.9 %fold.1 = bf16[448,1792]{1,0:T(8,128)(2,1)} custom-call(bf16[448,128]{1,0:T(8,128)(2,1)S(1)} %copy-done.9, bf16[128,1792]{1,0:T(8,128)(2,1)S(1)} %bitcast.17, bf16[448,1792]{1,0:T(8,128)(2,1)S(1)} %collective-permute-done.4.arrived), custom_call_target="tpu_custom_call" | custom-call | tf_op jit(solution)/shard_map/fold/pallas_call | solution.py:300
  46.8 0.0 copy-start.10
  46.8 0.0 copy-start.11
  46.8 0.0 reduce-scatter.2.cloned.1.call-update
  46.8 20.9 %all-gather.2.cloned.1.call-done.w = bf16[896,1792]{1,0:T(8,128)(2,1)} async-done(((bf16[56,1792]{1,0:T(8,128)(2,1)}), bf16[896,1792]{1,0:T(8,128)(2,1)}) %all-gather.2.cloned.1.call-update) | async-done | bytes 3211280 | tf_op jit(solution)/shard_map/all_gather | solution.py:258
  67.8 0.0 copy-done.10
  67.8 0.0 copy-done.11
  67.8 0.0 copy-start
  67.8 1.9 %copy-done = bf16[896,1792]{1,0:T(8,128)(2,1)S(1)} copy-done((bf16[896,1792]{1,0:T(8,128)(2,1)S(1)}, bf16[896,1792]{1,0:T(8,128)(2,1)}, u32[]{:S(2)}) %copy-start) | copy-done | bytes 3211288
  69.7 0.0 copy-start.3
  69.7 1.0 copy-done.3
  70.7 0.0 copy-start.6
  70.7 1.1 copy-done.6
  71.8 0.0 copy-start.7
  71.8 1.0 copy-done.7
  72.8 0.0 copy-start.1
  72.8 0.0 copy-start.8
  72.8 5.1 %backward.1 = (bf16[3,128,896]{2,1,0:T(8,128)(2,1)S(1)}, bf16[3,16,896]{2,1,0:T(8,128)(2,1)}, bf16[3,16,896]{2,1,0:T(8,128)(2,1)}, bf16[3,16,896]{2,1,0:T(8,128)(2,1)}, bf16[3,16,896]{2,1,0:T(8,128)(2,1)}) custom-call(s32[3,4,64]{2,1,0:T(4,128)S(1)} %bitcast.21, s32[1,1]{1,0:T(1,128)S(6)} %copy.10.kept, bf16[896,1792]{1,0:T(8,128)(2,1)S(1)} %copy-done, ...), custom_call_target="tpu_custom_call" | custom-call | tf_op jit(solution)/shard_map/backward/pallas_call | solution.py:314
  77.9 0.0 copy-start.4
  77.9 0.8 copy-done.4
  78.8 3.3 %collective-permute-start.5 = (bf16[3,16,896]{2,1,0:T(8,128)(2,1)}, bf16[3,16,896]{2,1,0:T(8,128)(2,1)S(1)}, u32[]{:S(2)}, u32[]{:S(2)}) collective-permute-start(bf16[3,16,896]{2,1,0:T(8,128)(2,1)} %get-tuple-element.30), channel_id=1, source_target_pairs={{16,0},{32,16},{48,32},{64,48},{80,64},{96,80},{112,96},{128,112},... | collective-permute-start | bytes 258056 | tf_op jit(solution)/shard_map/ppermute | solution.py:24
  82.1 4.6 %collective-permute-start.6 = (bf16[3,16,896]{2,1,0:T(8,128)(2,1)}, bf16[3,16,896]{2,1,0:T(8,128)(2,1)}, u32[]{:S(2)}, u32[]{:S(2)}) collective-permute-start(bf16[3,16,896]{2,1,0:T(8,128)(2,1)} %get-tuple-element.31), channel_id=1, source_target_pairs={{0,16},{16,32},{32,48},{48,64},{64,80},{80,96},{96,112},{112,128},... | collective-permute-start | bytes 258056 | tf_op jit(solution)/shard_map/ppermute | solution.py:24
  86.7 2.1 %collective-permute-start.7 = (bf16[3,16,896]{2,1,0:T(8,128)(2,1)}, bf16[3,16,896]{2,1,0:T(8,128)(2,1)}, u32[]{:S(2)}, u32[]{:S(2)}) collective-permute-start(bf16[3,16,896]{2,1,0:T(8,128)(2,1)} %get-tuple-element.32), channel_id=1, source_target_pairs={{32,0},{48,16},{64,32},{80,48},{96,64},{112,80},{128,96},{144,112}... | collective-permute-start | bytes 258056 | tf_op jit(solution)/shard_map/ppermute | solution.py:24
  88.8 6.8 %collective-permute-start.8 = (bf16[3,16,896]{2,1,0:T(8,128)(2,1)}, bf16[3,16,896]{2,1,0:T(8,128)(2,1)}, u32[]{:S(2)}, u32[]{:S(2)}) collective-permute-start(bf16[3,16,896]{2,1,0:T(8,128)(2,1)} %get-tuple-element.33), channel_id=1, source_target_pairs={{0,32},{16,48},{32,64},{48,80},{64,96},{80,112},{96,128},{112,144}... | collective-permute-start | bytes 258056 | tf_op jit(solution)/shard_map/ppermute | solution.py:24
  95.6 4.5 %reduce-scatter.2.cloned.1.call-done.narrow = bf16[56,1792]{1,0:T(8,128)(2,1)} async-done(((bf16[448,1792]{1,0:T(8,128)(2,1)}), bf16[56,1792]{1,0:T(8,128)(2,1)}) %reduce-scatter.2.cloned.1.call-update) | async-done | bytes 200720 | tf_op jit(solution)/shard_map/reduce_scatter | solution.py:310
  100.1 1.7 %widen.1 = f32[56,1792]{1,0:T(8,128)} custom-call(bf16[56,1792]{1,0:T(8,128)(2,1)} %reduce-scatter.2.cloned.1.call-done.narrow), custom_call_target="tpu_custom_call" | custom-call | tf_op jit(solution)/shard_map/widen/pallas_call | solution.py:351
  101.8 0.0 copy-done.1
  101.8 0.0 copy-done.8
  101.8 0.0 copy-start.5
  101.8 3.6 %project.1 = bf16[128,1792]{1,0:T(8,128)(2,1)} custom-call(bf16[128,896]{1,0:T(8,128)(2,1)S(1)} %copy-done.8, bf16[896,1792]{1,0:T(8,128)(2,1)S(1)} %copy-done.1), custom_call_target="tpu_custom_call" | custom-call | tf_op jit(solution)/shard_map/project/pallas_call | solution.py:332
  105.4 0.0 collective-permute-done.5.r0
  105.4 0.0 collective-permute-done.6.r1
  105.4 0.0 collective-permute-done.7.r2
  105.4 0.0 collective-permute-done.8.r3
  105.4 0.0 copy-done.5
  105.4 2.6 %restore.1 = bf16[3,128,896]{2,1,0:T(8,128)(2,1)} custom-call(s32[3,4,64]{2,1,0:T(4,128)S(1)} %bitcast.22, bf16[3,128,896]{2,1,0:T(8,128)(2,1)S(1)} %copy-done.5, bf16[3,7,128]{2,1,0:T(8,128)(2,1)S(1)} %bitcast.26, bf16[3,16,896]{2,1,0:T(8,128)(2,1)S(1)} %collective-permute-done.5.r0, bf16[3,16,896]{2,1,0:T(8,128)(2,1)} %collective-permute-done.6.r1, ...), custom_call_target="tpu_custom_call" | custom-call | tf_op jit(solution)/shard_map/restore/pallas_call | solution.py:343
Async XLA Ops:
  8.0 36.0 %copy-start.2 = (bf16[1,1,128,1792]{3,2,1,0:T(8,128)(2,1)S(1)}, bf16[1,1,128,1792]{3,2,1,0:T(8,128)(2,1)}, u32[]{:S(2)}) copy-start(bf16[1,1,128,1792]{3,2,1,0:T(8,128)(2,1)} %param.13) | copy-start | bytes 1376260
  8.0 59.7 %all-gather.2.cloned.1.call-start = ((), (), s32[]{:S(2)}) async-start(), calls=%async_computation.1 | async-start | bytes 3411968 | tf_op jit(solution)/shard_map/all_gather | solution.py:258
  8.7 91.3 %reduce-scatter.2.cloned.1.call-start = ((), (), s32[]{:S(2)}) async-start(), calls=%async_computation.2 | async-start | bytes 1806336 | tf_op jit(solution)/shard_map/reduce_scatter | solution.py:310
  11.1 13.3 %collective-permute-start = (bf16[3,16,896]{2,1,0:T(8,128)(2,1)}, bf16[3,16,896]{2,1,0:T(8,128)(2,1)S(1)}, u32[]{:S(2)}, u32[]{:S(2)}) collective-permute-start(bf16[3,16,896]{2,1,0:T(8,128)(2,1)} %get-tuple-element.19), channel_id=1, source_target_pairs={{0,16},{16,32},{32,48},{48,64},{64,80},{80,96},{96,112},{112,128},... | collective-permute-start | bytes 258056 | tf_op jit(solution)/shard_map/ppermute | solution.py:24
  14.7 9.7 %collective-permute-start.1 = (bf16[3,16,896]{2,1,0:T(8,128)(2,1)}, bf16[3,16,896]{2,1,0:T(8,128)(2,1)S(1)}, u32[]{:S(2)}, u32[]{:S(2)}) collective-permute-start(bf16[3,16,896]{2,1,0:T(8,128)(2,1)} %get-tuple-element.20), channel_id=1, source_target_pairs={{16,0},{32,16},{48,32},{64,48},{80,64},{96,80},{112,96},{128,112},... | collective-permute-start | bytes 258056 | tf_op jit(solution)/shard_map/ppermute | solution.py:24
  16.9 7.9 %collective-permute-start.2 = (bf16[3,16,896]{2,1,0:T(8,128)(2,1)}, bf16[3,16,896]{2,1,0:T(8,128)(2,1)S(1)}, u32[]{:S(2)}, u32[]{:S(2)}) collective-permute-start(bf16[3,16,896]{2,1,0:T(8,128)(2,1)} %get-tuple-element.21), channel_id=1, source_target_pairs={{0,32},{16,48},{32,64},{48,80},{64,96},{80,112},{96,128},{112,144}... | collective-permute-start | bytes 258056 | tf_op jit(solution)/shard_map/ppermute | solution.py:24
  21.7 10.5 %collective-permute-start.3 = (bf16[3,16,896]{2,1,0:T(8,128)(2,1)}, bf16[3,16,896]{2,1,0:T(8,128)(2,1)S(1)}, u32[]{:S(2)}, u32[]{:S(2)}) collective-permute-start(bf16[3,16,896]{2,1,0:T(8,128)(2,1)} %get-tuple-element.22), channel_id=1, source_target_pairs={{32,0},{48,16},{64,32},{80,48},{96,64},{112,80},{128,96},{144,112}... | collective-permute-start | bytes 258056 | tf_op jit(solution)/shard_map/ppermute | solution.py:24
  24.3 7.9 %copy-start.12 = (bf16[3,16,896]{2,1,0:T(8,128)(2,1)}, bf16[3,16,896]{2,1,0:T(8,128)(2,1)S(1)}, u32[]{:S(2)}) copy-start(bf16[3,16,896]{2,1,0:T(8,128)(2,1)S(1)} %collective-permute-done.r0) | copy-start | bytes 258052
  24.4 7.8 %copy-start.13 = (bf16[3,16,896]{2,1,0:T(8,128)(2,1)}, bf16[3,16,896]{2,1,0:T(8,128)(2,1)S(1)}, u32[]{:S(2)}) copy-start(bf16[3,16,896]{2,1,0:T(8,128)(2,1)S(1)} %collective-permute-done.1.r1) | copy-start | bytes 258052
  24.9 7.3 %copy-start.14 = (bf16[3,16,896]{2,1,0:T(8,128)(2,1)}, bf16[3,16,896]{2,1,0:T(8,128)(2,1)S(1)}, u32[]{:S(2)}) copy-start(bf16[3,16,896]{2,1,0:T(8,128)(2,1)S(1)} %collective-permute-done.2.r2) | copy-start | bytes 258052
  32.2 0.6 copy-start.15
  38.5 5.5 %collective-permute-start.4 = (bf16[448,1792]{1,0:T(8,128)(2,1)}, bf16[448,1792]{1,0:T(8,128)(2,1)S(1)}, u32[]{:S(2)}, u32[]{:S(2)}) collective-permute-start(bf16[448,1792]{1,0:T(8,128)(2,1)} %get-tuple-element.26), channel_id=1, source_target_pairs={{0,1},{1,0},{2,3},{3,2},{4,5},{5,4},{6,7},{7,6},{8,9},{9,8},{10,11... | collective-permute-start | bytes 4816904 | tf_op jit(solution)/shard_map/ppermute | solution.py:299
  44.0 0.9 copy-start.9
  46.8 21.0 %copy-start.10 = (s32[64,1,4,3]{0,2,3,1:T(4,128)S(1)}, s32[64,1,4,3]{0,2,3,1:T(4,128)}, u32[]{:S(2)}) copy-start(s32[64,1,4,3]{0,2,3,1:T(4,128)} %param.11) | copy-start | bytes 9220
  46.8 21.0 %copy-start.11 = (bf16[1,1,128,3,7]{2,4,3,1,0:T(8,128)(2,1)S(1)}, bf16[1,1,128,3,7]{2,4,3,1,0:T(8,128)(2,1)}, u32[]{:S(2)}) copy-start(bf16[1,1,128,3,7]{2,4,3,1,0:T(8,128)(2,1)} %param.8) | copy-start | bytes 16132
  67.8 1.9 %copy-start = (bf16[896,1792]{1,0:T(8,128)(2,1)S(1)}, bf16[896,1792]{1,0:T(8,128)(2,1)}, u32[]{:S(2)}) copy-start(bf16[896,1792]{1,0:T(8,128)(2,1)} %all-gather.2.cloned.1.call-done.w) | copy-start | bytes 9633796
  69.7 1.0 copy-start.3
  70.7 1.1 copy-start.6
  71.8 1.0 copy-start.7
  72.8 28.9 %copy-start.1 = (bf16[896,1792]{1,0:T(8,128)(2,1)S(1)}, bf16[896,1792]{1,0:T(8,128)(2,1)}, u32[]{:S(2)}) copy-start(bf16[896,1792]{1,0:T(8,128)(2,1)} %all-gather.2.cloned.1.call-done.w) | copy-start | bytes 9633796
  72.8 28.9 %copy-start.8 = (bf16[128,896]{1,0:T(8,128)(2,1)S(1)}, bf16[128,896]{1,0:T(8,128)(2,1)}, u32[]{:S(2)}) copy-start(bf16[128,896]{1,0:T(8,128)(2,1)} %get-tuple-element.23.context) | copy-start | bytes 688132
  77.9 0.8 copy-start.4
  78.8 26.6 %collective-permute-start.5 = (bf16[3,16,896]{2,1,0:T(8,128)(2,1)}, bf16[3,16,896]{2,1,0:T(8,128)(2,1)S(1)}, u32[]{:S(2)}, u32[]{:S(2)}) collective-permute-start(bf16[3,16,896]{2,1,0:T(8,128)(2,1)} %get-tuple-element.30), channel_id=1, source_target_pairs={{16,0},{32,16},{48,32},{64,48},{80,64},{96,80},{112,96},{128,112},... | collective-permute-start | bytes 258056 | tf_op jit(solution)/shard_map/ppermute | solution.py:24
  82.1 23.3 %collective-permute-start.6 = (bf16[3,16,896]{2,1,0:T(8,128)(2,1)}, bf16[3,16,896]{2,1,0:T(8,128)(2,1)}, u32[]{:S(2)}, u32[]{:S(2)}) collective-permute-start(bf16[3,16,896]{2,1,0:T(8,128)(2,1)} %get-tuple-element.31), channel_id=1, source_target_pairs={{0,16},{16,32},{32,48},{48,64},{64,80},{80,96},{96,112},{112,128},... | collective-permute-start | bytes 258056 | tf_op jit(solution)/shard_map/ppermute | solution.py:24
  86.7 18.7 %collective-permute-start.7 = (bf16[3,16,896]{2,1,0:T(8,128)(2,1)}, bf16[3,16,896]{2,1,0:T(8,128)(2,1)}, u32[]{:S(2)}, u32[]{:S(2)}) collective-permute-start(bf16[3,16,896]{2,1,0:T(8,128)(2,1)} %get-tuple-element.32), channel_id=1, source_target_pairs={{32,0},{48,16},{64,32},{80,48},{96,64},{112,80},{128,96},{144,112}... | collective-permute-start | bytes 258056 | tf_op jit(solution)/shard_map/ppermute | solution.py:24
  88.8 16.6 %collective-permute-start.8 = (bf16[3,16,896]{2,1,0:T(8,128)(2,1)}, bf16[3,16,896]{2,1,0:T(8,128)(2,1)}, u32[]{:S(2)}, u32[]{:S(2)}) collective-permute-start(bf16[3,16,896]{2,1,0:T(8,128)(2,1)} %get-tuple-element.33), channel_id=1, source_target_pairs={{0,32},{16,48},{32,64},{48,80},{64,96},{80,112},{96,128},{112,144}... | collective-permute-start | bytes 258056 | tf_op jit(solution)/shard_map/ppermute | solution.py:24
  101.8 3.6 %copy-start.5 = (bf16[3,128,896]{2,1,0:T(8,128)(2,1)S(1)}, bf16[3,128,896]{2,1,0:T(8,128)(2,1)}, u32[]{:S(2)}) copy-start(bf16[3,128,896]{2,1,0:T(8,128)(2,1)} %copy-done.4) | copy-start | bytes 2064388
Sparse Core Ops, SparseCore 0:
  11.5 56.1 all-gather.1
Sparse Core Ops, SparseCore 1:
  46.9 53.1 reduce-scatter.1

commit v5 on v4

--- a/solution.py
+++ b/solution.py
@@ -165,7 +165,7 @@
     folded[...] = (own.astype(F32) + arrived[...].astype(F32)).astype(BF16)
 
 
-def widen_kernel(narrow, wide):
+def widen_kernel(_, narrow, wide):
     wide[...] = narrow[...].astype(F32)
 
 
@@ -325,7 +325,7 @@
         ],
         out_specs=[codes_spec] + [piece_spec] * 4,
         scratch_shapes=[pltpu.VMEM((rows, width), BF16)],
-        compiler_params=light,
+        compiler_params=params,
         name="backward",
     )(table, kept_rows, w_full, grad_out, balanced, probs, scales)
     chunk = 256
@@ -335,7 +335,7 @@
         out_shape=jax.ShapeDtypeStruct((rows, depth), BF16),
         in_specs=[whole((rows, width)), pl.BlockSpec((width, chunk), lambda n: (0, n))],
         out_specs=pl.BlockSpec((rows, chunk), lambda n: (0, n)),
-        compiler_params=light,
+        compiler_params=params,
         name="project",
     )(context, w_full)
     returned = [shifted(back[d], "dp", -OFFSETS[d]) for d in range(4)]
@@ -348,12 +348,15 @@
         compiler_params=light,
         name="restore",
     )(table, home, scales, *returned)
+    gate, grad_codes, output = lax.optimization_barrier((kept_rows, grad_codes, output))
     grad_w = pl.pallas_call(
         widen_kernel,
         out_shape=jax.ShapeDtypeStruct(w_out.shape, F32),
+        in_specs=[smem, whole(w_out.shape)],
+        out_specs=whole(w_out.shape),
         compiler_params=params,
         name="widen",
-    )(scattered)
+    )(gate, scattered)
     grad_codes = jnp.transpose(grad_codes, (1, 0, 2))
     return (output[None, None], grad_codes[None, None], grad_w[None])
 

time: 118 us -> 120 us (1.017)
  local copies, waits for them, and re-layouts: 7.49 us -> 1.56 us
  Pallas kernels: 22.8 us -> 26.8 us
  waiting for transfers between devices: 37.6 us -> 41.6 us
    unnamed x32 -> x18, local copies, waits for them, and re-layouts: 7.49 us -> 1.56 us
    reduce_scatter x1, waiting for transfers between devices: 4.48 us -> 8.56 us  [local(): lax.psum_scatter(folded, 'fsdp', scatter_dimension=0, tiled=True, axis_in...]
    pallas_call x1, Pallas kernels: 3.6 us -> 5.96 us  [local(): pl.pallas_call(output_kernel, grid=(depth // chunk,), out_shape=jax.Shape...]
    pallas_call x1, Pallas kernels: 5.07 us -> 7.04 us  [local(): pl.pallas_call(functools.partial(backward_kernel, group), out_shape=[jax....]
  transfers between devices with their start and end apart: 11 -> 11, of which waited for: 5 -> 5; matrix products, arithmetic and copies ran while one was open for 0% -> 0% of each run, Pallas kernels for 17% -> 21%
where the time goes in v5:
time: 120 us; the launch traced here: 118 us
  waiting for transfers between devices  41.6 us (35%)
  starting transfers between devices  31.3 us (26%)
  Pallas kernels  26.8 us (22%)
  between operations  16.3 us (14%)
  local copies, waits for them, and re-layouts  1.56 us (1%)
    ppermute x8, starting transfers between devices, shifted(): return lax.ppermute(block, axis, route)  29.4 us
    all_gather x1, waiting for transfers between devices, local(): w_full = lax.all_gather(w_out, 'fsdp', axis=0, tiled=True)  20.9 us
    reduce_scatter x1, waiting for transfers between devices, local(): lax.psum_scatter(folded, 'fsdp', scatter_dimension=0, tiled=True, axis_in...  8.56 us
    ppermute x8, waiting for transfers between devices, shifted(): return lax.ppermute(block, axis, route)  7.83 us
    pallas_call x1, Pallas kernels, local(): pl.pallas_call(functools.partial(backward_kernel, group), out_shape=[jax....  7.04 us
    pallas_call x1, Pallas kernels, local(): pl.pallas_call(output_kernel, grid=(depth // chunk,), out_shape=jax.Shape...  5.96 us
    pallas_call x1, Pallas kernels, local(): pl.pallas_call(functools.partial(forward_kernel, group), grid=(2,), out_s...  5.66 us
    ppermute x1, waiting for transfers between devices, local(): arrived = lax.ppermute(term_other, 'fsdp', swap)  3.63 us
  transfers between devices with their start and end apart: 11, of which 5 were waited for; matrix products, arithmetic and copies ran while one was open for 0% of the time, Pallas kernels for 21%

profile of v5, /device:TPU:112, one launch (start us, length us, event | category | flops | bytes accessed | tf_op | source)
XLA Modules:
  0.0 117.6 jit_solution(18315937391040630902)
XLA Ops:
  8.0 0.0 copy-start
  8.0 0.0 all-gather.2.cloned.1.call-start
  8.1 0.7 all-gather.2.cloned.1.call-update
  8.7 0.0 reduce-scatter.2.cloned.1.call-start
  8.8 2.3 %pack.1 = (bf16[3,16,896]{2,1,0:T(8,128)(2,1)}, bf16[3,16,896]{2,1,0:T(8,128)(2,1)}, bf16[3,16,896]{2,1,0:T(8,128)(2,1)}, bf16[3,16,896]{2,1,0:T(8,128)(2,1)}) custom-call(s32[3,4,64]{2,1,0:T(4,128)} %bitcast.19, bf16[3,128,896]{2,1,0:T(8,128)(2,1)} %bitcast.27, bf16[3,7,128]{2,1,0:T(8,128)(2,1)} %bitcast.23), custom_call_target="tpu_custom_call" | custom-call | flops 1 | bytes 1 | tf_op jit(solution)/shard_map/pack/pallas_call | solution.py:260
  11.1 3.6 %collective-permute-start = (bf16[3,16,896]{2,1,0:T(8,128)(2,1)}, bf16[3,16,896]{2,1,0:T(8,128)(2,1)S(1)}, u32[]{:S(2)}, u32[]{:S(2)}) collective-permute-start(bf16[3,16,896]{2,1,0:T(8,128)(2,1)} %get-tuple-element.22), channel_id=1, source_target_pairs={{0,16},{16,32},{32,48},{48,64},{64,80},{80,96},{96,112},{112,128},... | collective-permute-start | bytes 258056 | tf_op jit(solution)/shard_map/ppermute | solution.py:24
  14.7 2.2 %collective-permute-start.1 = (bf16[3,16,896]{2,1,0:T(8,128)(2,1)}, bf16[3,16,896]{2,1,0:T(8,128)(2,1)S(1)}, u32[]{:S(2)}, u32[]{:S(2)}) collective-permute-start(bf16[3,16,896]{2,1,0:T(8,128)(2,1)} %get-tuple-element.23), channel_id=1, source_target_pairs={{16,0},{32,16},{48,32},{64,48},{80,64},{96,80},{112,96},{128,112},... | collective-permute-start | bytes 258056 | tf_op jit(solution)/shard_map/ppermute | solution.py:24
  16.9 4.7 %collective-permute-start.2 = (bf16[3,16,896]{2,1,0:T(8,128)(2,1)}, bf16[3,16,896]{2,1,0:T(8,128)(2,1)S(1)}, u32[]{:S(2)}, u32[]{:S(2)}) collective-permute-start(bf16[3,16,896]{2,1,0:T(8,128)(2,1)} %get-tuple-element.24), channel_id=1, source_target_pairs={{0,32},{16,48},{32,64},{48,80},{64,96},{80,112},{96,128},{112,144}... | collective-permute-start | bytes 258056 | tf_op jit(solution)/shard_map/ppermute | solution.py:24
  21.7 2.0 %collective-permute-start.3 = (bf16[3,16,896]{2,1,0:T(8,128)(2,1)}, bf16[3,16,896]{2,1,0:T(8,128)(2,1)S(1)}, u32[]{:S(2)}, u32[]{:S(2)}) collective-permute-start(bf16[3,16,896]{2,1,0:T(8,128)(2,1)} %get-tuple-element.25), channel_id=1, source_target_pairs={{32,0},{48,16},{64,32},{80,48},{96,64},{112,80},{128,96},{144,112}... | collective-permute-start | bytes 258056 | tf_op jit(solution)/shard_map/ppermute | solution.py:24
  24.3 0.0 collective-permute-done.r0
  24.3 0.0 copy-start.5
  24.4 0.0 collective-permute-done.1.r1
  24.4 0.0 copy-start.6
  24.4 0.5 collective-permute-done.2.r2
  24.9 0.0 copy-start.7
  24.9 7.3 %collective-permute-done.3.r3 = bf16[3,16,896]{2,1,0:T(8,128)(2,1)S(1)} collective-permute-done((bf16[3,16,896]{2,1,0:T(8,128)(2,1)}, bf16[3,16,896]{2,1,0:T(8,128)(2,1)S(1)}, u32[]{:S(2)}, u32[]{:S(2)}) %collective-permute-start.3) | collective-permute-done | bytes 86048 | tf_op jit(solution)/shard_map/ppermute | solution.py:24
  32.2 0.0 copy-start.8
  32.2 0.0 copy-done.5
  32.2 0.0 copy-done.6
  32.2 0.0 copy-done.7
  32.2 0.6 copy-done.8
  32.8 5.7 %forward.1 = (bf16[448,1792]{1,0:T(8,128)(2,1)}, bf16[128,896]{1,0:T(8,128)(2,1)}, bf16[448,128]{1,0:T(8,128)(2,1)}, bf16[3,128,896]{2,1,0:T(8,128)(2,1)}, f32[8,128,128]{2,1,0:T(8,128)}) custom-call(s32[3,4,64]{2,1,0:T(4,128)} %bitcast.20, s32[1,1]{1,0:T(1,128)S(6)} %copy.10.kept._, s32[1,128]{1,0:T(1,128)} %bitcast.32, bf16[3,128,896]{2,1,0:T(8,128)(2,1)} %bitcast.28, ...), custom_call_target="tpu_custom_call" | custom-call | flops 1 | bytes 1 | tf_op jit(solution)/shard_map/forward/pallas_call | solution.py:274
  38.5 1.9 %collective-permute-start.4 = (bf16[448,1792]{1,0:T(8,128)(2,1)}, bf16[448,1792]{1,0:T(8,128)(2,1)S(1)}, u32[]{:S(2)}, u32[]{:S(2)}) collective-permute-start(bf16[448,1792]{1,0:T(8,128)(2,1)} %get-tuple-element.28), channel_id=1, source_target_pairs={{0,1},{1,0},{2,3},{3,2},{4,5},{5,4},{6,7},{7,6},{8,9},{9,8},{10,11... | collective-permute-start | bytes 4816904 | tf_op jit(solution)/shard_map/ppermute | solution.py:299
  40.4 3.6 %collective-permute-done.4.arrived = bf16[448,1792]{1,0:T(8,128)(2,1)S(1)} collective-permute-done((bf16[448,1792]{1,0:T(8,128)(2,1)}, bf16[448,1792]{1,0:T(8,128)(2,1)S(1)}, u32[]{:S(2)}, u32[]{:S(2)}) %collective-permute-start.4) | collective-permute-done | bytes 1605664 | tf_op jit(solution)/shard_map/ppermute | solution.py:299
  44.0 0.0 copy-done
  44.1 0.0 copy-start.2
  44.1 0.9 copy-done.2
  45.0 1.9 %fold.1 = bf16[448,1792]{1,0:T(8,128)(2,1)} custom-call(bf16[448,128]{1,0:T(8,128)(2,1)S(1)} %copy-done.2, bf16[128,1792]{1,0:T(8,128)(2,1)S(1)} %bitcast.18, bf16[448,1792]{1,0:T(8,128)(2,1)S(1)} %collective-permute-done.4.arrived), custom_call_target="tpu_custom_call" | custom-call | tf_op jit(solution)/shard_map/fold/pallas_call | solution.py:300
  46.8 0.0 reduce-scatter.2.cloned.1.call-update
  46.9 20.9 %all-gather.2.cloned.1.call-done.w = bf16[896,1792]{1,0:T(8,128)(2,1)} async-done(((bf16[56,1792]{1,0:T(8,128)(2,1)}), bf16[896,1792]{1,0:T(8,128)(2,1)}) %all-gather.2.cloned.1.call-update) | async-done | bytes 3211280 | tf_op jit(solution)/shard_map/all_gather | solution.py:258
  67.8 7.0 %backward.1 = (bf16[3,128,896]{2,1,0:T(8,128)(2,1)}, bf16[3,16,896]{2,1,0:T(8,128)(2,1)}, bf16[3,16,896]{2,1,0:T(8,128)(2,1)}, bf16[3,16,896]{2,1,0:T(8,128)(2,1)}, bf16[3,16,896]{2,1,0:T(8,128)(2,1)}) custom-call(s32[3,4,64]{2,1,0:T(4,128)} %bitcast.21, s32[1,1]{1,0:T(1,128)S(6)} %copy.10.kept._, bf16[896,1792]{1,0:T(8,128)(2,1)} %all-gather.2.cloned.1.call-done.w, ...), custom_call_target="tpu_custom_call" | custom-call | tf_op jit(solution)/shard_map/backward/pallas_call | solution.py:314
  74.8 3.3 %collective-permute-start.5 = (bf16[3,16,896]{2,1,0:T(8,128)(2,1)}, bf16[3,16,896]{2,1,0:T(8,128)(2,1)S(1)}, u32[]{:S(2)}, u32[]{:S(2)}) collective-permute-start(bf16[3,16,896]{2,1,0:T(8,128)(2,1)} %get-tuple-element.32), channel_id=1, source_target_pairs={{16,0},{32,16},{48,32},{64,48},{80,64},{96,80},{112,96},{128,112},... | collective-permute-start | bytes 258056 | tf_op jit(solution)/shard_map/ppermute | solution.py:24
  78.1 4.6 %collective-permute-start.6 = (bf16[3,16,896]{2,1,0:T(8,128)(2,1)}, bf16[3,16,896]{2,1,0:T(8,128)(2,1)S(1)}, u32[]{:S(2)}, u32[]{:S(2)}) collective-permute-start(bf16[3,16,896]{2,1,0:T(8,128)(2,1)} %get-tuple-element.33), channel_id=1, source_target_pairs={{0,16},{16,32},{32,48},{48,64},{64,80},{80,96},{96,112},{112,128},... | collective-permute-start | bytes 258056 | tf_op jit(solution)/shard_map/ppermute | solution.py:24
  82.7 2.1 %collective-permute-start.7 = (bf16[3,16,896]{2,1,0:T(8,128)(2,1)}, bf16[3,16,896]{2,1,0:T(8,128)(2,1)S(1)}, u32[]{:S(2)}, u32[]{:S(2)}) collective-permute-start(bf16[3,16,896]{2,1,0:T(8,128)(2,1)} %get-tuple-element.34), channel_id=1, source_target_pairs={{32,0},{48,16},{64,32},{80,48},{96,64},{112,80},{128,96},{144,112}... | collective-permute-start | bytes 258056 | tf_op jit(solution)/shard_map/ppermute | solution.py:24
  84.8 6.8 %collective-permute-start.8 = (bf16[3,16,896]{2,1,0:T(8,128)(2,1)}, bf16[3,16,896]{2,1,0:T(8,128)(2,1)S(1)}, u32[]{:S(2)}, u32[]{:S(2)}) collective-permute-start(bf16[3,16,896]{2,1,0:T(8,128)(2,1)} %get-tuple-element.35), channel_id=1, source_target_pairs={{0,32},{16,48},{32,64},{48,80},{64,96},{80,112},{96,128},{112,144}... | collective-permute-start | bytes 258056 | tf_op jit(solution)/shard_map/ppermute | solution.py:24
  91.6 8.6 %reduce-scatter.2.cloned.1.call-done.narrow = bf16[56,1792]{1,0:T(8,128)(2,1)} async-done(((bf16[448,1792]{1,0:T(8,128)(2,1)}), bf16[56,1792]{1,0:T(8,128)(2,1)}) %reduce-scatter.2.cloned.1.call-update) | async-done | bytes 200720 | tf_op jit(solution)/shard_map/reduce_scatter | solution.py:310
  100.2 1.7 %widen.1 = f32[56,1792]{1,0:T(8,128)} custom-call(s32[1,1]{1,0:T(1,128)S(6)} %copy.10.kept._, bf16[56,1792]{1,0:T(8,128)(2,1)} %reduce-scatter.2.cloned.1.call-done.narrow), custom_call_target="tpu_custom_call" | custom-call | tf_op jit(solution)/shard_map/widen/pallas_call | solution.py:352
  101.9 0.0 copy-start.1
  101.9 0.0 copy-start.3
  101.9 0.0 copy-start.4
  101.9 6.0 %project.1 = bf16[128,1792]{1,0:T(8,128)(2,1)} custom-call(bf16[128,896]{1,0:T(8,128)(2,1)} %get-tuple-element.36.context, bf16[896,1792]{1,0:T(8,128)(2,1)} %all-gather.2.cloned.1.call-done.w), custom_call_target="tpu_custom_call" | custom-call | tf_op jit(solution)/shard_map/project/pallas_call | solution.py:332
  107.8 0.0 collective-permute-done.5.r0
  107.8 0.0 collective-permute-done.6.r1
  107.8 0.0 collective-permute-done.7.r2
  107.9 0.0 collective-permute-done.8.r3
  107.9 0.0 copy-done.1
  107.9 0.0 copy-done.3
  107.9 0.0 copy-done.4
  107.9 2.2 %restore.1 = bf16[3,128,896]{2,1,0:T(8,128)(2,1)} custom-call(s32[3,4,64]{2,1,0:T(4,128)S(1)} %bitcast.22, bf16[3,128,896]{2,1,0:T(8,128)(2,1)S(1)} %copy-done.1, bf16[3,7,128]{2,1,0:T(8,128)(2,1)S(1)} %bitcast.26, bf16[3,16,896]{2,1,0:T(8,128)(2,1)S(1)} %collective-permute-done.5.r0, bf16[3,16,896]{2,1,0:T(8,128)(2,1)S(1)} %collective-permute-done.6.r1, ...), custom_call_target="tpu_custom_call" | custom-call | tf_op jit(solution)/shard_map/restore/pallas_call | solution.py:343
Async XLA Ops:
  8.0 36.1 %copy-start = (bf16[1,1,128,1792]{3,2,1,0:T(8,128)(2,1)S(1)}, bf16[1,1,128,1792]{3,2,1,0:T(8,128)(2,1)}, u32[]{:S(2)}) copy-start(bf16[1,1,128,1792]{3,2,1,0:T(8,128)(2,1)} %param.13) | copy-start | bytes 1376260
  8.0 59.7 %all-gather.2.cloned.1.call-start = ((), (), s32[]{:S(2)}) async-start(), calls=%async_computation.1 | async-start | bytes 3411968 | tf_op jit(solution)/shard_map/all_gather | solution.py:258
  8.7 91.4 %reduce-scatter.2.cloned.1.call-start = ((), (), s32[]{:S(2)}) async-start(), calls=%async_computation.2 | async-start | bytes 1806336 | tf_op jit(solution)/shard_map/reduce_scatter | solution.py:310
  11.1 13.3 %collective-permute-start = (bf16[3,16,896]{2,1,0:T(8,128)(2,1)}, bf16[3,16,896]{2,1,0:T(8,128)(2,1)S(1)}, u32[]{:S(2)}, u32[]{:S(2)}) collective-permute-start(bf16[3,16,896]{2,1,0:T(8,128)(2,1)} %get-tuple-element.22), channel_id=1, source_target_pairs={{0,16},{16,32},{32,48},{48,64},{64,80},{80,96},{96,112},{112,128},... | collective-permute-start | bytes 258056 | tf_op jit(solution)/shard_map/ppermute | solution.py:24
  14.7 9.7 %collective-permute-start.1 = (bf16[3,16,896]{2,1,0:T(8,128)(2,1)}, bf16[3,16,896]{2,1,0:T(8,128)(2,1)S(1)}, u32[]{:S(2)}, u32[]{:S(2)}) collective-permute-start(bf16[3,16,896]{2,1,0:T(8,128)(2,1)} %get-tuple-element.23), channel_id=1, source_target_pairs={{16,0},{32,16},{48,32},{64,48},{80,64},{96,80},{112,96},{128,112},... | collective-permute-start | bytes 258056 | tf_op jit(solution)/shard_map/ppermute | solution.py:24
  16.9 7.9 %collective-permute-start.2 = (bf16[3,16,896]{2,1,0:T(8,128)(2,1)}, bf16[3,16,896]{2,1,0:T(8,128)(2,1)S(1)}, u32[]{:S(2)}, u32[]{:S(2)}) collective-permute-start(bf16[3,16,896]{2,1,0:T(8,128)(2,1)} %get-tuple-element.24), channel_id=1, source_target_pairs={{0,32},{16,48},{32,64},{48,80},{64,96},{80,112},{96,128},{112,144}... | collective-permute-start | bytes 258056 | tf_op jit(solution)/shard_map/ppermute | solution.py:24
  21.7 10.5 %collective-permute-start.3 = (bf16[3,16,896]{2,1,0:T(8,128)(2,1)}, bf16[3,16,896]{2,1,0:T(8,128)(2,1)S(1)}, u32[]{:S(2)}, u32[]{:S(2)}) collective-permute-start(bf16[3,16,896]{2,1,0:T(8,128)(2,1)} %get-tuple-element.25), channel_id=1, source_target_pairs={{32,0},{48,16},{64,32},{80,48},{96,64},{112,80},{128,96},{144,112}... | collective-permute-start | bytes 258056 | tf_op jit(solution)/shard_map/ppermute | solution.py:24
  24.3 7.9 %copy-start.5 = (bf16[3,16,896]{2,1,0:T(8,128)(2,1)}, bf16[3,16,896]{2,1,0:T(8,128)(2,1)S(1)}, u32[]{:S(2)}) copy-start(bf16[3,16,896]{2,1,0:T(8,128)(2,1)S(1)} %collective-permute-done.r0) | copy-start | bytes 258052
  24.4 7.8 %copy-start.6 = (bf16[3,16,896]{2,1,0:T(8,128)(2,1)}, bf16[3,16,896]{2,1,0:T(8,128)(2,1)S(1)}, u32[]{:S(2)}) copy-start(bf16[3,16,896]{2,1,0:T(8,128)(2,1)S(1)} %collective-permute-done.1.r1) | copy-start | bytes 258052
  24.9 7.3 %copy-start.7 = (bf16[3,16,896]{2,1,0:T(8,128)(2,1)}, bf16[3,16,896]{2,1,0:T(8,128)(2,1)S(1)}, u32[]{:S(2)}) copy-start(bf16[3,16,896]{2,1,0:T(8,128)(2,1)S(1)} %collective-permute-done.2.r2) | copy-start | bytes 258052
  32.2 0.6 copy-start.8
  38.5 5.5 %collective-permute-start.4 = (bf16[448,1792]{1,0:T(8,128)(2,1)}, bf16[448,1792]{1,0:T(8,128)(2,1)S(1)}, u32[]{:S(2)}, u32[]{:S(2)}) collective-permute-start(bf16[448,1792]{1,0:T(8,128)(2,1)} %get-tuple-element.28), channel_id=1, source_target_pairs={{0,1},{1,0},{2,3},{3,2},{4,5},{5,4},{6,7},{7,6},{8,9},{9,8},{10,11... | collective-permute-start | bytes 4816904 | tf_op jit(solution)/shard_map/ppermute | solution.py:299
  44.1 0.9 copy-start.2
  74.8 33.1 %collective-permute-start.5 = (bf16[3,16,896]{2,1,0:T(8,128)(2,1)}, bf16[3,16,896]{2,1,0:T(8,128)(2,1)S(1)}, u32[]{:S(2)}, u32[]{:S(2)}) collective-permute-start(bf16[3,16,896]{2,1,0:T(8,128)(2,1)} %get-tuple-element.32), channel_id=1, source_target_pairs={{16,0},{32,16},{48,32},{64,48},{80,64},{96,80},{112,96},{128,112},... | collective-permute-start | bytes 258056 | tf_op jit(solution)/shard_map/ppermute | solution.py:24
  78.1 29.7 %collective-permute-start.6 = (bf16[3,16,896]{2,1,0:T(8,128)(2,1)}, bf16[3,16,896]{2,1,0:T(8,128)(2,1)S(1)}, u32[]{:S(2)}, u32[]{:S(2)}) collective-permute-start(bf16[3,16,896]{2,1,0:T(8,128)(2,1)} %get-tuple-element.33), channel_id=1, source_target_pairs={{0,16},{16,32},{32,48},{48,64},{64,80},{80,96},{96,112},{112,128},... | collective-permute-start | bytes 258056 | tf_op jit(solution)/shard_map/ppermute | solution.py:24
  82.7 25.1 %collective-permute-start.7 = (bf16[3,16,896]{2,1,0:T(8,128)(2,1)}, bf16[3,16,896]{2,1,0:T(8,128)(2,1)S(1)}, u32[]{:S(2)}, u32[]{:S(2)}) collective-permute-start(bf16[3,16,896]{2,1,0:T(8,128)(2,1)} %get-tuple-element.34), channel_id=1, source_target_pairs={{32,0},{48,16},{64,32},{80,48},{96,64},{112,80},{128,96},{144,112}... | collective-permute-start | bytes 258056 | tf_op jit(solution)/shard_map/ppermute | solution.py:24
  84.8 23.0 %collective-permute-start.8 = (bf16[3,16,896]{2,1,0:T(8,128)(2,1)}, bf16[3,16,896]{2,1,0:T(8,128)(2,1)S(1)}, u32[]{:S(2)}, u32[]{:S(2)}) collective-permute-start(bf16[3,16,896]{2,1,0:T(8,128)(2,1)} %get-tuple-element.35), channel_id=1, source_target_pairs={{0,32},{16,48},{32,64},{48,80},{64,96},{80,112},{96,128},{112,144}... | collective-permute-start | bytes 258056 | tf_op jit(solution)/shard_map/ppermute | solution.py:24
  101.9 6.0 %copy-start.1 = (bf16[3,128,896]{2,1,0:T(8,128)(2,1)S(1)}, bf16[3,128,896]{2,1,0:T(8,128)(2,1)}, u32[]{:S(2)}) copy-start(bf16[3,128,896]{2,1,0:T(8,128)(2,1)} %get-tuple-element.31.home) | copy-start | bytes 2064388
  101.9 6.0 %copy-start.3 = (s32[64,1,4,3]{0,2,3,1:T(4,128)S(1)}, s32[64,1,4,3]{0,2,3,1:T(4,128)}, u32[]{:S(2)}) copy-start(s32[64,1,4,3]{0,2,3,1:T(4,128)} %param.11) | copy-start | bytes 9220
  101.9 6.0 %copy-start.4 = (bf16[1,1,128,3,7]{2,4,3,1,0:T(8,128)(2,1)S(1)}, bf16[1,1,128,3,7]{2,4,3,1,0:T(8,128)(2,1)}, u32[]{:S(2)}) copy-start(bf16[1,1,128,3,7]{2,4,3,1,0:T(8,128)(2,1)} %param.8) | copy-start | bytes 16132
Sparse Core Ops, SparseCore 0:
  11.5 56.1 all-gather.1
Sparse Core Ops, SparseCore 1:
  47.0 53.2 reduce-scatter.1

commit v6 on v5

--- a/solution.py
+++ b/solution.py
@@ -215,7 +215,7 @@
             ref[c] = back[d * SLOT : (d + 1) * SLOT]
 
 
-def return_kernel(table, home, scales, r0, r1, r2, r3, grad_codes):
+def return_kernel(table, home, scales, r0, r1, r2, r3, _, grad_codes):
     at = lax.axis_index("dp")
     rows = home.shape[1]
     place = one_hot(sent_spans(table, at), rows, False)
@@ -343,20 +343,21 @@
     grad_codes = pl.pallas_call(
         return_kernel,
         out_shape=jax.ShapeDtypeStruct((3, rows, width), BF16),
-        in_specs=[smem, codes_spec, scales_spec] + [piece_spec] * 4,
+        in_specs=[smem, codes_spec, scales_spec]
+        + [piece_spec] * 4
+        + [pl.BlockSpec(memory_space=pl.ANY)],
         out_specs=codes_spec,
-        compiler_params=light,
+        compiler_params=params,
         name="restore",
-    )(table, home, scales, *returned)
-    gate, grad_codes, output = lax.optimization_barrier((kept_rows, grad_codes, output))
+    )(table, home, scales, *returned, output)
     grad_w = pl.pallas_call(
         widen_kernel,
         out_shape=jax.ShapeDtypeStruct(w_out.shape, F32),
-        in_specs=[smem, whole(w_out.shape)],
+        in_specs=[pl.BlockSpec(memory_space=pl.ANY), whole(w_out.shape)],
         out_specs=whole(w_out.shape),
         compiler_params=params,
         name="widen",
-    )(gate, scattered)
+    )(grad_codes, scattered)
     grad_codes = jnp.transpose(grad_codes, (1, 0, 2))
     return (output[None, None], grad_codes[None, None], grad_w[None])
 

time: 120 us -> 111 us (0.925); the launches traced: 118 us -> 110 us
  waiting for transfers between devices: 41.6 us -> 33 us
    reduce_scatter x1, waiting for transfers between devices: 8.56 us -> 0.01 us  [local(): lax.psum_scatter(folded, 'fsdp', scatter_dimension=0, tiled=True, axis_in...]
  transfers between devices with their start and end apart: 11 -> 11, of which waited for: 5 -> 4; matrix products, arithmetic and copies ran while one was open for 0% -> 0% of each run, Pallas kernels for 21% -> 23%
where the time goes in v6:
time: 111 us; the launch traced here: 110 us
  waiting for transfers between devices  33 us (30%)
  starting transfers between devices  31.3 us (28%)
  Pallas kernels  27.4 us (25%)
  between operations  16.3 us (15%)
  local copies, waits for them, and re-layouts  2.22 us (2%)
    ppermute x8, starting transfers between devices, shifted(): return lax.ppermute(block, axis, route)  29.4 us
    all_gather x1, waiting for transfers between devices, local(): w_full = lax.all_gather(w_out, 'fsdp', axis=0, tiled=True)  20.8 us
    ppermute x8, waiting for transfers between devices, shifted(): return lax.ppermute(block, axis, route)  7.84 us
    pallas_call x1, Pallas kernels, local(): pl.pallas_call(functools.partial(backward_kernel, group), out_shape=[jax....  7.03 us
    pallas_call x1, Pallas kernels, local(): pl.pallas_call(output_kernel, grid=(depth // chunk,), out_shape=jax.Shape...  5.92 us
    pallas_call x1, Pallas kernels, local(): pl.pallas_call(functools.partial(forward_kernel, group), grid=(2,), out_s...  5.7 us
    ppermute x1, waiting for transfers between devices, local(): arrived = lax.ppermute(term_other, 'fsdp', swap)  3.63 us
    pallas_call x1, Pallas kernels, local(): pl.pallas_call(return_kernel, out_shape=jax.ShapeDtypeStruct((3, rows, wi...  2.83 us
  transfers between devices with their start and end apart: 11, of which 4 were waited for; matrix products, arithmetic and copies ran while one was open for 0% of the time, Pallas kernels for 23%

profile of v6, /device:TPU:112, one launch (start us, length us, event | category | flops | bytes accessed | tf_op | source)
XLA Modules:
  0.0 110.2 jit_solution(16935219053074324667)
XLA Ops:
  8.0 0.0 copy-start
  8.0 0.0 all-gather.2.cloned.1.call-start
  8.1 0.7 all-gather.2.cloned.1.call-update
  8.7 0.0 reduce-scatter.2.cloned.1.call-start
  8.8 2.3 %pack.1 = (bf16[3,16,896]{2,1,0:T(8,128)(2,1)}, bf16[3,16,896]{2,1,0:T(8,128)(2,1)}, bf16[3,16,896]{2,1,0:T(8,128)(2,1)}, bf16[3,16,896]{2,1,0:T(8,128)(2,1)}) custom-call(s32[3,4,64]{2,1,0:T(4,128)} %bitcast.24, bf16[3,128,896]{2,1,0:T(8,128)(2,1)} %bitcast.19, bf16[3,7,128]{2,1,0:T(8,128)(2,1)} %bitcast.28), custom_call_target="tpu_custom_call" | custom-call | flops 1 | bytes 1 | tf_op jit(solution)/shard_map/pack/pallas_call | solution.py:260
  11.1 3.6 %collective-permute-start = (bf16[3,16,896]{2,1,0:T(8,128)(2,1)}, bf16[3,16,896]{2,1,0:T(8,128)(2,1)S(1)}, u32[]{:S(2)}, u32[]{:S(2)}) collective-permute-start(bf16[3,16,896]{2,1,0:T(8,128)(2,1)} %get-tuple-element.19), channel_id=1, source_target_pairs={{0,16},{16,32},{32,48},{48,64},{64,80},{80,96},{96,112},{112,128},... | collective-permute-start | bytes 258056 | tf_op jit(solution)/shard_map/ppermute | solution.py:24
  14.7 2.2 %collective-permute-start.1 = (bf16[3,16,896]{2,1,0:T(8,128)(2,1)}, bf16[3,16,896]{2,1,0:T(8,128)(2,1)S(1)}, u32[]{:S(2)}, u32[]{:S(2)}) collective-permute-start(bf16[3,16,896]{2,1,0:T(8,128)(2,1)} %get-tuple-element.20), channel_id=1, source_target_pairs={{16,0},{32,16},{48,32},{64,48},{80,64},{96,80},{112,96},{128,112},... | collective-permute-start | bytes 258056 | tf_op jit(solution)/shard_map/ppermute | solution.py:24
  16.9 4.7 %collective-permute-start.2 = (bf16[3,16,896]{2,1,0:T(8,128)(2,1)}, bf16[3,16,896]{2,1,0:T(8,128)(2,1)S(1)}, u32[]{:S(2)}, u32[]{:S(2)}) collective-permute-start(bf16[3,16,896]{2,1,0:T(8,128)(2,1)} %get-tuple-element.21), channel_id=1, source_target_pairs={{0,32},{16,48},{32,64},{48,80},{64,96},{80,112},{96,128},{112,144}... | collective-permute-start | bytes 258056 | tf_op jit(solution)/shard_map/ppermute | solution.py:24
  21.7 2.0 %collective-permute-start.3 = (bf16[3,16,896]{2,1,0:T(8,128)(2,1)}, bf16[3,16,896]{2,1,0:T(8,128)(2,1)S(1)}, u32[]{:S(2)}, u32[]{:S(2)}) collective-permute-start(bf16[3,16,896]{2,1,0:T(8,128)(2,1)} %get-tuple-element.22), channel_id=1, source_target_pairs={{32,0},{48,16},{64,32},{80,48},{96,64},{112,80},{128,96},{144,112}... | collective-permute-start | bytes 258056 | tf_op jit(solution)/shard_map/ppermute | solution.py:24
  24.3 0.0 collective-permute-done.r0
  24.3 0.0 copy-start.6
  24.3 0.0 collective-permute-done.1.r1
  24.4 0.0 copy-start.7
  24.4 0.5 collective-permute-done.2.r2
  24.9 0.0 copy-start.8
  24.9 7.3 %collective-permute-done.3.r3 = bf16[3,16,896]{2,1,0:T(8,128)(2,1)S(1)} collective-permute-done((bf16[3,16,896]{2,1,0:T(8,128)(2,1)}, bf16[3,16,896]{2,1,0:T(8,128)(2,1)S(1)}, u32[]{:S(2)}, u32[]{:S(2)}) %collective-permute-start.3) | collective-permute-done | bytes 86048 | tf_op jit(solution)/shard_map/ppermute | solution.py:24
  32.2 0.0 copy-start.9
  32.2 0.0 copy-done.6
  32.2 0.0 copy-done.7
  32.2 0.0 copy-done.8
  32.2 0.6 copy-done.9
  32.8 5.7 %forward.1 = (bf16[448,1792]{1,0:T(8,128)(2,1)}, bf16[128,896]{1,0:T(8,128)(2,1)}, bf16[448,128]{1,0:T(8,128)(2,1)}, bf16[3,128,896]{2,1,0:T(8,128)(2,1)}, f32[8,128,128]{2,1,0:T(8,128)}) custom-call(s32[3,4,64]{2,1,0:T(4,128)} %bitcast.25, s32[1,1]{1,0:T(1,128)S(6)} %copy.10.kept, s32[1,128]{1,0:T(1,128)} %bitcast.32, bf16[3,128,896]{2,1,0:T(8,128)(2,1)} %bitcast.20, ...), custom_call_target="tpu_custom_call" | custom-call | flops 1 | bytes 1 | tf_op jit(solution)/shard_map/forward/pallas_call | solution.py:274
  38.5 1.9 %collective-permute-start.4 = (bf16[448,1792]{1,0:T(8,128)(2,1)}, bf16[448,1792]{1,0:T(8,128)(2,1)S(1)}, u32[]{:S(2)}, u32[]{:S(2)}) collective-permute-start(bf16[448,1792]{1,0:T(8,128)(2,1)} %get-tuple-element.26), channel_id=1, source_target_pairs={{0,1},{1,0},{2,3},{3,2},{4,5},{5,4},{6,7},{7,6},{8,9},{9,8},{10,11... | collective-permute-start | bytes 4816904 | tf_op jit(solution)/shard_map/ppermute | solution.py:299
  40.5 3.6 %collective-permute-done.4.arrived = bf16[448,1792]{1,0:T(8,128)(2,1)S(1)} collective-permute-done((bf16[448,1792]{1,0:T(8,128)(2,1)}, bf16[448,1792]{1,0:T(8,128)(2,1)S(1)}, u32[]{:S(2)}, u32[]{:S(2)}) %collective-permute-start.4) | collective-permute-done | bytes 1605664 | tf_op jit(solution)/shard_map/ppermute | solution.py:299
  44.1 0.0 copy-done
  44.1 0.0 copy-start.1
  44.1 0.9 copy-done.1
  45.0 1.9 %fold.1 = bf16[448,1792]{1,0:T(8,128)(2,1)} custom-call(bf16[448,128]{1,0:T(8,128)(2,1)S(1)} %copy-done.1, bf16[128,1792]{1,0:T(8,128)(2,1)S(1)} %bitcast.18, bf16[448,1792]{1,0:T(8,128)(2,1)S(1)} %collective-permute-done.4.arrived), custom_call_target="tpu_custom_call" | custom-call | tf_op jit(solution)/shard_map/fold/pallas_call | solution.py:300
  46.9 0.0 reduce-scatter.2.cloned.1.call-update
  46.9 20.8 %all-gather.2.cloned.1.call-done.w = bf16[896,1792]{1,0:T(8,128)(2,1)} async-done(((bf16[56,1792]{1,0:T(8,128)(2,1)}), bf16[896,1792]{1,0:T(8,128)(2,1)}) %all-gather.2.cloned.1.call-update) | async-done | bytes 3211280 | tf_op jit(solution)/shard_map/all_gather | solution.py:258
  67.8 7.0 %backward.1 = (bf16[3,128,896]{2,1,0:T(8,128)(2,1)}, bf16[3,16,896]{2,1,0:T(8,128)(2,1)}, bf16[3,16,896]{2,1,0:T(8,128)(2,1)}, bf16[3,16,896]{2,1,0:T(8,128)(2,1)}, bf16[3,16,896]{2,1,0:T(8,128)(2,1)}) custom-call(s32[3,4,64]{2,1,0:T(4,128)} %bitcast.26, s32[1,1]{1,0:T(1,128)S(6)} %copy.10.kept, bf16[896,1792]{1,0:T(8,128)(2,1)} %all-gather.2.cloned.1.call-done.w, ...), custom_call_target="tpu_custom_call" | custom-call | tf_op jit(solution)/shard_map/backward/pallas_call | solution.py:314
  74.8 3.3 %collective-permute-start.5 = (bf16[3,16,896]{2,1,0:T(8,128)(2,1)}, bf16[3,16,896]{2,1,0:T(8,128)(2,1)S(1)}, u32[]{:S(2)}, u32[]{:S(2)}) collective-permute-start(bf16[3,16,896]{2,1,0:T(8,128)(2,1)} %get-tuple-element.30), channel_id=1, source_target_pairs={{16,0},{32,16},{48,32},{64,48},{80,64},{96,80},{112,96},{128,112},... | collective-permute-start | bytes 258056 | tf_op jit(solution)/shard_map/ppermute | solution.py:24
  78.1 4.6 %collective-permute-start.6 = (bf16[3,16,896]{2,1,0:T(8,128)(2,1)}, bf16[3,16,896]{2,1,0:T(8,128)(2,1)S(1)}, u32[]{:S(2)}, u32[]{:S(2)}) collective-permute-start(bf16[3,16,896]{2,1,0:T(8,128)(2,1)} %get-tuple-element.31), channel_id=1, source_target_pairs={{0,16},{16,32},{32,48},{48,64},{64,80},{80,96},{96,112},{112,128},... | collective-permute-start | bytes 258056 | tf_op jit(solution)/shard_map/ppermute | solution.py:24
  82.7 2.1 %collective-permute-start.7 = (bf16[3,16,896]{2,1,0:T(8,128)(2,1)}, bf16[3,16,896]{2,1,0:T(8,128)(2,1)S(1)}, u32[]{:S(2)}, u32[]{:S(2)}) collective-permute-start(bf16[3,16,896]{2,1,0:T(8,128)(2,1)} %get-tuple-element.32), channel_id=1, source_target_pairs={{32,0},{48,16},{64,32},{80,48},{96,64},{112,80},{128,96},{144,112}... | collective-permute-start | bytes 258056 | tf_op jit(solution)/shard_map/ppermute | solution.py:24
  84.8 6.8 %collective-permute-start.8 = (bf16[3,16,896]{2,1,0:T(8,128)(2,1)}, bf16[3,16,896]{2,1,0:T(8,128)(2,1)S(1)}, u32[]{:S(2)}, u32[]{:S(2)}) collective-permute-start(bf16[3,16,896]{2,1,0:T(8,128)(2,1)} %get-tuple-element.33), channel_id=1, source_target_pairs={{0,32},{16,48},{32,64},{48,80},{64,96},{80,112},{96,128},{112,144}... | collective-permute-start | bytes 258056 | tf_op jit(solution)/shard_map/ppermute | solution.py:24
  91.6 5.9 %project.1._ = bf16[128,1792]{1,0:T(8,128)(2,1)} custom-call(bf16[128,896]{1,0:T(8,128)(2,1)} %get-tuple-element.23.context, bf16[896,1792]{1,0:T(8,128)(2,1)} %all-gather.2.cloned.1.call-done.w), custom_call_target="tpu_custom_call" | custom-call | tf_op jit(solution)/shard_map/project/pallas_call | solution.py:332
  97.5 0.0 collective-permute-done.5.r0
  97.5 0.0 copy-start.2
  97.5 0.0 collective-permute-done.6.r1
  97.5 0.0 copy-start.3
  97.5 0.0 collective-permute-done.7.r2
  97.5 0.0 copy-start.4
  97.6 0.0 collective-permute-done.8.r3
  97.6 0.0 copy-start.5
  97.6 0.6 copy-done.2
  98.2 0.0 copy-done.3
  98.2 0.0 copy-done.4
  98.2 0.0 copy-done.5
  98.2 2.8 %restore.1._ = bf16[3,128,896]{2,1,0:T(8,128)(2,1)} custom-call(s32[3,4,64]{2,1,0:T(4,128)} %bitcast.27, bf16[3,128,896]{2,1,0:T(8,128)(2,1)} %get-tuple-element.29.home, bf16[3,7,128]{2,1,0:T(8,128)(2,1)} %bitcast.31, bf16[3,16,896]{2,1,0:T(8,128)(2,1)} %copy-done.2, bf16[3,16,896]{2,1,0:T(8,128)(2,1)} %copy-done.3, bf16[3,16,896]{2,1,0:T(8,128)(2,1)} %copy-done.4, ...), custom_call_target="tpu_custom_call" | custom-call | tf_op jit(solution)/shard_map/restore/pallas_call | solution.py:343
  101.1 0.0 reduce-scatter.2.cloned.1.call-done.narrow
  101.1 1.7 %widen.1 = f32[56,1792]{1,0:T(8,128)} custom-call(bf16[3,128,896]{2,1,0:T(8,128)(2,1)} %restore.1._, bf16[56,1792]{1,0:T(8,128)(2,1)} %reduce-scatter.2.cloned.1.call-done.narrow), custom_call_target="tpu_custom_call" | custom-call | tf_op jit(solution)/shard_map/widen/pallas_call | solution.py:353
Async XLA Ops:
  8.0 36.1 %copy-start = (bf16[1,1,128,1792]{3,2,1,0:T(8,128)(2,1)S(1)}, bf16[1,1,128,1792]{3,2,1,0:T(8,128)(2,1)}, u32[]{:S(2)}) copy-start(bf16[1,1,128,1792]{3,2,1,0:T(8,128)(2,1)} %param.13) | copy-start | bytes 1376260
  8.0 59.7 %all-gather.2.cloned.1.call-start = ((), (), s32[]{:S(2)}) async-start(), calls=%async_computation.1 | async-start | bytes 3411968 | tf_op jit(solution)/shard_map/all_gather | solution.py:258
  8.7 92.3 %reduce-scatter.2.cloned.1.call-start = ((), (), s32[]{:S(2)}) async-start(), calls=%async_computation.2 | async-start | bytes 1806336 | tf_op jit(solution)/shard_map/reduce_scatter | solution.py:310
  11.1 13.3 %collective-permute-start = (bf16[3,16,896]{2,1,0:T(8,128)(2,1)}, bf16[3,16,896]{2,1,0:T(8,128)(2,1)S(1)}, u32[]{:S(2)}, u32[]{:S(2)}) collective-permute-start(bf16[3,16,896]{2,1,0:T(8,128)(2,1)} %get-tuple-element.19), channel_id=1, source_target_pairs={{0,16},{16,32},{32,48},{48,64},{64,80},{80,96},{96,112},{112,128},... | collective-permute-start | bytes 258056 | tf_op jit(solution)/shard_map/ppermute | solution.py:24
  14.7 9.7 %collective-permute-start.1 = (bf16[3,16,896]{2,1,0:T(8,128)(2,1)}, bf16[3,16,896]{2,1,0:T(8,128)(2,1)S(1)}, u32[]{:S(2)}, u32[]{:S(2)}) collective-permute-start(bf16[3,16,896]{2,1,0:T(8,128)(2,1)} %get-tuple-element.20), channel_id=1, source_target_pairs={{16,0},{32,16},{48,32},{64,48},{80,64},{96,80},{112,96},{128,112},... | collective-permute-start | bytes 258056 | tf_op jit(solution)/shard_map/ppermute | solution.py:24
  16.9 7.9 %collective-permute-start.2 = (bf16[3,16,896]{2,1,0:T(8,128)(2,1)}, bf16[3,16,896]{2,1,0:T(8,128)(2,1)S(1)}, u32[]{:S(2)}, u32[]{:S(2)}) collective-permute-start(bf16[3,16,896]{2,1,0:T(8,128)(2,1)} %get-tuple-element.21), channel_id=1, source_target_pairs={{0,32},{16,48},{32,64},{48,80},{64,96},{80,112},{96,128},{112,144}... | collective-permute-start | bytes 258056 | tf_op jit(solution)/shard_map/ppermute | solution.py:24
  21.7 10.5 %collective-permute-start.3 = (bf16[3,16,896]{2,1,0:T(8,128)(2,1)}, bf16[3,16,896]{2,1,0:T(8,128)(2,1)S(1)}, u32[]{:S(2)}, u32[]{:S(2)}) collective-permute-start(bf16[3,16,896]{2,1,0:T(8,128)(2,1)} %get-tuple-element.22), channel_id=1, source_target_pairs={{32,0},{48,16},{64,32},{80,48},{96,64},{112,80},{128,96},{144,112}... | collective-permute-start | bytes 258056 | tf_op jit(solution)/shard_map/ppermute | solution.py:24
  24.3 7.9 %copy-start.6 = (bf16[3,16,896]{2,1,0:T(8,128)(2,1)}, bf16[3,16,896]{2,1,0:T(8,128)(2,1)S(1)}, u32[]{:S(2)}) copy-start(bf16[3,16,896]{2,1,0:T(8,128)(2,1)S(1)} %collective-permute-done.r0) | copy-start | bytes 258052
  24.4 7.8 %copy-start.7 = (bf16[3,16,896]{2,1,0:T(8,128)(2,1)}, bf16[3,16,896]{2,1,0:T(8,128)(2,1)S(1)}, u32[]{:S(2)}) copy-start(bf16[3,16,896]{2,1,0:T(8,128)(2,1)S(1)} %collective-permute-done.1.r1) | copy-start | bytes 258052
  24.9 7.3 %copy-start.8 = (bf16[3,16,896]{2,1,0:T(8,128)(2,1)}, bf16[3,16,896]{2,1,0:T(8,128)(2,1)S(1)}, u32[]{:S(2)}) copy-start(bf16[3,16,896]{2,1,0:T(8,128)(2,1)S(1)} %collective-permute-done.2.r2) | copy-start | bytes 258052
  32.2 0.7 copy-start.9
  38.5 5.5 %collective-permute-start.4 = (bf16[448,1792]{1,0:T(8,128)(2,1)}, bf16[448,1792]{1,0:T(8,128)(2,1)S(1)}, u32[]{:S(2)}, u32[]{:S(2)}) collective-permute-start(bf16[448,1792]{1,0:T(8,128)(2,1)} %get-tuple-element.26), channel_id=1, source_target_pairs={{0,1},{1,0},{2,3},{3,2},{4,5},{5,4},{6,7},{7,6},{8,9},{9,8},{10,11... | collective-permute-start | bytes 4816904 | tf_op jit(solution)/shard_map/ppermute | solution.py:299
  44.1 0.9 copy-start.1
  74.8 22.7 %collective-permute-start.5 = (bf16[3,16,896]{2,1,0:T(8,128)(2,1)}, bf16[3,16,896]{2,1,0:T(8,128)(2,1)S(1)}, u32[]{:S(2)}, u32[]{:S(2)}) collective-permute-start(bf16[3,16,896]{2,1,0:T(8,128)(2,1)} %get-tuple-element.30), channel_id=1, source_target_pairs={{16,0},{32,16},{48,32},{64,48},{80,64},{96,80},{112,96},{128,112},... | collective-permute-start | bytes 258056 | tf_op jit(solution)/shard_map/ppermute | solution.py:24
  78.1 19.4 %collective-permute-start.6 = (bf16[3,16,896]{2,1,0:T(8,128)(2,1)}, bf16[3,16,896]{2,1,0:T(8,128)(2,1)S(1)}, u32[]{:S(2)}, u32[]{:S(2)}) collective-permute-start(bf16[3,16,896]{2,1,0:T(8,128)(2,1)} %get-tuple-element.31), channel_id=1, source_target_pairs={{0,16},{16,32},{32,48},{48,64},{64,80},{80,96},{96,112},{112,128},... | collective-permute-start | bytes 258056 | tf_op jit(solution)/shard_map/ppermute | solution.py:24
  82.7 14.8 %collective-permute-start.7 = (bf16[3,16,896]{2,1,0:T(8,128)(2,1)}, bf16[3,16,896]{2,1,0:T(8,128)(2,1)S(1)}, u32[]{:S(2)}, u32[]{:S(2)}) collective-permute-start(bf16[3,16,896]{2,1,0:T(8,128)(2,1)} %get-tuple-element.32), channel_id=1, source_target_pairs={{32,0},{48,16},{64,32},{80,48},{96,64},{112,80},{128,96},{144,112}... | collective-permute-start | bytes 258056 | tf_op jit(solution)/shard_map/ppermute | solution.py:24
  84.8 12.7 %collective-permute-start.8 = (bf16[3,16,896]{2,1,0:T(8,128)(2,1)}, bf16[3,16,896]{2,1,0:T(8,128)(2,1)S(1)}, u32[]{:S(2)}, u32[]{:S(2)}) collective-permute-start(bf16[3,16,896]{2,1,0:T(8,128)(2,1)} %get-tuple-element.33), channel_id=1, source_target_pairs={{0,32},{16,48},{32,64},{48,80},{64,96},{80,112},{96,128},{112,144}... | collective-permute-start | bytes 258056 | tf_op jit(solution)/shard_map/ppermute | solution.py:24
  97.5 0.6 copy-start.2
  97.5 0.7 copy-start.3
  97.5 0.7 copy-start.4
  97.6 0.7 copy-start.5
Sparse Core Ops, SparseCore 0:
  11.5 56.1 all-gather.1
Sparse Core Ops, SparseCore 1:
  47.0 53.1 reduce-scatter.1

commit v7 on v6

--- a/solution.py
+++ b/solution.py
@@ -10,6 +10,7 @@
 
 HEADS = 8
 OFFSETS = (1, -1, 2, -2)
+FAR_FIRST = (2, 3, 0, 1)
 SLOT = 16
 LANES = 128
 F32 = jnp.float32
@@ -108,7 +109,7 @@
 
 
 def forward_kernel(
-    group, table, kept, segments, codes, scales, r0, r1, r2, r3, grad_out,
+    group, table, kept, segments, codes, scales, r2, r3, r0, r1, grad_out,
     term_other, context_out, turned_own, balanced, probs_out, turned
 ):
     rows, width = codes.shape[1:]
@@ -215,7 +216,7 @@
             ref[c] = back[d * SLOT : (d + 1) * SLOT]
 
 
-def return_kernel(table, home, scales, r0, r1, r2, r3, _, grad_codes):
+def return_kernel(table, home, scales, r2, r3, r0, r1, _, grad_codes):
     at = lax.axis_index("dp")
     rows = home.shape[1]
     place = one_hot(sent_spans(table, at), rows, False)
@@ -266,7 +267,7 @@
         cost_estimate=small,
         name="pack",
     )(table, codes, scales)
-    received = [shifted(sent[d], "dp", OFFSETS[d]) for d in range(4)]
+    received = [shifted(sent[d], "dp", OFFSETS[d]) for d in FAR_FIRST]
 
     span = depth // 2
     term_spec = pl.BlockSpec((half, span), lambda n: (0, n))
@@ -338,7 +339,7 @@
         compiler_params=params,
         name="project",
     )(context, w_full)
-    returned = [shifted(back[d], "dp", -OFFSETS[d]) for d in range(4)]
+    returned = [shifted(back[d], "dp", -OFFSETS[d]) for d in FAR_FIRST]
 
     grad_codes = pl.pallas_call(
         return_kernel,

time: 111 us -> 111 us (level)
  starting transfers between devices: 31.3 us -> 33.1 us
  waiting for transfers between devices: 33 us -> 31.2 us
    ppermute x8, starting transfers between devices: 29.4 us -> 31.1 us  [shifted(): return lax.ppermute(block, axis, route)]
    ppermute x8, waiting for transfers between devices: 7.84 us -> 6.08 us  [shifted(): return lax.ppermute(block, axis, route)]
  transfers between devices with their start and end apart: 11 -> 11, of which waited for: 4 -> 3; matrix products, arithmetic and copies ran while one was open for 0% -> 0% of each run, Pallas kernels for 23% -> 23%
where the time goes in v7:
time: 111 us; the launch traced here: 110 us
  starting transfers between devices  33.1 us (30%)
  waiting for transfers between devices  31.2 us (28%)
  Pallas kernels  27.4 us (25%)
  between operations  16.3 us (15%)
  local copies, waits for them, and re-layouts  2.22 us (2%)
    ppermute x8, starting transfers between devices, shifted(): return lax.ppermute(block, axis, route)  31.1 us
    all_gather x1, waiting for transfers between devices, local(): w_full = lax.all_gather(w_out, 'fsdp', axis=0, tiled=True)  20.8 us
    pallas_call x1, Pallas kernels, local(): pl.pallas_call(functools.partial(backward_kernel, group), out_shape=[jax....  7.03 us
    ppermute x8, waiting for transfers between devices, shifted(): return lax.ppermute(block, axis, route)  6.08 us
    pallas_call x1, Pallas kernels, local(): pl.pallas_call(output_kernel, grid=(depth // chunk,), out_shape=jax.Shape...  5.91 us
    pallas_call x1, Pallas kernels, local(): pl.pallas_call(functools.partial(forward_kernel, group), grid=(2,), out_s...  5.69 us
    ppermute x1, waiting for transfers between devices, local(): arrived = lax.ppermute(term_other, 'fsdp', swap)  3.63 us
    pallas_call x1, Pallas kernels, local(): pl.pallas_call(return_kernel, out_shape=jax.ShapeDtypeStruct((3, rows, wi...  2.84 us
  transfers between devices with their start and end apart: 11, of which 3 were waited for; matrix products, arithmetic and copies ran while one was open for 0% of the time, Pallas kernels for 23%

profile of v7, /device:TPU:112, one launch (start us, length us, event | category | flops | bytes accessed | tf_op | source)
XLA Modules:
  0.0 110.2 jit_solution(4672382171911853421)
XLA Ops:
  8.0 0.0 copy-start
  8.0 0.0 all-gather.2.cloned.1.call-start
  8.1 0.7 all-gather.2.cloned.1.call-update
  8.7 0.0 reduce-scatter.2.cloned.1.call-start
  8.8 2.3 %pack.1 = (bf16[3,16,896]{2,1,0:T(8,128)(2,1)}, bf16[3,16,896]{2,1,0:T(8,128)(2,1)}, bf16[3,16,896]{2,1,0:T(8,128)(2,1)}, bf16[3,16,896]{2,1,0:T(8,128)(2,1)}) custom-call(s32[3,4,64]{2,1,0:T(4,128)} %bitcast.24, bf16[3,128,896]{2,1,0:T(8,128)(2,1)} %bitcast.19, bf16[3,7,128]{2,1,0:T(8,128)(2,1)} %bitcast.28), custom_call_target="tpu_custom_call" | custom-call | flops 1 | bytes 1 | tf_op jit(solution)/shard_map/pack/pallas_call | solution.py:261
  11.1 4.7 %collective-permute-start = (bf16[3,16,896]{2,1,0:T(8,128)(2,1)}, bf16[3,16,896]{2,1,0:T(8,128)(2,1)S(1)}, u32[]{:S(2)}, u32[]{:S(2)}) collective-permute-start(bf16[3,16,896]{2,1,0:T(8,128)(2,1)} %get-tuple-element.19), channel_id=1, source_target_pairs={{0,32},{16,48},{32,64},{48,80},{64,96},{80,112},{96,128},{112,144}... | collective-permute-start | bytes 258056 | tf_op jit(solution)/shard_map/ppermute | solution.py:25
  15.8 2.0 %collective-permute-start.1 = (bf16[3,16,896]{2,1,0:T(8,128)(2,1)}, bf16[3,16,896]{2,1,0:T(8,128)(2,1)S(1)}, u32[]{:S(2)}, u32[]{:S(2)}) collective-permute-start(bf16[3,16,896]{2,1,0:T(8,128)(2,1)} %get-tuple-element.20), channel_id=1, source_target_pairs={{32,0},{48,16},{64,32},{80,48},{96,64},{112,80},{128,96},{144,112}... | collective-permute-start | bytes 258056 | tf_op jit(solution)/shard_map/ppermute | solution.py:25
  17.8 5.7 %collective-permute-start.2 = (bf16[3,16,896]{2,1,0:T(8,128)(2,1)}, bf16[3,16,896]{2,1,0:T(8,128)(2,1)S(1)}, u32[]{:S(2)}, u32[]{:S(2)}) collective-permute-start(bf16[3,16,896]{2,1,0:T(8,128)(2,1)} %get-tuple-element.21), channel_id=1, source_target_pairs={{0,16},{16,32},{32,48},{48,64},{64,80},{80,96},{96,112},{112,128},... | collective-permute-start | bytes 258056 | tf_op jit(solution)/shard_map/ppermute | solution.py:25
  23.5 1.9 %collective-permute-start.3 = (bf16[3,16,896]{2,1,0:T(8,128)(2,1)}, bf16[3,16,896]{2,1,0:T(8,128)(2,1)S(1)}, u32[]{:S(2)}, u32[]{:S(2)}) collective-permute-start(bf16[3,16,896]{2,1,0:T(8,128)(2,1)} %get-tuple-element.22), channel_id=1, source_target_pairs={{16,0},{32,16},{48,32},{64,48},{80,64},{96,80},{112,96},{128,112},... | collective-permute-start | bytes 258056 | tf_op jit(solution)/shard_map/ppermute | solution.py:25
  26.1 0.0 collective-permute-done.r2
  26.1 0.0 copy-start.6
  26.1 0.0 collective-permute-done.1.r3
  26.1 0.0 copy-start.7
  26.2 0.0 collective-permute-done.2.r0
  26.2 0.0 copy-start.8
  26.2 6.1 %collective-permute-done.3.r1 = bf16[3,16,896]{2,1,0:T(8,128)(2,1)S(1)} collective-permute-done((bf16[3,16,896]{2,1,0:T(8,128)(2,1)}, bf16[3,16,896]{2,1,0:T(8,128)(2,1)S(1)}, u32[]{:S(2)}, u32[]{:S(2)}) %collective-permute-start.3) | collective-permute-done | bytes 86048 | tf_op jit(solution)/shard_map/ppermute | solution.py:25
  32.2 0.0 copy-start.9
  32.2 0.0 copy-done.6
  32.2 0.0 copy-done.7
  32.2 0.0 copy-done.8
  32.3 0.6 copy-done.9
  32.9 5.7 %forward.1 = (bf16[448,1792]{1,0:T(8,128)(2,1)}, bf16[128,896]{1,0:T(8,128)(2,1)}, bf16[448,128]{1,0:T(8,128)(2,1)}, bf16[3,128,896]{2,1,0:T(8,128)(2,1)}, f32[8,128,128]{2,1,0:T(8,128)}) custom-call(s32[3,4,64]{2,1,0:T(4,128)} %bitcast.25, s32[1,1]{1,0:T(1,128)S(6)} %copy.10.kept, s32[1,128]{1,0:T(1,128)} %bitcast.32, bf16[3,128,896]{2,1,0:T(8,128)(2,1)} %bitcast.20, ...), custom_call_target="tpu_custom_call" | custom-call | flops 1 | bytes 1 | tf_op jit(solution)/shard_map/forward/pallas_call | solution.py:275
  38.6 1.9 %collective-permute-start.4 = (bf16[448,1792]{1,0:T(8,128)(2,1)}, bf16[448,1792]{1,0:T(8,128)(2,1)S(1)}, u32[]{:S(2)}, u32[]{:S(2)}) collective-permute-start(bf16[448,1792]{1,0:T(8,128)(2,1)} %get-tuple-element.26), channel_id=1, source_target_pairs={{0,1},{1,0},{2,3},{3,2},{4,5},{5,4},{6,7},{7,6},{8,9},{9,8},{10,11... | collective-permute-start | bytes 4816904 | tf_op jit(solution)/shard_map/ppermute | solution.py:300
  40.5 3.6 %collective-permute-done.4.arrived = bf16[448,1792]{1,0:T(8,128)(2,1)S(1)} collective-permute-done((bf16[448,1792]{1,0:T(8,128)(2,1)}, bf16[448,1792]{1,0:T(8,128)(2,1)S(1)}, u32[]{:S(2)}, u32[]{:S(2)}) %collective-permute-start.4) | collective-permute-done | bytes 1605664 | tf_op jit(solution)/shard_map/ppermute | solution.py:300
  44.1 0.0 copy-done
  44.1 0.0 copy-start.1
  44.1 0.9 copy-done.1
  45.0 1.9 %fold.1 = bf16[448,1792]{1,0:T(8,128)(2,1)} custom-call(bf16[448,128]{1,0:T(8,128)(2,1)S(1)} %copy-done.1, bf16[128,1792]{1,0:T(8,128)(2,1)S(1)} %bitcast.18, bf16[448,1792]{1,0:T(8,128)(2,1)S(1)} %collective-permute-done.4.arrived), custom_call_target="tpu_custom_call" | custom-call | tf_op jit(solution)/shard_map/fold/pallas_call | solution.py:301
  47.0 0.0 reduce-scatter.2.cloned.1.call-update
  47.0 20.8 %all-gather.2.cloned.1.call-done.w = bf16[896,1792]{1,0:T(8,128)(2,1)} async-done(((bf16[56,1792]{1,0:T(8,128)(2,1)}), bf16[896,1792]{1,0:T(8,128)(2,1)}) %all-gather.2.cloned.1.call-update) | async-done | bytes 3211280 | tf_op jit(solution)/shard_map/all_gather | solution.py:259
  67.8 7.0 %backward.1 = (bf16[3,128,896]{2,1,0:T(8,128)(2,1)}, bf16[3,16,896]{2,1,0:T(8,128)(2,1)}, bf16[3,16,896]{2,1,0:T(8,128)(2,1)}, bf16[3,16,896]{2,1,0:T(8,128)(2,1)}, bf16[3,16,896]{2,1,0:T(8,128)(2,1)}) custom-call(s32[3,4,64]{2,1,0:T(4,128)} %bitcast.26, s32[1,1]{1,0:T(1,128)S(6)} %copy.10.kept, bf16[896,1792]{1,0:T(8,128)(2,1)} %all-gather.2.cloned.1.call-done.w, ...), custom_call_target="tpu_custom_call" | custom-call | tf_op jit(solution)/shard_map/backward/pallas_call | solution.py:315
  74.8 4.2 %collective-permute-start.5 = (bf16[3,16,896]{2,1,0:T(8,128)(2,1)}, bf16[3,16,896]{2,1,0:T(8,128)(2,1)S(1)}, u32[]{:S(2)}, u32[]{:S(2)}) collective-permute-start(bf16[3,16,896]{2,1,0:T(8,128)(2,1)} %get-tuple-element.30), channel_id=1, source_target_pairs={{32,0},{48,16},{64,32},{80,48},{96,64},{112,80},{128,96},{144,112}... | collective-permute-start | bytes 258056 | tf_op jit(solution)/shard_map/ppermute | solution.py:25
  79.0 4.7 %collective-permute-start.6 = (bf16[3,16,896]{2,1,0:T(8,128)(2,1)}, bf16[3,16,896]{2,1,0:T(8,128)(2,1)S(1)}, u32[]{:S(2)}, u32[]{:S(2)}) collective-permute-start(bf16[3,16,896]{2,1,0:T(8,128)(2,1)} %get-tuple-element.31), channel_id=1, source_target_pairs={{0,32},{16,48},{32,64},{48,80},{64,96},{80,112},{96,128},{112,144}... | collective-permute-start | bytes 258056 | tf_op jit(solution)/shard_map/ppermute | solution.py:25
  83.6 3.3 %collective-permute-start.7 = (bf16[3,16,896]{2,1,0:T(8,128)(2,1)}, bf16[3,16,896]{2,1,0:T(8,128)(2,1)S(1)}, u32[]{:S(2)}, u32[]{:S(2)}) collective-permute-start(bf16[3,16,896]{2,1,0:T(8,128)(2,1)} %get-tuple-element.32), channel_id=1, source_target_pairs={{16,0},{32,16},{48,32},{64,48},{80,64},{96,80},{112,96},{128,112},... | collective-permute-start | bytes 258056 | tf_op jit(solution)/shard_map/ppermute | solution.py:25
  87.0 4.6 %collective-permute-start.8 = (bf16[3,16,896]{2,1,0:T(8,128)(2,1)}, bf16[3,16,896]{2,1,0:T(8,128)(2,1)S(1)}, u32[]{:S(2)}, u32[]{:S(2)}) collective-permute-start(bf16[3,16,896]{2,1,0:T(8,128)(2,1)} %get-tuple-element.33), channel_id=1, source_target_pairs={{0,16},{16,32},{32,48},{48,64},{64,80},{80,96},{96,112},{112,128},... | collective-permute-start | bytes 258056 | tf_op jit(solution)/shard_map/ppermute | solution.py:25
  91.6 5.9 %project.1._ = bf16[128,1792]{1,0:T(8,128)(2,1)} custom-call(bf16[128,896]{1,0:T(8,128)(2,1)} %get-tuple-element.23.context, bf16[896,1792]{1,0:T(8,128)(2,1)} %all-gather.2.cloned.1.call-done.w), custom_call_target="tpu_custom_call" | custom-call | tf_op jit(solution)/shard_map/project/pallas_call | solution.py:333
  97.5 0.0 collective-permute-done.5.r2
  97.5 0.0 copy-start.2
  97.5 0.0 collective-permute-done.6.r3
  97.5 0.0 copy-start.3
  97.5 0.0 collective-permute-done.7.r0
  97.5 0.0 copy-start.4
  97.6 0.0 collective-permute-done.8.r1
  97.6 0.0 copy-start.5
  97.6 0.6 copy-done.2
  98.1 0.0 copy-done.3
  98.2 0.0 copy-done.4
  98.2 0.0 copy-done.5
  98.2 2.8 %restore.1._ = bf16[3,128,896]{2,1,0:T(8,128)(2,1)} custom-call(s32[3,4,64]{2,1,0:T(4,128)} %bitcast.27, bf16[3,128,896]{2,1,0:T(8,128)(2,1)} %get-tuple-element.29.home, bf16[3,7,128]{2,1,0:T(8,128)(2,1)} %bitcast.31, bf16[3,16,896]{2,1,0:T(8,128)(2,1)} %copy-done.2, bf16[3,16,896]{2,1,0:T(8,128)(2,1)} %copy-done.3, bf16[3,16,896]{2,1,0:T(8,128)(2,1)} %copy-done.4, ...), custom_call_target="tpu_custom_call" | custom-call | tf_op jit(solution)/shard_map/restore/pallas_call | solution.py:344
  101.1 0.0 reduce-scatter.2.cloned.1.call-done.narrow
  101.1 1.7 %widen.1 = f32[56,1792]{1,0:T(8,128)} custom-call(bf16[3,128,896]{2,1,0:T(8,128)(2,1)} %restore.1._, bf16[56,1792]{1,0:T(8,128)(2,1)} %reduce-scatter.2.cloned.1.call-done.narrow), custom_call_target="tpu_custom_call" | custom-call | tf_op jit(solution)/shard_map/widen/pallas_call | solution.py:354
Async XLA Ops:
  8.0 36.1 %copy-start = (bf16[1,1,128,1792]{3,2,1,0:T(8,128)(2,1)S(1)}, bf16[1,1,128,1792]{3,2,1,0:T(8,128)(2,1)}, u32[]{:S(2)}) copy-start(bf16[1,1,128,1792]{3,2,1,0:T(8,128)(2,1)} %param.13) | copy-start | bytes 1376260
  8.0 59.7 %all-gather.2.cloned.1.call-start = ((), (), s32[]{:S(2)}) async-start(), calls=%async_computation.1 | async-start | bytes 3411968 | tf_op jit(solution)/shard_map/all_gather | solution.py:259
  8.7 92.3 %reduce-scatter.2.cloned.1.call-start = ((), (), s32[]{:S(2)}) async-start(), calls=%async_computation.2 | async-start | bytes 1806336 | tf_op jit(solution)/shard_map/reduce_scatter | solution.py:311
  11.1 15.0 %collective-permute-start = (bf16[3,16,896]{2,1,0:T(8,128)(2,1)}, bf16[3,16,896]{2,1,0:T(8,128)(2,1)S(1)}, u32[]{:S(2)}, u32[]{:S(2)}) collective-permute-start(bf16[3,16,896]{2,1,0:T(8,128)(2,1)} %get-tuple-element.19), channel_id=1, source_target_pairs={{0,32},{16,48},{32,64},{48,80},{64,96},{80,112},{96,128},{112,144}... | collective-permute-start | bytes 258056 | tf_op jit(solution)/shard_map/ppermute | solution.py:25
  15.8 10.3 %collective-permute-start.1 = (bf16[3,16,896]{2,1,0:T(8,128)(2,1)}, bf16[3,16,896]{2,1,0:T(8,128)(2,1)S(1)}, u32[]{:S(2)}, u32[]{:S(2)}) collective-permute-start(bf16[3,16,896]{2,1,0:T(8,128)(2,1)} %get-tuple-element.20), channel_id=1, source_target_pairs={{32,0},{48,16},{64,32},{80,48},{96,64},{112,80},{128,96},{144,112}... | collective-permute-start | bytes 258056 | tf_op jit(solution)/shard_map/ppermute | solution.py:25
  17.8 8.3 %collective-permute-start.2 = (bf16[3,16,896]{2,1,0:T(8,128)(2,1)}, bf16[3,16,896]{2,1,0:T(8,128)(2,1)S(1)}, u32[]{:S(2)}, u32[]{:S(2)}) collective-permute-start(bf16[3,16,896]{2,1,0:T(8,128)(2,1)} %get-tuple-element.21), channel_id=1, source_target_pairs={{0,16},{16,32},{32,48},{48,64},{64,80},{80,96},{96,112},{112,128},... | collective-permute-start | bytes 258056 | tf_op jit(solution)/shard_map/ppermute | solution.py:25
  23.5 8.7 %collective-permute-start.3 = (bf16[3,16,896]{2,1,0:T(8,128)(2,1)}, bf16[3,16,896]{2,1,0:T(8,128)(2,1)S(1)}, u32[]{:S(2)}, u32[]{:S(2)}) collective-permute-start(bf16[3,16,896]{2,1,0:T(8,128)(2,1)} %get-tuple-element.22), channel_id=1, source_target_pairs={{16,0},{32,16},{48,32},{64,48},{80,64},{96,80},{112,96},{128,112},... | collective-permute-start | bytes 258056 | tf_op jit(solution)/shard_map/ppermute | solution.py:25
  26.1 6.1 %copy-start.6 = (bf16[3,16,896]{2,1,0:T(8,128)(2,1)}, bf16[3,16,896]{2,1,0:T(8,128)(2,1)S(1)}, u32[]{:S(2)}) copy-start(bf16[3,16,896]{2,1,0:T(8,128)(2,1)S(1)} %collective-permute-done.r2) | copy-start | bytes 258052
  26.1 6.1 %copy-start.7 = (bf16[3,16,896]{2,1,0:T(8,128)(2,1)}, bf16[3,16,896]{2,1,0:T(8,128)(2,1)S(1)}, u32[]{:S(2)}) copy-start(bf16[3,16,896]{2,1,0:T(8,128)(2,1)S(1)} %collective-permute-done.1.r3) | copy-start | bytes 258052
  26.2 6.1 %copy-start.8 = (bf16[3,16,896]{2,1,0:T(8,128)(2,1)}, bf16[3,16,896]{2,1,0:T(8,128)(2,1)S(1)}, u32[]{:S(2)}) copy-start(bf16[3,16,896]{2,1,0:T(8,128)(2,1)S(1)} %collective-permute-done.2.r0) | copy-start | bytes 258052
  32.2 0.7 copy-start.9
  38.6 5.5 %collective-permute-start.4 = (bf16[448,1792]{1,0:T(8,128)(2,1)}, bf16[448,1792]{1,0:T(8,128)(2,1)S(1)}, u32[]{:S(2)}, u32[]{:S(2)}) collective-permute-start(bf16[448,1792]{1,0:T(8,128)(2,1)} %get-tuple-element.26), channel_id=1, source_target_pairs={{0,1},{1,0},{2,3},{3,2},{4,5},{5,4},{6,7},{7,6},{8,9},{9,8},{10,11... | collective-permute-start | bytes 4816904 | tf_op jit(solution)/shard_map/ppermute | solution.py:300
  44.1 0.9 copy-start.1
  74.8 22.7 %collective-permute-start.5 = (bf16[3,16,896]{2,1,0:T(8,128)(2,1)}, bf16[3,16,896]{2,1,0:T(8,128)(2,1)S(1)}, u32[]{:S(2)}, u32[]{:S(2)}) collective-permute-start(bf16[3,16,896]{2,1,0:T(8,128)(2,1)} %get-tuple-element.30), channel_id=1, source_target_pairs={{32,0},{48,16},{64,32},{80,48},{96,64},{112,80},{128,96},{144,112}... | collective-permute-start | bytes 258056 | tf_op jit(solution)/shard_map/ppermute | solution.py:25
  79.0 18.6 %collective-permute-start.6 = (bf16[3,16,896]{2,1,0:T(8,128)(2,1)}, bf16[3,16,896]{2,1,0:T(8,128)(2,1)S(1)}, u32[]{:S(2)}, u32[]{:S(2)}) collective-permute-start(bf16[3,16,896]{2,1,0:T(8,128)(2,1)} %get-tuple-element.31), channel_id=1, source_target_pairs={{0,32},{16,48},{32,64},{48,80},{64,96},{80,112},{96,128},{112,144}... | collective-permute-start | bytes 258056 | tf_op jit(solution)/shard_map/ppermute | solution.py:25
  83.6 13.9 %collective-permute-start.7 = (bf16[3,16,896]{2,1,0:T(8,128)(2,1)}, bf16[3,16,896]{2,1,0:T(8,128)(2,1)S(1)}, u32[]{:S(2)}, u32[]{:S(2)}) collective-permute-start(bf16[3,16,896]{2,1,0:T(8,128)(2,1)} %get-tuple-element.32), channel_id=1, source_target_pairs={{16,0},{32,16},{48,32},{64,48},{80,64},{96,80},{112,96},{128,112},... | collective-permute-start | bytes 258056 | tf_op jit(solution)/shard_map/ppermute | solution.py:25
  87.0 10.6 %collective-permute-start.8 = (bf16[3,16,896]{2,1,0:T(8,128)(2,1)}, bf16[3,16,896]{2,1,0:T(8,128)(2,1)S(1)}, u32[]{:S(2)}, u32[]{:S(2)}) collective-permute-start(bf16[3,16,896]{2,1,0:T(8,128)(2,1)} %get-tuple-element.33), channel_id=1, source_target_pairs={{0,16},{16,32},{32,48},{48,64},{64,80},{80,96},{96,112},{112,128},... | collective-permute-start | bytes 258056 | tf_op jit(solution)/shard_map/ppermute | solution.py:25
  97.5 0.6 copy-start.2
  97.5 0.7 copy-start.3
  97.5 0.7 copy-start.4
  97.6 0.7 copy-start.5
Sparse Core Ops, SparseCore 0:
  11.5 56.1 all-gather.1
Sparse Core Ops, SparseCore 1:
  47.1 52.2 reduce-scatter.1
